TPU v7x, 512 devices: a whole 4x4x16 slice. The times are simulated.
512 devices in a mesh: pipe: 8 (over z_lo), dp: 16 (over x, z_hi, core), tensor: 4 (over y).
Axes of the slice: x: 4, y: 4, z: 16 (z_hi: 2, z_lo: 8; z = z_hi * 8 + z_lo), core: 2. Of those that a mesh axis runs over, the one named last changes fastest.
Arguments:
- outputs: bfloat16 [8, 2048, 6144], P('pipe', 'dp', 'tensor'), may hold values from -6 to 6
- cotangents: bfloat16 [4, 8, 2048, 6144], P(None, 'pipe', 'dp', 'tensor'), may hold values from -3 to 3
- gains: bfloat16 [8, 6144], P('pipe', 'tensor'), may hold values from 0.099609375 to 1.8984375
- first_weight: bfloat16 [8, 6144, 256], P('pipe', 'tensor'), may hold values from -0.078125 to 0.078125
- second_weight: bfloat16 [8, 256, 32], P('pipe'), may hold values from -0.375 to 0.375
Outputs:
- output_grads: bfloat16 [8, 2048, 6144], P('pipe', 'dp', 'tensor')
- first_grads: float32 [8, 6144, 256], P('pipe', 'tensor')
- second_grads: float32 [8, 256, 32], P('pipe')
All inputs are finite; a program needn't handle non-finite values.
Results may differ from a plain program's by a relative error of at most 0.025.
Values may be sent and summed in bfloat16 or wider, within the bound.
No kernel may reach another device: no remote copies, remote signals or barrier semaphores. Data moves between devices by JAX's collectives and lax.ppermute only.
A program may use at most 64 MiB of HBM per device.

v0:
```python
import jax
import jax.numpy as jnp
from jax import lax
from jax.sharding import PartitionSpec as P

D = 6144


epsilon = 1e-06


def on_device(outputs, cotangents, gains, first_weight, second_weight):
    layers = lax.axis_size("pipe")
    section = lax.axis_index("pipe")
    current_bf = outputs[0]
    current = current_bf.astype(jnp.float32)
    incoming = cotangents[:, 0]
    gain_row = gains[0].astype(jnp.float32)
    w_first = first_weight[0]
    w_second = second_weight[0]
    tokens = current.shape[0]
    squares = lax.psum(jnp.sum(current * current, axis=1), "tensor")
    factor = lax.rsqrt(squares / D + epsilon)
    normed = (current * factor[:, None] * gain_row[None, :]).astype(jnp.bfloat16)
    preact = lax.psum(
        jnp.dot(normed, w_first, preferred_element_type=jnp.float32).astype(jnp.bfloat16), "tensor"
    ).astype(jnp.float32)
    active = jax.nn.gelu(preact).astype(jnp.bfloat16)
    column_ids = jnp.arange(layers)
    allowed = (column_ids <= section).astype(jnp.float32)
    mixing = jnp.dot(active, w_second, preferred_element_type=jnp.float32)
    mixing = mixing.reshape(tokens, 4, layers) * allowed[None, None, :]
    result = jnp.zeros((1 * lax.axis_size("pipe"),) + current.shape, jnp.float32)
    for stream in range(4):
        result = (
            result + jnp.transpose(mixing[:, stream, :])[:, :, None] * incoming[stream][None, :, :]
        )
    received = lax.psum_scatter(
        result.astype(jnp.bfloat16), "pipe", scatter_dimension=0, tiled=True
    ).astype(jnp.float32)[0]
    partial_value = jnp.einsum(
        "std,jtd->sjt",
        incoming,
        lax.all_gather(outputs, "pipe", axis=0, tiled=True),
        preferred_element_type=jnp.float32,
    )
    products = lax.psum(partial_value, "tensor")
    products = products * allowed[None, :, None]
    depth_grads = (
        jnp.transpose(products, (2, 0, 1)).reshape(tokens, 4 * layers).astype(jnp.bfloat16)
    )
    dactive = jnp.dot(depth_grads, w_second.T, preferred_element_type=jnp.float32)
    unused, pullback = jax.vjp(jax.nn.gelu, preact)
    dpreact = pullback(dactive)[0].astype(jnp.bfloat16)
    weighted = jnp.dot(dpreact, w_first.T, preferred_element_type=jnp.float32) * gain_row[None, :]
    inner = lax.psum(jnp.sum(weighted * current, axis=1), "tensor")
    generated = factor[:, None] * weighted - current * (factor**3 * inner / D)[:, None]
    output_grads = (received + generated).astype(jnp.bfloat16)
    first_local = jnp.dot(normed.T, dpreact, preferred_element_type=jnp.float32)
    second_local = jnp.dot(active.T, depth_grads, preferred_element_type=jnp.float32)
    first_sum, second_sum = (
        lax.psum(first_local.astype(jnp.bfloat16), "dp").astype(jnp.float32),
        lax.psum(second_local.astype(jnp.bfloat16), "dp").astype(jnp.float32),
    )
    divisor = tokens * lax.axis_size("dp")
    return (output_grads[None], (first_sum / divisor)[None], (second_sum / divisor)[None])


def solution(mesh):
    placed = (
        P("pipe", "dp", "tensor"),
        P(None, "pipe", "dp", "tensor"),
        P("pipe", "tensor"),
        P("pipe", "tensor", None),
        P("pipe", None, None),
    )
    return jax.shard_map(
        on_device,
        mesh=mesh,
        in_specs=placed,
        out_specs=(P("pipe", "dp", "tensor"), P("pipe", "tensor", None), P("pipe", None, None)),
        check_vma=False,
    )
```

profile of v0, /device:TPU:1, one launch (start us, length us, event | category | flops | bytes accessed | tf_op | source)
XLA Modules:
  0.0 539.3 jit_solution(15606187282478067220)
XLA Ops:
  7.2 0.0 copy-start
  7.2 0.0 all-gather.2.cloned.1.call-start
  7.2 0.7 all-gather.2.cloned.1.call-update
  7.9 0.0 all-reduce.4.cloned.1.call-start
  8.0 0.0 copy-start.6
  8.0 0.7 convert_reduce_fusion
  8.7 1.2 fusion.12
  9.9 2.6 bitcast_convert_fusion.3
  12.5 86.9 %all-gather.2.cloned.1.call-done = bf16[8,128,1536]{2,1,0:T(8,128)(2,1)} async-done(((bf16[1,128,1536]{2,1,0:T(8,128)(2,1)}), bf16[8,128,1536]{2,1,0:T(8,128)(2,1)}) %all-gather.2.cloned.1.call-update) | async-done | bytes 3145744 | tf_op jit(solution)/shard_map/all_gather | solution.py:44
  99.4 0.0 copy-start.1
  99.4 6.0 %fusion.3 = f32[4,8,128]{1,0,2:T(4,128)} fusion(bf16[4,128,1536]{2,1,0:T(8,128)(2,1)} %bitcast.98, bf16[8,128,1536]{2,1,0:T(8,128)(2,1)} %all-gather.2.cloned.1.call-done), kind=kOutput, calls=%fused_computation.7 | convolution fusion | flops 12582912 | bytes 4734976 | tf_op jit(solution)/shard_map/std,jtd->sjt/dot_general | solution.py:41
  105.4 17.1 %all-reduce = (f32[128]{0:T(128)}, f32[4,8,128]{1,0,2:T(4,128)}) all-reduce(f32[128]{0:T(128)S(1)} %fusion.12, f32[4,8,128]{1,0,2:T(4,128)} %fusion.3), channel_id=1, replica_groups=mesh['pipe'=8,'dp'=16,'tensor'=4] {'tensor'}, use_global_device_ids=true, to_apply=%region_1.0 | all-reduce | flops 4224 | bytes 33792 | tf_op jit(solution)/shard_map/psum | solution.py:22
  122.5 0.7 add_rsqrt_fusion
  123.1 0.0 copy-start.4
  123.1 0.5 copy-done.4
  123.7 0.0 copy-done
  123.7 0.0 copy-done.1
  123.7 0.9 convolution_convert_fusion.1
  124.6 0.0 all-reduce.4.cloned.1.call-update
  124.6 0.0 all-reduce.6.cloned.1.call-start
  124.7 0.0 copy-done.6
  124.7 1.6 fusion.41
  126.3 1.0 copy.15
  127.3 48.9 %all-reduce.4.cloned.1.call-done = bf16[128,256]{1,0:T(8,128)(2,1)} async-done(((bf16[128,256]{1,0:T(8,128)(2,1)}), bf16[128,256]{1,0:T(8,128)(2,1)}) %all-reduce.4.cloned.1.call-update) | async-done | bytes 65552 | tf_op jit(solution)/shard_map/psum | solution.py:25
  176.2 1.1 fusion.34
  177.3 0.0 copy-start.2
  177.3 0.6 copy-done.2
  177.9 2.0 convolution_convert_fusion
  179.9 0.0 all-reduce.6.cloned.1.call-update
  179.9 0.0 reduce-scatter.2.cloned.1.call-start
  180.0 1.0 convolution_multiply_fusion.1
  181.0 4.2 add_convert_fusion
  185.2 0.0 copy-start.3
  185.2 0.0 copy-start.7
  185.2 0.0 reduce-scatter.2.cloned.1.call-update
  185.2 0.8 copy-done.3
  186.1 0.5 fusion.13
  186.5 7.4 %psum.45 = f32[128]{0:T(128)S(1)} all-reduce(f32[128]{0:T(128)S(1)} %get-tuple-element.13), channel_id=1, replica_groups=mesh['pipe'=8,'dp'=16,'tensor'=4] {'tensor'}, use_global_device_ids=true, to_apply=%region_6.0 | all-reduce | flops 128 | bytes 1024 | tf_op jit(solution)/shard_map/psum | solution.py:56
  193.9 0.0 copy-done.7
  193.9 0.2 convolution_convert_fusion.2
  194.1 122.9 %psum.47 = bf16[256,32]{0,1:T(8,128)(2,1)S(1)} all-reduce(bf16[256,32]{0,1:T(8,128)(2,1)S(1)} %convolution_convert_fusion.2), channel_id=1, replica_groups=mesh['pipe'=8,'dp'=16,'tensor'=4] {'dp'}, use_global_device_ids=true, to_apply=%region_8.0 | all-reduce | flops 8192 | bytes 32768 | tf_op jit(solution)/shard_map/psum | solution.py:63
  317.0 0.0 copy-done.8
  317.0 0.6 multiply_bitcast_fusion.1
  317.6 125.5 %all-reduce.6.cloned.1.call-done = bf16[1536,256]{1,0:T(8,128)(2,1)} async-done(((bf16[1536,256]{1,0:T(8,128)(2,1)}), bf16[1536,256]{1,0:T(8,128)(2,1)}) %all-reduce.6.cloned.1.call-update) | async-done | bytes 786448 | tf_op jit(solution)/shard_map/psum | solution.py:62
  443.2 2.4 multiply_bitcast_fusion
  445.5 85.3 %reduce-scatter.2.cloned.1.call-done = bf16[1,128,1536]{2,1,0:T(8,128)(2,1)} async-done(((bf16[8,128,1536]{2,1,0:T(8,128)(2,1)}), bf16[1,128,1536]{2,1,0:T(8,128)(2,1)}) %reduce-scatter.2.cloned.1.call-update) | async-done | bytes 393232 | tf_op jit(solution)/shard_map/reduce_scatter | solution.py:38
  530.8 0.0 copy-done.5
  530.8 2.0 fusion.26
  (5 shorter events, 0.0 us)
Async XLA Ops:
  7.2 116.5 %copy-start = (bf16[1,1536,256]{2,1,0:T(8,128)(2,1)S(1)}, bf16[1,1536,256]{2,1,0:T(8,128)(2,1)}, u32[]{:S(2)}) copy-start(bf16[1,1536,256]{2,1,0:T(8,128)(2,1)} %param.8) | copy-start | bytes 2359300
  7.2 92.2 %all-gather.2.cloned.1.call-start = ((), (), s32[]{:S(2)}) async-start(), calls=%async_computation.3 | async-start | bytes 3538944 | tf_op jit(solution)/shard_map/all_gather | solution.py:44
  7.9 168.3 %all-reduce.4.cloned.1.call-start = ((), (), s32[]{:S(2)}) async-start(), calls=%async_computation.1 | async-start | bytes 131072 | tf_op jit(solution)/shard_map/psum | solution.py:25
  8.0 116.7 %copy-start.6 = (f32[8]{0:T(128)}, f32[8]{0:T(128)S(1)}, u32[]{:S(2)}) copy-start(f32[8]{0:T(128)S(1)} %compare_convert_fusion) | copy-start | bytes 100
  99.4 24.3 %copy-start.1 = (bf16[1,128,1536]{2,1,0:T(8,128)(2,1)S(1)}, bf16[1,128,1536]{2,1,0:T(8,128)(2,1)}, u32[]{:S(2)}) copy-start(bf16[1,128,1536]{2,1,0:T(8,128)(2,1)} %param.5) | copy-start | bytes 1179652
  123.1 0.5 copy-start.4
  124.6 318.5 %all-reduce.6.cloned.1.call-start = ((), (), s32[]{:S(2)}) async-start(), calls=%async_computation.4 | async-start | bytes 1572864 | tf_op jit(solution)/shard_map/psum | solution.py:62
  177.3 0.6 copy-start.2
  179.9 350.9 %reduce-scatter.2.cloned.1.call-start = ((), (), s32[]{:S(2)}) async-start(), calls=%async_computation.2 | async-start | bytes 3538944 | tf_op jit(solution)/shard_map/reduce_scatter | solution.py:38
  185.2 0.8 copy-start.3
  185.2 8.7 %copy-start.7 = (bf16[128,256]{1,0:T(8,128)(2,1)S(1)}, bf16[128,256]{1,0:T(8,128)(2,1)}, u32[]{:S(2)}) copy-start(bf16[128,256]{1,0:T(8,128)(2,1)} %all-reduce.4.cloned.1.call-done) | copy-start | bytes 196612
  185.2 131.8 %copy-start.8 = (f32[128]{0:T(128)S(1)}, f32[128]{0:T(128)}, u32[]{:S(2)}) copy-start(f32[128]{0:T(128)} %get-tuple-element.3) | copy-start | bytes 1540
  186.1 344.7 %copy-start.5 = (f32[128]{0:T(128)S(1)}, f32[128]{0:T(128)}, u32[]{:S(2)}) copy-start(f32[128]{0:T(128)} %copy-done.4) | copy-start | bytes 1540
Sparse Core Ops, SparseCore 0:
  10.1 89.2 all-gather.1
  124.8 51.4 all-reduce.3
  180.1 263.0 all-reduce.5
  445.9 84.9 reduce-scatter.1
where the time goes:
time: 540 us; the launch traced here: 539 us
  waiting for transfers between devices  347 us (64%)
  blocking collectives  147 us (27%)
  other arithmetic  16 us (3%)
  between operations  13.8 us (3%)
  matrix products  11.6 us (2%)
    psum x1, waiting for transfers between devices, on_device(): lax.psum(first_local.astype(jnp.bfloat16), 'dp').astype(jnp.float32)  126 us
    psum x1, blocking collectives, on_device(): lax.psum(second_local.astype(jnp.bfloat16), 'dp').astype(jnp.float32)  123 us
    all_gather x1, waiting for transfers between devices, on_device(): lax.all_gather(outputs, 'pipe', axis=0, tiled=True)  86.9 us
    reduce_scatter x1, waiting for transfers between devices, on_device(): lax.psum_scatter(result.astype(jnp.bfloat16), 'pipe', scatter_dimension=0...  85.3 us
    psum x1, waiting for transfers between devices, on_device(): lax.psum(jnp.dot(normed, w_first, preferred_element_type=jnp.float32).ast...  48.9 us
    psum x1, blocking collectives, on_device(): squares = lax.psum(jnp.sum(current * current, axis=1), 'tensor')  17.1 us
  transfers between devices with their start and end apart: 4, of which 4 were waited for; matrix products, arithmetic and copies ran while one was open for 3% of the time, Pallas kernels for 0%

commit v1 on v0

v1 whole, which is shorter than its diff:
```python
import functools

import jax
import jax.numpy as jnp
from jax import lax
from jax.experimental import pallas as pl
from jax.experimental.pallas import tpu as pltpu
from jax.sharding import PartitionSpec as P

D = 6144
epsilon = 1e-06
SPREAD = 8
LANES = 512

f32 = jnp.float32
bf16 = jnp.bfloat16


def call(kernel, shapes, flops, moved, scratch=(), smem=0, count=0):
    return pl.pallas_call(
        kernel,
        out_shape=shapes,
        in_specs=[pl.BlockSpec(memory_space=pltpu.SMEM)] * smem
        + [pl.BlockSpec(memory_space=pltpu.VMEM)] * (count - smem),
        out_specs=[pl.BlockSpec(memory_space=pltpu.VMEM)] * len(shapes),
        scratch_shapes=list(scratch),
        compiler_params=pltpu.CompilerParams(vmem_limit_bytes=20 * 1024 * 1024),
        cost_estimate=pl.CostEstimate(flops=flops, bytes_accessed=moved, transcendentals=0),
    )


def project_kernel(x_ref, gain_ref, weight_ref, packed_ref, scaled_ref):
    hidden = weight_ref.shape[1]
    tokens = x_ref.shape[0]
    x = x_ref[...].astype(f32)
    scaled = (x * gain_ref[...].astype(f32)).astype(bf16)
    scaled_ref[...] = scaled
    projected = jnp.dot(scaled, weight_ref[...], preferred_element_type=f32).astype(bf16)
    squares = jnp.broadcast_to(jnp.sum(x * x, axis=1, keepdims=True), (tokens, 128)).astype(bf16)
    for m in range(packed_ref.shape[0]):
        packed_ref[m, :, :hidden] = projected
        packed_ref[m, :, hidden:] = squares


def weights_of(mixed, layer, layers):
    lane = lax.broadcasted_iota(jnp.int32, mixed.shape, 1)
    return [
        jnp.sum(jnp.where(lane == jnp.where(layer < 0, -1, s * layers + layer), mixed, 0.0), axis=1, keepdims=True)
        for s in range(4)
    ]


def add_term(rows, lanes, weights, incoming_ref, total):
    for s in range(4):
        total = total + weights[s][rows] * incoming_ref[s, rows, lanes].astype(f32)
    return total


def put_products(held_ref, incoming_ref, products_ref, layer, layers):
    tokens = held_ref.shape[0]
    same = lax.broadcasted_iota(jnp.int32, (tokens, tokens), 0) == lax.broadcasted_iota(jnp.int32, (tokens, tokens), 1)
    for s in range(4):
        every = lax.dot_general(
            incoming_ref[s], held_ref[...], (((1,), (1,)), ((), ())), preferred_element_type=f32
        )
        products_ref[pl.ds(s * layers + layer, 1), :] = jnp.sum(jnp.where(same, every, 0.0), axis=0, keepdims=True)


def generate_kernel(
    parts_ref, weight_ref,
    mixing_ref, active_ref, slope_ref, preact_ref, factor_ref,
):
    hidden = weight_ref.shape[0]
    parts = parts_ref[...].astype(f32)
    packed = (parts[0] + parts[1]) + (parts[2] + parts[3])
    factor = lax.rsqrt(packed[:, hidden : hidden + 1] / D + epsilon)
    preact = factor * packed[:, :hidden]
    factor_ref[...] = jnp.broadcast_to(factor, factor_ref.shape)
    preact_ref[...] = preact
    inside = 0.7978845608028654 * (preact + 0.044715 * (preact * preact * preact))
    bent = jnp.tanh(inside)
    active = (0.5 * preact * (1.0 + bent)).astype(bf16)
    active_ref[...] = active
    slope_ref[...] = 0.5 * (1.0 + bent) + 0.5 * preact * (1.0 - bent * bent) * (
        0.7978845608028654 * (1.0 + 3 * 0.044715 * (preact * preact))
    )
    mixing_ref[...] = jnp.dot(active, weight_ref[...], preferred_element_type=f32)


def own_kernel(layers, place_ref, held_ref, incoming_ref, products_ref):
    products_ref[...] = jnp.zeros_like(products_ref)
    put_products(held_ref, incoming_ref, products_ref, place_ref[0], layers)


def depth_kernel(turn, chain, layers, place_ref, held_ref, incoming_ref, before_ref, products_ref):
    products_ref[...] = before_ref[...]

    @pl.when(place_ref[1] == chain)
    def _():
        put_products(held_ref, incoming_ref, products_ref, (place_ref[0] - (turn - 1)) & (layers - 1), layers)


def tiles(shape):
    return [(slice(r, r + 16), slice(at, at + LANES)) for r in range(0, shape[0], 16) for at in range(0, shape[1], LANES)]


def hop_kernel(turn, chain, layers, place_ref, held_ref, incoming_ref, mixing_ref, sent_ref):
    rising = place_ref[1] == chain

    @pl.when(rising)
    def _():
        sent_ref[...] = held_ref[...]

    @pl.when(jnp.logical_not(rising))
    def _():
        weights = weights_of(mixing_ref[...], place_ref[0] + turn - 1 - layers, layers)
        for rows, lanes in tiles(sent_ref.shape):
            total = add_term(rows, lanes, weights, incoming_ref, held_ref[rows, lanes].astype(f32))
            sent_ref[rows, lanes] = total.astype(bf16)


def finish_kernel(layers, place_ref, even_ref, odd_ref, incoming_ref, mixing_ref, generated_ref, out_ref):
    even = place_ref[1] == 0
    weights = weights_of(mixing_ref[...], place_ref[0], layers)
    for rows, lanes in tiles(out_ref.shape):
        came = jnp.where(even, odd_ref[rows, lanes].astype(f32), even_ref[rows, lanes].astype(f32))
        total = add_term(rows, lanes, weights, incoming_ref, came)
        out_ref[rows, lanes] = (total + generated_ref[rows, lanes]).astype(bf16)


def gradient_kernel(
    parts_ref, weight_ref, active_ref, slope_ref, preact_ref, factor_ref, turned_ref, local_ref, scaled_grad_ref, back_ref
):
    rows = turned_ref.shape[0] // SPREAD
    parts = parts_ref[...]
    products = (parts[0] + parts[1]) + (parts[2] + parts[3])
    depth_turned = products.astype(bf16)
    depth_grads = products.T.astype(bf16)
    dactive = jnp.dot(depth_grads, weight_ref[...], preferred_element_type=f32)
    dpreact = dactive * slope_ref[...]
    factor = factor_ref[...][:, :1]
    inner = jnp.sum(dpreact * preact_ref[...], axis=1, keepdims=True)
    back_ref[...] = jnp.broadcast_to(factor * factor * inner / D, back_ref.shape)
    scaled_grad = (dpreact * factor).astype(bf16)
    scaled_grad_ref[...] = scaled_grad
    second = jnp.dot(depth_turned, active_ref[...], preferred_element_type=f32).astype(bf16)
    half = second.shape[0] // 2
    for m in range(SPREAD):
        local_ref[m, :rows] = jnp.dot(
            turned_ref[m * rows : (m + 1) * rows], scaled_grad, preferred_element_type=f32
        ).astype(bf16)
        local_ref[m, rows:] = second[(m % 2) * half : (m % 2 + 1) * half]


def over_dp(local, chains):
    size = lax.axis_size("dp")
    groups = [[x * 4 + z * 2 + core for x in range(size // 4) for core in range(2)] for z in range(2)]
    arrived = lax.all_to_all(local, "dp", 0, 0, axis_index_groups=groups, tiled=True)
    mine = jnp.sum(arrived.astype(f32), axis=0).astype(bf16)
    mine, *chains = lax.optimization_barrier((mine, *chains))
    other = lax.ppermute(mine, "dp", [(i, i ^ 2) for i in range(size)])
    total = (mine.astype(f32) + other.astype(f32)).astype(bf16)
    spread = jnp.broadcast_to(total[None], local.shape)
    return lax.all_to_all(spread, "dp", 0, 0, axis_index_groups=groups, tiled=True), chains


def on_device(outputs, cotangents, gains, first_weight, second_weight):
    layers = lax.axis_size("pipe")
    section = lax.axis_index("pipe")
    size = lax.axis_size("dp")
    last = layers - 1
    current = outputs[0]
    incoming = cotangents[:, 0]
    tokens, width = current.shape
    hidden = first_weight.shape[2]
    columns = 4 * layers
    shape = jax.ShapeDtypeStruct
    place = jnp.stack([section, lax.axis_index("dp") & 1]).astype(jnp.int32)

    def hop(array, turn, chain):
        pairs = [(k * size + i, (k + 1) * size + i) for k in range(turn - 1, last) for i in range(chain, size, 2)]
        if turn > 1:
            pairs += [
                (k * size + i, (k - 1) * size + i) for k in range(layers + 1 - turn, layers) for i in range(1 - chain, size, 2)
            ]
        return lax.ppermute(array, ("pipe", "dp"), pairs)

    packed, scaled = call(
        project_kernel,
        [shape((4, tokens, hidden + 128), bf16), shape((tokens, width), bf16)],
        2 * tokens * width * hidden,
        4 * width * (tokens + hidden),
        count=3,
    )(current, gains, first_weight[0])
    scaled, current = lax.optimization_barrier((scaled, current))
    packed = lax.all_to_all(packed, "tensor", 0, 0, tiled=True)
    mixing, active, slope, preact, factor = call(
        generate_kernel,
        [
            shape((tokens, columns), f32),
            shape((tokens, hidden), bf16),
            shape((tokens, hidden), f32),
            shape((tokens, hidden), f32),
            shape((tokens, 128), f32),
        ],
        2 * tokens * hidden * columns,
        20 * tokens * hidden,
        count=2,
    )(packed, second_weight[0])
    [products] = call(
        functools.partial(own_kernel, layers),
        [shape((columns, tokens), f32)],
        8 * tokens * width,
        10 * tokens * width,
        smem=1,
        count=3,
    )(place, current, incoming)

    chains = [hop(current, 1, chain) for chain in range(2)]
    for turn in range(2, layers + 1):
        for chain in range(2):
            held = chains[chain]
            [sent] = call(
                functools.partial(hop_kernel, turn, chain, layers),
                [shape((tokens, width), bf16)],
                8 * tokens * width,
                12 * tokens * width,
                smem=1,
                count=4,
            )(place, held, incoming, mixing)
            chains[chain] = hop(sent, turn, chain)
            [products] = call(
                functools.partial(depth_kernel, turn, chain, layers),
                [shape((columns, tokens), f32)],
                8 * tokens * width,
                10 * tokens * width,
                smem=1,
                count=4,
            )(place, held, incoming, products)
        mixing, products = lax.optimization_barrier((mixing, products))

    spread = lax.all_to_all(jnp.broadcast_to(products[None], (4, columns, tokens)), "tensor", 0, 0, tiled=True)
    local, scaled_grad, back = call(
        gradient_kernel,
        [
            shape((SPREAD, width // SPREAD + columns // 2, hidden), bf16),
            shape((tokens, hidden), bf16),
            shape((tokens, 128), f32),
        ],
        2 * tokens * width * hidden,
        4 * width * (tokens + hidden),
        count=7,
    )(spread, second_weight[0].T, active, slope, preact, factor, scaled.T)
    summed, chains = over_dp(local, chains)
    summed = summed.astype(f32)
    divisor = tokens * size
    first_grads = summed[:, : width // SPREAD].reshape(width, hidden) / divisor
    second_grads = summed[:2, width // SPREAD :].reshape(columns, hidden).T / divisor

    weighted = lax.dot_general(scaled_grad, first_weight[0], (((1,), (1,)), ((), ())), preferred_element_type=f32)
    generated = weighted * gains[0].astype(f32)[None] - current.astype(f32) * back[:, :1]
    [output_grads] = call(
        functools.partial(finish_kernel, layers),
        [shape((tokens, width), bf16)],
        8 * tokens * width,
        16 * tokens * width,
        smem=1,
        count=6,
    )(place, chains[0], chains[1], incoming, mixing, generated)
    return (output_grads[None], first_grads[None], second_grads[None])


def solution(mesh):
    placed = (
        P("pipe", "dp", "tensor"),
        P(None, "pipe", "dp", "tensor"),
        P("pipe", "tensor"),
        P("pipe", "tensor", None),
        P("pipe", None, None),
    )
    return jax.shard_map(
        on_device,
        mesh=mesh,
        in_specs=placed,
        out_specs=(P("pipe", "dp", "tensor"), P("pipe", "tensor", None), P("pipe", None, None)),
        check_vma=False,
    )
```

time: 540 us -> 190 us (0.35)
  the two profiles are of different devices: /device:TPU:1 before, /device:TPU:96 now
where the time goes in v1:
time: 190 us; the launch traced here: 189 us
  waiting for transfers between devices  84.8 us (45%)
  starting transfers between devices  56.5 us (30%)
  Pallas kernels  29.9 us (16%)
  local copies, waits for them, and re-layouts  10.5 us (6%)
  other arithmetic  4.58 us (2%)
    ppermute x16, waiting for transfers between devices, hop(): return lax.ppermute(array, ('pipe', 'dp'), pairs)  41.9 us
    ppermute x16, starting transfers between devices, hop(): return lax.ppermute(array, ('pipe', 'dp'), pairs)  32 us
    pallas_call x14, Pallas kernels, on_device(): call(functools.partial(hop_kernel, turn, chain, layers), [shape((tokens,...  12.4 us
    pallas_call x14, Pallas kernels, on_device(): call(functools.partial(depth_kernel, turn, chain, layers), [shape((column...  12 us
    ppermute x1, waiting for transfers between devices, over_dp(): other = lax.ppermute(mine, 'dp', [(i, i ^ 2) for i in range(size)])  11.1 us
    all_to_all x1, waiting for transfers between devices, over_dp(): lax.all_to_all(spread, 'dp', 0, 0, axis_index_groups=groups, tiled=True)  10.5 us
    unnamed x34, local copies, waits for them, and re-layouts  8.5 us
    all_to_all x1, waiting for transfers between devices, over_dp(): lax.all_to_all(local, 'dp', 0, 0, axis_index_groups=groups, tiled=True)  8.3 us
  transfers between devices with their start and end apart: 21, of which 12 were waited for; matrix products, arithmetic and copies ran while one was open for 2% of the time, Pallas kernels for 15%

profile of v1, /device:TPU:96, one launch (start us, length us, event | category | flops | bytes accessed | tf_op | source)
XLA Modules:
  0.0 188.9 jit_solution(5588931050547916109)
XLA Ops:
  0.7 1.2 copy-done.1
  2.6 1.3 shard_map.76
  4.6 5.0 %collective-permute-start.1 = (bf16[128,1536]{1,0:T(8,128)(2,1)}, bf16[128,1536]{1,0:T(8,128)(2,1)S(1)}, u32[]{:S(2)}, u32[]{:S(2)}) collective-permute-start(bf16[128,1536]{1,0:T(8,128)(2,1)} %bitcast.2.x_ref.held_ref), channel_id=1, source_target_pairs={{0,64},{8,72},{16,80},{24,88},{32,96},{40,104},{48,112},{56,120},{... | collective-permute-start | bytes 1179656 | tf_op jit(solution)/shard_map/ppermute | solution.py:186
  10.4 4.5 %all-to-all-start = ((bf16[4,128,384]{2,1,0:T(8,128)(2,1)}), bf16[4,128,384]{2,1,0:T(8,128)(2,1)S(1)}, u32[]{:S(2)}, u32[]{:S(2)}) async-start(bf16[4,128,384]{2,1,0:T(8,128)(2,1)} %copy-done.4), calls=%async_computation | async-start | bytes 786432 | tf_op jit(solution)/shard_map/all_to_all | solution.py:196
  15.0 7.6 %all-to-all-done.parts_ref = bf16[4,128,384]{2,1,0:T(8,128)(2,1)S(1)} async-done(((bf16[4,128,384]{2,1,0:T(8,128)(2,1)}), bf16[4,128,384]{2,1,0:T(8,128)(2,1)S(1)}, u32[]{:S(2)}, u32[]{:S(2)}) %all-to-all-start) | async-done | bytes 393248 | tf_op jit(solution)/shard_map/all_to_all | solution.py:196
  24.8 3.8 %collective-permute-start.3 = (bf16[128,1536]{1,0:T(8,128)(2,1)S(1)}, bf16[128,1536]{1,0:T(8,128)(2,1)S(1)}, u32[]{:S(2)}, u32[]{:S(2)}) collective-permute-start(bf16[128,1536]{1,0:T(8,128)(2,1)S(1)} %shard_map.82), channel_id=1, source_target_pairs={{64,128},{72,136},{80,144},{88,152},{96,160},{104,168},{112,176},{... | collective-permute-start | bytes 1179656 | tf_op jit(solution)/shard_map/ppermute | solution.py:186
  28.6 1.0 shard_map.81
  30.3 1.6 shard_map.78.before_ref
  31.9 1.1 shard_map.79.before_ref
  33.6 3.9 %collective-permute-done.3.held_ref = bf16[128,1536]{1,0:T(8,128)(2,1)S(1)} collective-permute-done((bf16[128,1536]{1,0:T(8,128)(2,1)S(1)}, bf16[128,1536]{1,0:T(8,128)(2,1)S(1)}, u32[]{:S(2)}, u32[]{:S(2)}) %collective-permute-start.3) | collective-permute-done | bytes 393248 | tf_op jit(solution)/shard_map/ppermute | solution.py:186
  38.0 5.0 %collective-permute-start.5 = (bf16[128,1536]{1,0:T(8,128)(2,1)S(1)}, bf16[128,1536]{1,0:T(8,128)(2,1)S(1)}, u32[]{:S(2)}, u32[]{:S(2)}) collective-permute-start(bf16[128,1536]{1,0:T(8,128)(2,1)S(1)} %shard_map.86), channel_id=1, source_target_pairs={{128,192},{136,200},{144,208},{152,216},{160,224},{168,232},{176,2... | collective-permute-start | bytes 1179656 | tf_op jit(solution)/shard_map/ppermute | solution.py:186
  43.1 1.0 shard_map.85
  44.7 1.1 shard_map.83.before_ref
  46.4 4.0 %collective-permute-done.5.held_ref = bf16[128,1536]{1,0:T(8,128)(2,1)S(1)} collective-permute-done((bf16[128,1536]{1,0:T(8,128)(2,1)S(1)}, bf16[128,1536]{1,0:T(8,128)(2,1)S(1)}, u32[]{:S(2)}, u32[]{:S(2)}) %collective-permute-start.5) | collective-permute-done | bytes 393248 | tf_op jit(solution)/shard_map/ppermute | solution.py:186
  51.0 5.6 %collective-permute-start.7 = (bf16[128,1536]{1,0:T(8,128)(2,1)S(1)}, bf16[128,1536]{1,0:T(8,128)(2,1)S(1)}, u32[]{:S(2)}, u32[]{:S(2)}) collective-permute-start(bf16[128,1536]{1,0:T(8,128)(2,1)S(1)} %shard_map.90), channel_id=1, source_target_pairs={{192,256},{200,264},{208,272},{216,280},{224,288},{232,296},{240,3... | collective-permute-start | bytes 1179656 | tf_op jit(solution)/shard_map/ppermute | solution.py:186
  56.6 1.0 shard_map.89
  58.3 1.1 shard_map.87.before_ref
  60.0 3.0 %collective-permute-done.7.held_ref = bf16[128,1536]{1,0:T(8,128)(2,1)S(1)} collective-permute-done((bf16[128,1536]{1,0:T(8,128)(2,1)S(1)}, bf16[128,1536]{1,0:T(8,128)(2,1)S(1)}, u32[]{:S(2)}, u32[]{:S(2)}) %collective-permute-start.7) | collective-permute-done | bytes 393248 | tf_op jit(solution)/shard_map/ppermute | solution.py:186
  64.4 1.0 shard_map.93
  65.4 1.3 collective-permute-start.8
  66.7 1.1 shard_map.91.before_ref
  69.6 15.6 %collective-permute-done.8.held_ref = bf16[128,1536]{1,0:T(8,128)(2,1)S(1)} collective-permute-done((bf16[128,1536]{1,0:T(8,128)(2,1)S(1)}, bf16[128,1536]{1,0:T(8,128)(2,1)S(1)}, u32[]{:S(2)}, u32[]{:S(2)}) %collective-permute-start.8) | collective-permute-done | bytes 393248 | tf_op jit(solution)/shard_map/ppermute | solution.py:186
  85.2 1.0 shard_map.97
  86.2 1.9 %collective-permute-start.10 = (bf16[128,1536]{1,0:T(8,128)(2,1)S(1)}, bf16[128,1536]{1,0:T(8,128)(2,1)S(1)}, u32[]{:S(2)}, u32[]{:S(2)}) collective-permute-start(bf16[128,1536]{1,0:T(8,128)(2,1)S(1)} %shard_map.97), channel_id=1, source_target_pairs={{324,388},{332,396},{340,404},{348,412},{356,420},{364,428},{372,4... | collective-permute-start | bytes 1179656 | tf_op jit(solution)/shard_map/ppermute | solution.py:186
  88.1 1.1 shard_map.95.before_ref
  91.1 8.2 %collective-permute-done.10.held_ref = bf16[128,1536]{1,0:T(8,128)(2,1)S(1)} collective-permute-done((bf16[128,1536]{1,0:T(8,128)(2,1)S(1)}, bf16[128,1536]{1,0:T(8,128)(2,1)S(1)}, u32[]{:S(2)}, u32[]{:S(2)}) %collective-permute-start.10) | collective-permute-done | bytes 393248 | tf_op jit(solution)/shard_map/ppermute | solution.py:186
  99.3 1.0 shard_map.101
  100.3 1.9 %collective-permute-start.12 = (bf16[128,1536]{1,0:T(8,128)(2,1)S(1)}, bf16[128,1536]{1,0:T(8,128)(2,1)S(1)}, u32[]{:S(2)}, u32[]{:S(2)}) collective-permute-start(bf16[128,1536]{1,0:T(8,128)(2,1)S(1)} %shard_map.101), channel_id=1, source_target_pairs={{388,452},{396,460},{404,468},{412,476},{420,484},{428,492},{436,5... | collective-permute-start | bytes 1179656 | tf_op jit(solution)/shard_map/ppermute | solution.py:186
  102.3 1.1 shard_map.99.before_ref
  104.0 1.3 shard_map.103.before_ref
  105.3 5.9 %collective-permute-done.12.held_ref = bf16[128,1536]{1,0:T(8,128)(2,1)S(1)} collective-permute-done((bf16[128,1536]{1,0:T(8,128)(2,1)S(1)}, bf16[128,1536]{1,0:T(8,128)(2,1)S(1)}, u32[]{:S(2)}, u32[]{:S(2)}) %collective-permute-start.12) | collective-permute-done | bytes 393248 | tf_op jit(solution)/shard_map/ppermute | solution.py:186
  112.4 3.3 %all-to-all-start.1 = ((f32[4,32,128]{2,1,0:T(8,128)}), f32[4,32,128]{2,1,0:T(8,128)S(1)}, u32[]{:S(2)}, u32[]{:S(2)}) async-start(f32[4,32,128]{2,1,0:T(8,128)} %broadcast_in_dim.8), calls=%async_computation.1 | async-start | bytes 131072 | tf_op jit(solution)/shard_map/all_to_all | solution.py:242
  115.9 5.4 %all-to-all-done.1.parts_ref = f32[4,32,128]{2,1,0:T(8,128)S(1)} async-done(((f32[4,32,128]{2,1,0:T(8,128)}), f32[4,32,128]{2,1,0:T(8,128)S(1)}, u32[]{:S(2)}, u32[]{:S(2)}) %all-to-all-start.1) | async-done | bytes 65568 | tf_op jit(solution)/shard_map/all_to_all | solution.py:242
  126.4 4.3 %all-to-all-start.2 = ((bf16[8,208,256]{2,1,0:T(8,128)(2,1)}), bf16[8,208,256]{2,1,0:T(8,128)(2,1)}, u32[]{:S(2)}, u32[]{:S(2)}) async-start(bf16[8,208,256]{2,1,0:T(8,128)(2,1)} %copy-done.3), calls=%async_computation.2 | async-start | bytes 1703936 | tf_op jit(solution)/shard_map/all_to_all | solution.py:158
  130.7 1.3 shard_map.106
  132.7 1.7 shard_map.107
  134.4 1.9 %collective-permute-start.15 = (bf16[128,1536]{1,0:T(8,128)(2,1)}, bf16[128,1536]{1,0:T(8,128)(2,1)S(1)}, u32[]{:S(2)}, u32[]{:S(2)}) collective-permute-start(bf16[128,1536]{1,0:T(8,128)(2,1)} %shard_map.107), channel_id=1, source_target_pairs={{64,0},{72,8},{80,16},{88,24},{96,32},{104,40},{112,48},{120,56},{... | collective-permute-start | bytes 1179656 | tf_op jit(solution)/shard_map/ppermute | solution.py:186
  136.3 8.3 %all-to-all-done.2 = bf16[8,208,256]{2,1,0:T(8,128)(2,1)} async-done(((bf16[8,208,256]{2,1,0:T(8,128)(2,1)}), bf16[8,208,256]{2,1,0:T(8,128)(2,1)}, u32[]{:S(2)}, u32[]{:S(2)}) %all-to-all-start.2) | async-done | bytes 852000 | tf_op jit(solution)/shard_map/all_to_all | solution.py:158
  144.6 1.3 reduce_sum.12
  146.0 1.3 collective-permute-done.15.odd_ref
  147.2 8.2 %collective-permute-start.16 = (bf16[208,256]{1,0:T(8,128)(2,1)S(1)}, bf16[208,256]{1,0:T(8,128)(2,1)S(1)}, u32[]{:S(2)}, u32[]{:S(2)}) collective-permute-start(bf16[208,256]{1,0:T(8,128)(2,1)S(1)} %reduce_sum.12), channel_id=1, source_target_pairs={{0,8},{4,12},{8,0},{12,4},{16,24},{20,28},{24,16},{28,20},{32,40},... | collective-permute-start | bytes 319496 | tf_op jit(solution)/shard_map/ppermute | solution.py:161
  155.5 11.1 %collective-permute-done.16 = bf16[208,256]{1,0:T(8,128)(2,1)S(1)} collective-permute-done((bf16[208,256]{1,0:T(8,128)(2,1)S(1)}, bf16[208,256]{1,0:T(8,128)(2,1)S(1)}, u32[]{:S(2)}, u32[]{:S(2)}) %collective-permute-start.16) | collective-permute-done | bytes 106528 | tf_op jit(solution)/shard_map/ppermute | solution.py:161
  167.6 4.2 %all-to-all-start.3 = ((bf16[8,208,256]{2,1,0:T(8,128)(2,1)}), bf16[8,208,256]{2,1,0:T(8,128)(2,1)}, u32[]{:S(2)}, u32[]{:S(2)}) async-start(bf16[8,208,256]{2,1,0:T(8,128)(2,1)} %broadcast_in_dim.10), calls=%async_computation.3 | async-start | bytes 1703936 | tf_op jit(solution)/shard_map/all_to_all | solution.py:164
  172.0 1.4 fusion.generated_ref
  173.4 1.8 shard_map.108
  175.2 10.5 %all-to-all-done.3 = bf16[8,208,256]{2,1,0:T(8,128)(2,1)} async-done(((bf16[8,208,256]{2,1,0:T(8,128)(2,1)}), bf16[8,208,256]{2,1,0:T(8,128)(2,1)}, u32[]{:S(2)}, u32[]{:S(2)}) %all-to-all-start.3) | async-done | bytes 852000 | tf_op jit(solution)/shard_map/all_to_all | solution.py:164
  185.7 1.3 convert_element_type.23
  187.6 1.3 slice_multiply_fusion
  (74 shorter events, 23.7 us)
Async XLA Ops:
  0.6 23.6 %copy-start = (bf16[4,1,128,1536]{3,2,1,0:T(8,128)(2,1)S(1)}, bf16[4,1,128,1536]{3,2,1,0:T(8,128)(2,1)}, u32[]{:S(2)}) copy-start(bf16[4,1,128,1536]{3,2,1,0:T(8,128)(2,1)} %param.6) | copy-start | bytes 4718596
  0.6 1.3 copy-start.1
  1.9 0.7 copy-start.15
  2.6 12.2 %copy-start.7 = (bf16[1,256,32]{1,2,0:T(8,128)(2,1)S(1)}, bf16[1,256,32]{1,2,0:T(8,128)(2,1)}, u32[]{:S(2)}) copy-start(bf16[1,256,32]{1,2,0:T(8,128)(2,1)} %param.9) | copy-start | bytes 49156
  3.9 0.7 copy-start.4
  4.6 19.5 %collective-permute-start.1 = (bf16[128,1536]{1,0:T(8,128)(2,1)}, bf16[128,1536]{1,0:T(8,128)(2,1)S(1)}, u32[]{:S(2)}, u32[]{:S(2)}) collective-permute-start(bf16[128,1536]{1,0:T(8,128)(2,1)} %bitcast.2.x_ref.held_ref), channel_id=1, source_target_pairs={{0,64},{8,72},{16,80},{24,88},{32,96},{40,104},{48,112},{56,120},{... | collective-permute-start | bytes 1179656 | tf_op jit(solution)/shard_map/ppermute | solution.py:186
  9.7 18.9 %collective-permute-start = (bf16[128,1536]{1,0:T(8,128)(2,1)}, bf16[128,1536]{1,0:T(8,128)(2,1)S(1)}, u32[]{:S(2)}, u32[]{:S(2)}) collective-permute-start(bf16[128,1536]{1,0:T(8,128)(2,1)} %bitcast.2.x_ref.held_ref), channel_id=1, source_target_pairs={{4,68},{12,76},{20,84},{28,92},{36,100},{44,108},{52,116},{60,124}... | collective-permute-start | bytes 1179656 | tf_op jit(solution)/shard_map/ppermute | solution.py:186
  10.4 12.3 %all-to-all-start = ((bf16[4,128,384]{2,1,0:T(8,128)(2,1)}), bf16[4,128,384]{2,1,0:T(8,128)(2,1)S(1)}, u32[]{:S(2)}, u32[]{:S(2)}) async-start(bf16[4,128,384]{2,1,0:T(8,128)(2,1)} %copy-done.4), calls=%async_computation | async-start | bytes 786432 | tf_op jit(solution)/shard_map/all_to_all | solution.py:196
  22.9 0.6 copy-start.11
  23.5 0.6 copy-start.13
  24.8 12.7 %collective-permute-start.3 = (bf16[128,1536]{1,0:T(8,128)(2,1)S(1)}, bf16[128,1536]{1,0:T(8,128)(2,1)S(1)}, u32[]{:S(2)}, u32[]{:S(2)}) collective-permute-start(bf16[128,1536]{1,0:T(8,128)(2,1)S(1)} %shard_map.82), channel_id=1, source_target_pairs={{64,128},{72,136},{80,144},{88,152},{96,160},{104,168},{112,176},{... | collective-permute-start | bytes 1179656 | tf_op jit(solution)/shard_map/ppermute | solution.py:186
  29.6 13.5 %collective-permute-start.2 = (bf16[128,1536]{1,0:T(8,128)(2,1)S(1)}, bf16[128,1536]{1,0:T(8,128)(2,1)S(1)}, u32[]{:S(2)}, u32[]{:S(2)}) collective-permute-start(bf16[128,1536]{1,0:T(8,128)(2,1)S(1)} %shard_map.81), channel_id=1, source_target_pairs={{68,132},{76,140},{84,148},{92,156},{100,164},{108,172},{116,180},... | collective-permute-start | bytes 1179656 | tf_op jit(solution)/shard_map/ppermute | solution.py:186
  38.0 12.4 %collective-permute-start.5 = (bf16[128,1536]{1,0:T(8,128)(2,1)S(1)}, bf16[128,1536]{1,0:T(8,128)(2,1)S(1)}, u32[]{:S(2)}, u32[]{:S(2)}) collective-permute-start(bf16[128,1536]{1,0:T(8,128)(2,1)S(1)} %shard_map.86), channel_id=1, source_target_pairs={{128,192},{136,200},{144,208},{152,216},{160,224},{168,232},{176,2... | collective-permute-start | bytes 1179656 | tf_op jit(solution)/shard_map/ppermute | solution.py:186
  44.0 12.6 %collective-permute-start.4 = (bf16[128,1536]{1,0:T(8,128)(2,1)S(1)}, bf16[128,1536]{1,0:T(8,128)(2,1)S(1)}, u32[]{:S(2)}, u32[]{:S(2)}) collective-permute-start(bf16[128,1536]{1,0:T(8,128)(2,1)S(1)} %shard_map.85), channel_id=1, source_target_pairs={{132,196},{140,204},{148,212},{156,220},{164,228},{172,236},{180,2... | collective-permute-start | bytes 1179656 | tf_op jit(solution)/shard_map/ppermute | solution.py:186
  51.0 12.1 %collective-permute-start.7 = (bf16[128,1536]{1,0:T(8,128)(2,1)S(1)}, bf16[128,1536]{1,0:T(8,128)(2,1)S(1)}, u32[]{:S(2)}, u32[]{:S(2)}) collective-permute-start(bf16[128,1536]{1,0:T(8,128)(2,1)S(1)} %shard_map.90), channel_id=1, source_target_pairs={{192,256},{200,264},{208,272},{216,280},{224,288},{232,296},{240,3... | collective-permute-start | bytes 1179656 | tf_op jit(solution)/shard_map/ppermute | solution.py:186
  57.6 6.7 %collective-permute-start.6 = (bf16[128,1536]{1,0:T(8,128)(2,1)S(1)}, bf16[128,1536]{1,0:T(8,128)(2,1)S(1)}, u32[]{:S(2)}, u32[]{:S(2)}) collective-permute-start(bf16[128,1536]{1,0:T(8,128)(2,1)S(1)} %shard_map.89), channel_id=1, source_target_pairs={{196,260},{204,268},{212,276},{220,284},{228,292},{236,300},{244,3... | collective-permute-start | bytes 1179656 | tf_op jit(solution)/shard_map/ppermute | solution.py:186
  63.7 4.7 %collective-permute-start.9 = (bf16[128,1536]{1,0:T(8,128)(2,1)S(1)}, bf16[128,1536]{1,0:T(8,128)(2,1)S(1)}, u32[]{:S(2)}, u32[]{:S(2)}) collective-permute-start(bf16[128,1536]{1,0:T(8,128)(2,1)S(1)} %shard_map.94), channel_id=1, source_target_pairs={{256,320},{264,328},{272,336},{280,344},{288,352},{296,360},{304,3... | collective-permute-start | bytes 1179656 | tf_op jit(solution)/shard_map/ppermute | solution.py:186
  65.4 19.9 %collective-permute-start.8 = (bf16[128,1536]{1,0:T(8,128)(2,1)S(1)}, bf16[128,1536]{1,0:T(8,128)(2,1)S(1)}, u32[]{:S(2)}, u32[]{:S(2)}) collective-permute-start(bf16[128,1536]{1,0:T(8,128)(2,1)S(1)} %shard_map.93), channel_id=1, source_target_pairs={{260,324},{268,332},{276,340},{284,348},{292,356},{300,364},{308,3... | collective-permute-start | bytes 1179656 | tf_op jit(solution)/shard_map/ppermute | solution.py:186
  69.0 20.9 %collective-permute-start.11 = (bf16[128,1536]{1,0:T(8,128)(2,1)S(1)}, bf16[128,1536]{1,0:T(8,128)(2,1)S(1)}, u32[]{:S(2)}, u32[]{:S(2)}) collective-permute-start(bf16[128,1536]{1,0:T(8,128)(2,1)S(1)} %shard_map.98), channel_id=1, source_target_pairs={{320,384},{328,392},{336,400},{344,408},{352,416},{360,424},{368,4... | collective-permute-start | bytes 1179656 | tf_op jit(solution)/shard_map/ppermute | solution.py:186
  86.2 13.1 %collective-permute-start.10 = (bf16[128,1536]{1,0:T(8,128)(2,1)S(1)}, bf16[128,1536]{1,0:T(8,128)(2,1)S(1)}, u32[]{:S(2)}, u32[]{:S(2)}) collective-permute-start(bf16[128,1536]{1,0:T(8,128)(2,1)S(1)} %shard_map.97), channel_id=1, source_target_pairs={{324,388},{332,396},{340,404},{348,412},{356,420},{364,428},{372,4... | collective-permute-start | bytes 1179656 | tf_op jit(solution)/shard_map/ppermute | solution.py:186
  90.4 13.5 %collective-permute-start.13 = (bf16[128,1536]{1,0:T(8,128)(2,1)S(1)}, bf16[128,1536]{1,0:T(8,128)(2,1)S(1)}, u32[]{:S(2)}, u32[]{:S(2)}) collective-permute-start(bf16[128,1536]{1,0:T(8,128)(2,1)S(1)} %shard_map.102), channel_id=1, source_target_pairs={{384,448},{392,456},{400,464},{408,472},{416,480},{424,488},{432,4... | collective-permute-start | bytes 1179656 | tf_op jit(solution)/shard_map/ppermute | solution.py:186
  100.3 10.9 %collective-permute-start.12 = (bf16[128,1536]{1,0:T(8,128)(2,1)S(1)}, bf16[128,1536]{1,0:T(8,128)(2,1)S(1)}, u32[]{:S(2)}, u32[]{:S(2)}) collective-permute-start(bf16[128,1536]{1,0:T(8,128)(2,1)S(1)} %shard_map.101), channel_id=1, source_target_pairs={{388,452},{396,460},{404,468},{412,476},{420,484},{428,492},{436,5... | collective-permute-start | bytes 1179656 | tf_op jit(solution)/shard_map/ppermute | solution.py:186
  112.4 8.9 %all-to-all-start.1 = ((f32[4,32,128]{2,1,0:T(8,128)}), f32[4,32,128]{2,1,0:T(8,128)S(1)}, u32[]{:S(2)}, u32[]{:S(2)}) async-start(f32[4,32,128]{2,1,0:T(8,128)} %broadcast_in_dim.8), calls=%async_computation.1 | async-start | bytes 131072 | tf_op jit(solution)/shard_map/all_to_all | solution.py:242
  121.3 0.7 copy-start.8
  122.0 0.8 copy-start.12
  122.8 0.8 copy-start.14
  124.2 0.9 copy-start.3
  125.2 0.6 copy-start.5
  125.8 0.6 copy-start.9
  126.4 18.2 %all-to-all-start.2 = ((bf16[8,208,256]{2,1,0:T(8,128)(2,1)}), bf16[8,208,256]{2,1,0:T(8,128)(2,1)}, u32[]{:S(2)}, u32[]{:S(2)}) async-start(bf16[8,208,256]{2,1,0:T(8,128)(2,1)} %copy-done.3), calls=%async_computation.2 | async-start | bytes 1703936 | tf_op jit(solution)/shard_map/all_to_all | solution.py:158
  132.0 14.0 %collective-permute-start.14 = (bf16[128,1536]{1,0:T(8,128)(2,1)}, bf16[128,1536]{1,0:T(8,128)(2,1)S(1)}, u32[]{:S(2)}, u32[]{:S(2)}) collective-permute-start(bf16[128,1536]{1,0:T(8,128)(2,1)} %shard_map.106), channel_id=1, source_target_pairs={{68,4},{76,12},{84,20},{92,28},{100,36},{108,44},{116,52},{124,60}... | collective-permute-start | bytes 1179656 | tf_op jit(solution)/shard_map/ppermute | solution.py:186
  134.4 12.8 %collective-permute-start.15 = (bf16[128,1536]{1,0:T(8,128)(2,1)}, bf16[128,1536]{1,0:T(8,128)(2,1)S(1)}, u32[]{:S(2)}, u32[]{:S(2)}) collective-permute-start(bf16[128,1536]{1,0:T(8,128)(2,1)} %shard_map.107), channel_id=1, source_target_pairs={{64,0},{72,8},{80,16},{88,24},{96,32},{104,40},{112,48},{120,56},{... | collective-permute-start | bytes 1179656 | tf_op jit(solution)/shard_map/ppermute | solution.py:186
  145.9 25.9 %copy-start.16 = (bf16[1,1536]{1,0:T(2,128)(2,1)S(1)}, bf16[1,1536]{1,0:T(2,128)(2,1)}, u32[]{:S(2)}) copy-start(bf16[1,1536]{1,0:T(2,128)(2,1)} %gain_ref.1) | copy-start | bytes 9220
  145.9 25.9 %copy-start.10 = (f32[128,128]{1,0:T(8,128)S(1)}, f32[128,128]{1,0:T(8,128)}, u32[]{:S(2)}) copy-start(f32[128,128]{1,0:T(8,128)} %copy-done.9) | copy-start | bytes 196612
  145.9 26.0 %copy-start.2 = (bf16[1,1536,256]{2,1,0:T(8,128)(2,1)S(1)}, bf16[1,1536,256]{2,1,0:T(8,128)(2,1)}, u32[]{:S(2)}) copy-start(bf16[1,1536,256]{2,1,0:T(8,128)(2,1)} %param.8) | copy-start | bytes 2359300
  146.0 26.0 %copy-start.6 = (bf16[128,256]{1,0:T(8,128)(2,1)S(1)}, bf16[128,256]{1,0:T(8,128)(2,1)}, u32[]{:S(2)}) copy-start(bf16[128,256]{1,0:T(8,128)(2,1)} %copy-done.5) | copy-start | bytes 196612
  147.2 19.4 %collective-permute-start.16 = (bf16[208,256]{1,0:T(8,128)(2,1)S(1)}, bf16[208,256]{1,0:T(8,128)(2,1)S(1)}, u32[]{:S(2)}, u32[]{:S(2)}) collective-permute-start(bf16[208,256]{1,0:T(8,128)(2,1)S(1)} %reduce_sum.12), channel_id=1, source_target_pairs={{0,8},{4,12},{8,0},{12,4},{16,24},{20,28},{24,16},{28,20},{32,40},... | collective-permute-start | bytes 319496 | tf_op jit(solution)/shard_map/ppermute | solution.py:161
  167.6 18.1 %all-to-all-start.3 = ((bf16[8,208,256]{2,1,0:T(8,128)(2,1)}), bf16[8,208,256]{2,1,0:T(8,128)(2,1)}, u32[]{:S(2)}, u32[]{:S(2)}) async-start(bf16[8,208,256]{2,1,0:T(8,128)(2,1)} %broadcast_in_dim.10), calls=%async_computation.3 | async-start | bytes 1703936 | tf_op jit(solution)/shard_map/all_to_all | solution.py:164

commit v2 on v1

v2 whole, which is shorter than its diff:
```python
import functools

import jax
import jax.numpy as jnp
from jax import lax
from jax.experimental import pallas as pl
from jax.experimental.pallas import tpu as pltpu
from jax.sharding import PartitionSpec as P

D = 6144
epsilon = 1e-06
LAG = 2
LANES = 512

f32 = jnp.float32
bf16 = jnp.bfloat16


def call(kernel, shapes, flops, moved, scratch=(), smem=0, count=0):
    return pl.pallas_call(
        kernel,
        out_shape=shapes,
        in_specs=[pl.BlockSpec(memory_space=pltpu.SMEM)] * smem
        + [pl.BlockSpec(memory_space=pltpu.VMEM)] * (count - smem),
        out_specs=[pl.BlockSpec(memory_space=pltpu.VMEM)] * len(shapes),
        scratch_shapes=list(scratch),
        compiler_params=pltpu.CompilerParams(vmem_limit_bytes=20 * 1024 * 1024),
        cost_estimate=pl.CostEstimate(flops=flops, bytes_accessed=moved, transcendentals=0),
    )


def project_kernel(x_ref, gain_ref, weight_ref, packed_ref, turned_ref):
    hidden = weight_ref.shape[1]
    tokens = x_ref.shape[0]
    x = x_ref[...].astype(f32)
    scaled = (x * gain_ref[...].astype(f32)).astype(bf16)
    turned_ref[...] = scaled.astype(f32).T.astype(bf16)
    projected = jnp.dot(scaled, weight_ref[...], preferred_element_type=f32).astype(bf16)
    squares = jnp.broadcast_to(jnp.sum(x * x, axis=1, keepdims=True), (tokens, 128)).astype(bf16)
    for m in range(packed_ref.shape[0]):
        packed_ref[m, :, :hidden] = projected
        packed_ref[m, :, hidden:] = squares


def weights_of(mixed, layer, layers):
    lane = lax.broadcasted_iota(jnp.int32, mixed.shape, 1)
    return [
        jnp.sum(jnp.where(lane == jnp.where(layer < 0, -1, s * layers + layer), mixed, 0.0), axis=1, keepdims=True)
        for s in range(4)
    ]


def add_term(rows, lanes, weights, incoming_ref, total):
    for s in range(4):
        total = total + weights[s][rows] * incoming_ref[s, rows, lanes].astype(f32)
    return total


def put_products(held_ref, incoming_ref, products_ref, layer, layers):
    tokens = held_ref.shape[0]
    same = lax.broadcasted_iota(jnp.int32, (tokens, tokens), 0) == lax.broadcasted_iota(jnp.int32, (tokens, tokens), 1)
    for s in range(4):
        every = lax.dot_general(
            incoming_ref[s], held_ref[...], (((1,), (1,)), ((), ())), preferred_element_type=f32
        )
        products_ref[pl.ds(s * layers + layer, 1), :] = jnp.sum(jnp.where(same, every, 0.0), axis=0, keepdims=True)


def generate_kernel(
    parts_ref, weight_ref, scaled_ref,
    mixing_ref, slope_ref, preact_ref, factor_ref, payload_ref,
):
    hidden = weight_ref.shape[0]
    parts = parts_ref[...].astype(f32)
    packed = (parts[0] + parts[1]) + (parts[2] + parts[3])
    factor = lax.rsqrt(packed[:, hidden : hidden + 1] / D + epsilon)
    preact = factor * packed[:, :hidden]
    factor_ref[...] = jnp.broadcast_to(factor, factor_ref.shape)
    preact_ref[...] = preact
    inside = 0.7978845608028654 * (preact + 0.044715 * (preact * preact * preact))
    bent = jnp.tanh(inside)
    active = (0.5 * preact * (1.0 + bent)).astype(bf16)
    slope = 0.5 * (1.0 + bent) + 0.5 * preact * (1.0 - bent * bent) * (
        0.7978845608028654 * (1.0 + 3 * 0.044715 * (preact * preact))
    )
    slope_ref[...] = slope
    first = (slope * factor).T.astype(bf16)
    second = active.astype(f32).T.astype(bf16)
    members, chunk = payload_ref.shape[0], payload_ref.shape[1] - 2 * hidden
    for m in range(members):
        payload_ref[m, :chunk] = scaled_ref[m * chunk : (m + 1) * chunk]
        payload_ref[m, chunk : chunk + hidden] = first
        payload_ref[m, chunk + hidden :] = second
    mixing_ref[...] = jnp.dot(active, weight_ref[...], preferred_element_type=f32)


def own_kernel(layers, place_ref, held_ref, incoming_ref, products_ref):
    products_ref[...] = jnp.zeros_like(products_ref)

    @pl.when(place_ref[1] == 0)
    def _():
        put_products(held_ref, incoming_ref, products_ref, place_ref[0], layers)


def depth_kernel(turn, layers, place_ref, held_ref, incoming_ref, before_ref, products_ref):
    products_ref[...] = before_ref[...]

    @pl.when(place_ref[1] == 0)
    def _():
        put_products(held_ref, incoming_ref, products_ref, (place_ref[0] - (turn - 1)) & (layers - 1), layers)


def tiles(shape):
    return [(slice(r, r + 16), slice(at, at + LANES)) for r in range(0, shape[0], 16) for at in range(0, shape[1], LANES)]


def hop_kernel(turn, layers, place_ref, held_ref, incoming_ref, mixing_ref, sent_ref):
    rising = place_ref[1] == 0

    @pl.when(rising)
    def _():
        sent_ref[...] = held_ref[...]

    @pl.when(jnp.logical_not(rising))
    def _():
        weights = weights_of(mixing_ref[...], place_ref[0] + turn - LAG - layers, layers)
        for rows, lanes in tiles(sent_ref.shape):
            total = add_term(rows, lanes, weights, incoming_ref, held_ref[rows, lanes].astype(f32))
            sent_ref[rows, lanes] = total.astype(bf16)


def finish_kernel(layers, place_ref, given_ref, kept_ref, incoming_ref, mixing_ref, generated_ref, out_ref):
    even = place_ref[1] == 0
    weights = weights_of(mixing_ref[...], place_ref[0], layers)
    for rows, lanes in tiles(out_ref.shape):
        came = jnp.where(even, given_ref[rows, lanes].astype(f32), kept_ref[rows, lanes].astype(f32))
        total = add_term(rows, lanes, weights, incoming_ref, came)
        out_ref[rows, lanes] = (total + generated_ref[rows, lanes]).astype(bf16)


def depth_grad_kernel(parts_ref, spread_ref):
    parts = parts_ref[...]
    turned = ((parts[0] + parts[1]) + (parts[2] + parts[3])).astype(bf16)
    for m in range(spread_ref.shape[0]):
        spread_ref[m] = turned


def chunk_kernel(depth_ref, weight_ref, gathered_ref, mine_ref):
    hidden, columns = weight_ref.shape
    members, rows = gathered_ref.shape[0], gathered_ref.shape[1] - 2 * hidden
    first = jnp.zeros((rows, hidden), f32)
    second = jnp.zeros((columns, hidden), f32)
    across = (((1,), (1,)), ((), ()))
    for m in range(members):
        depth = depth_ref[m // 2 * 2, m % 2 * columns : (m % 2 + 1) * columns]
        dactive = jnp.dot(weight_ref[...], depth, preferred_element_type=f32)
        scaled_grad = (dactive * gathered_ref[m, rows : rows + hidden].astype(f32)).astype(bf16)
        first = first + lax.dot_general(gathered_ref[m, :rows], scaled_grad, across, preferred_element_type=f32)
        second = second + lax.dot_general(depth, gathered_ref[m, rows + hidden :], across, preferred_element_type=f32)
    mine_ref[:rows] = first.astype(bf16)
    mine_ref[rows:] = second.astype(bf16)


def gradient_kernel(place_ref, depth_ref, weight_ref, slope_ref, preact_ref, factor_ref, scaled_grad_ref, back_ref):
    both = depth_ref[place_ref[2]].astype(f32)
    columns = weight_ref.shape[0]
    depth_grads = jnp.where(place_ref[1] == 0, both[:columns], both[columns:]).T.astype(bf16)
    dactive = jnp.dot(depth_grads, weight_ref[...], preferred_element_type=f32)
    dpreact = dactive * slope_ref[...]
    factor = factor_ref[...][:, :1]
    inner = jnp.sum(dpreact * preact_ref[...], axis=1, keepdims=True)
    back_ref[...] = jnp.broadcast_to(factor * factor * inner / D, back_ref.shape)
    scaled_grad_ref[...] = (dpreact * factor).astype(bf16)


def on_device(outputs, cotangents, gains, first_weight, second_weight):
    layers = lax.axis_size("pipe")
    section = lax.axis_index("pipe")
    size = lax.axis_size("dp")
    last = layers - 1
    current = outputs[0]
    incoming = cotangents[:, 0]
    tokens, width = current.shape
    hidden = first_weight.shape[2]
    columns = 4 * layers
    shape = jax.ShapeDtypeStruct
    index = lax.axis_index("dp")
    even = lax.shift_right_logical(index, 2) * 2
    place = jnp.stack([section, index & 1, even]).astype(jnp.int32)
    members = size // 2
    chunk = width // members
    groups = [[x * 4 + z * 2 + core for x in range(size // 4) for core in range(2)] for z in range(2)]

    def swap(array):
        return lax.ppermute(array, "dp", [(i, i ^ 1) for i in range(size)])

    def hop(array, turn):
        pairs = [(k * size + i, (k + 1) * size + i) for k in range(turn - 1, last) for i in range(0, size, 2)]
        if turn > LAG:
            pairs += [(k * size + i, (k - 1) * size + i) for k in range(layers + LAG - turn, layers) for i in range(1, size, 2)]
        return lax.ppermute(array, ("pipe", "dp"), pairs)

    swapped, incoming = lax.optimization_barrier((swap(current), incoming))
    halves = [current, swapped]
    chains = [hop(halves[h], 1) for h in range(2)]
    across = swap(incoming)
    rising = [incoming, across]
    falling = [across, incoming]

    packed, scaled_turned = call(
        project_kernel,
        [shape((4, tokens, hidden + 128), bf16), shape((width, tokens), bf16)],
        2 * tokens * width * hidden,
        4 * width * (tokens + hidden),
        count=3,
    )(current, gains, first_weight[0])
    packed = lax.all_to_all(packed, "tensor", 0, 0, tiled=True)
    mixing, slope, preact, factor, payload = call(
        generate_kernel,
        [
            shape((tokens, columns), f32),
            shape((tokens, hidden), f32),
            shape((tokens, hidden), f32),
            shape((tokens, 128), f32),
            shape((members, chunk + 2 * hidden, tokens), bf16),
        ],
        2 * tokens * hidden * columns,
        20 * tokens * hidden,
        count=3,
    )(packed, second_weight[0], scaled_turned)
    mixings = [swap(mixing), mixing]
    products = [
        call(
            functools.partial(own_kernel, layers),
            [shape((columns, tokens), f32)],
            8 * tokens * width,
            10 * tokens * width,
            smem=1,
            count=3,
        )(place, halves[h], rising[h])[0]
        for h in range(2)
    ]

    def advance(turn, h):
        if turn <= LAG:
            return hop(chains[h], turn)
        [sent] = call(
            functools.partial(hop_kernel, turn, layers),
            [shape((tokens, width), bf16)],
            8 * tokens * width,
            12 * tokens * width,
            smem=1,
            count=4,
        )(place, chains[h], falling[h], mixings[h])
        return hop(sent, turn)

    for turn in range(2, layers + 1):
        for h in range(2):
            held = chains[h]
            chains[h] = advance(turn, h)
            [products[h]] = call(
                functools.partial(depth_kernel, turn, layers),
                [shape((columns, tokens), f32)],
                8 * tokens * width,
                10 * tokens * width,
                smem=1,
                count=4,
            )(place, held, rising[h], products[h])
        if turn == LAG:
            payload, *products = lax.optimization_barrier((payload, *products))
            gathered = lax.all_to_all(payload, "dp", 0, 0, axis_index_groups=groups, tiled=True)
        if turn == 2 * LAG:
            gathered, *products = lax.optimization_barrier((gathered, *products))
        *mixings, products[0], products[1] = lax.optimization_barrier((*mixings, *products))

    both = jnp.concatenate(products, axis=0)
    spread = lax.all_to_all(jnp.broadcast_to(both[None], (4, *both.shape)), "tensor", 0, 0, tiled=True)
    [depth_grads] = call(depth_grad_kernel, [shape((members, 2 * columns, tokens), bf16)], 0, 8 * columns * tokens, count=1)(spread)
    depth_all = lax.all_to_all(depth_grads, "dp", 0, 0, axis_index_groups=groups, tiled=True)
    [mine] = call(
        chunk_kernel,
        [shape((chunk + columns, hidden), bf16)],
        2 * tokens * width * hidden,
        4 * members * tokens * hidden,
        count=3,
    )(depth_all, second_weight[0], gathered)
    mine, *chains = lax.optimization_barrier((mine, *chains))
    other = lax.ppermute(mine, "dp", [(i, i ^ 2) for i in range(size)])
    for turn in range(layers + 1, layers + LAG):
        chains = [advance(turn, h) for h in range(2)]
    other, *chains = lax.optimization_barrier((other, *chains))
    total = mine.astype(f32) + other.astype(f32)
    divisor = tokens * size
    second_grads = total[chunk:].T / divisor
    spread = jnp.broadcast_to(total[None, :chunk].astype(bf16), (members, chunk, hidden))
    summed = lax.all_to_all(spread, "dp", 0, 0, axis_index_groups=groups, tiled=True)
    first_grads = summed.astype(f32).reshape(width, hidden) / divisor

    scaled_grad, back = call(
        gradient_kernel,
        [shape((tokens, hidden), bf16), shape((tokens, 128), f32)],
        2 * tokens * hidden * columns,
        16 * tokens * hidden,
        smem=1,
        count=6,
    )(place, depth_all, second_weight[0].T, slope, preact, factor)

    weighted = lax.dot_general(scaled_grad, first_weight[0], (((1,), (1,)), ((), ())), preferred_element_type=f32)
    generated = weighted * gains[0].astype(f32)[None] - current.astype(f32) * back[:, :1]
    given = lax.ppermute(chains[0], "dp", [(i, i ^ 1) for i in range(1, size, 2)])
    [output_grads] = call(
        functools.partial(finish_kernel, layers),
        [shape((tokens, width), bf16)],
        8 * tokens * width,
        16 * tokens * width,
        smem=1,
        count=6,
    )(place, given, chains[1], incoming, mixing, generated)
    return (output_grads[None], first_grads[None], second_grads[None])


def solution(mesh):
    placed = (
        P("pipe", "dp", "tensor"),
        P(None, "pipe", "dp", "tensor"),
        P("pipe", "tensor"),
        P("pipe", "tensor", None),
        P("pipe", None, None),
    )
    return jax.shard_map(
        on_device,
        mesh=mesh,
        in_specs=placed,
        out_specs=(P("pipe", "dp", "tensor"), P("pipe", "tensor", None), P("pipe", None, None)),
        check_vma=False,
    )
```

time: 190 us -> 183 us (0.963)
  the two profiles are of different devices: /device:TPU:96 before, /device:TPU:224 now
where the time goes in v2:
time: 183 us; the launch traced here: 181 us
  starting transfers between devices  53.4 us (29%)
  waiting for transfers between devices  50.9 us (28%)
  Pallas kernels  36.7 us (20%)
  blocking collectives  19.1 us (10%)
  local copies, waits for them, and re-layouts  15.2 us (8%)
  other arithmetic  3.93 us (2%)
    ppermute x18, waiting for transfers between devices, hop(): return lax.ppermute(array, ('pipe', 'dp'), pairs)  26.5 us
    ppermute x18, starting transfers between devices, hop(): return lax.ppermute(array, ('pipe', 'dp'), pairs)  21.5 us
    pallas_call x14, Pallas kernels, on_device(): call(functools.partial(depth_kernel, turn, layers), [shape((columns, toke...  17.7 us
    unnamed x54, local copies, waits for them, and re-layouts  13.4 us
    all_to_all x1, blocking collectives, on_device(): lax.all_to_all(depth_grads, 'dp', 0, 0, axis_index_groups=groups, tiled=T...  10.7 us
    pallas_call x14, Pallas kernels, advance(): call(functools.partial(hop_kernel, turn, layers), [shape((tokens, width),...  10.7 us
    ppermute x1, starting transfers between devices, on_device(): other = lax.ppermute(mine, 'dp', [(i, i ^ 2) for i in range(size)])  9.11 us
    ppermute x1, waiting for transfers between devices, on_device(): other = lax.ppermute(mine, 'dp', [(i, i ^ 2) for i in range(size)])  8.53 us
  transfers between devices with their start and end apart: 26, of which 18 were waited for; matrix products, arithmetic and copies ran while one was open for 2% of the time, Pallas kernels for 19%

profile of v2, /device:TPU:224, one launch (start us, length us, event | category | flops | bytes accessed | tf_op | source)
XLA Modules:
  0.0 180.9 jit_solution(6011821662079729514)
XLA Ops:
  0.6 2.1 %collective-permute-start.2 = (bf16[128,1536]{1,0:T(8,128)(2,1)}, bf16[128,1536]{1,0:T(8,128)(2,1)}, u32[]{:S(2)}, u32[]{:S(2)}) collective-permute-start(bf16[128,1536]{1,0:T(8,128)(2,1)} %bitcast.36), channel_id=1, source_target_pairs={{0,4},{4,0},{8,12},{12,8},{16,20},{20,16},{24,28},{28,24},{32,36},... | collective-permute-start | bytes 1179656 | tf_op jit(solution)/shard_map/ppermute | solution.py:195
  2.7 2.0 %collective-permute-done.2.held_ref = bf16[128,1536]{1,0:T(8,128)(2,1)} collective-permute-done((bf16[128,1536]{1,0:T(8,128)(2,1)}, bf16[128,1536]{1,0:T(8,128)(2,1)}, u32[]{:S(2)}, u32[]{:S(2)}) %collective-permute-start.2) | collective-permute-done | bytes 393248 | tf_op jit(solution)/shard_map/ppermute | solution.py:195
  4.7 2.0 %collective-permute-start.4 = (bf16[4,128,1536]{2,1,0:T(8,128)(2,1)}, bf16[4,128,1536]{2,1,0:T(8,128)(2,1)S(1)}, u32[]{:S(2)}, u32[]{:S(2)}) collective-permute-start(bf16[4,128,1536]{2,1,0:T(8,128)(2,1)} %bitcast.19), channel_id=1, source_target_pairs={{0,4},{4,0},{8,12},{12,8},{16,20},{20,16},{24,28},{28,24},{32,36},... | collective-permute-start | bytes 4718600 | tf_op jit(solution)/shard_map/ppermute | solution.py:195
  6.8 1.3 collective-permute-start.1
  8.1 1.3 collective-permute-start.3
  14.0 4.5 %all-to-all-start = ((bf16[4,128,384]{2,1,0:T(8,128)(2,1)}), bf16[4,128,384]{2,1,0:T(8,128)(2,1)S(1)}, u32[]{:S(2)}, u32[]{:S(2)}) async-start(bf16[4,128,384]{2,1,0:T(8,128)(2,1)} %copy-done.11), calls=%async_computation | async-start | bytes 786432 | tf_op jit(solution)/shard_map/all_to_all | solution.py:217
  19.3 8.0 %all-to-all-done.parts_ref = bf16[4,128,384]{2,1,0:T(8,128)(2,1)S(1)} async-done(((bf16[4,128,384]{2,1,0:T(8,128)(2,1)}), bf16[4,128,384]{2,1,0:T(8,128)(2,1)S(1)}, u32[]{:S(2)}, u32[]{:S(2)}) %all-to-all-start) | async-done | bytes 393248 | tf_op jit(solution)/shard_map/all_to_all | solution.py:217
  34.5 1.6 shard_map.79.before_ref
  36.1 1.6 shard_map.80.before_ref
  37.7 1.6 shard_map.81.before_ref
  39.3 4.3 %all-to-all-start.1 = ((bf16[8,704,128]{2,1,0:T(8,128)(2,1)}), bf16[8,704,128]{2,1,0:T(8,128)(2,1)}, u32[]{:S(2)}, u32[]{:S(2)}) async-start(bf16[8,704,128]{2,1,0:T(8,128)(2,1)} %copy-done.8), calls=%async_computation.1 | async-start | bytes 2883584 | tf_op jit(solution)/shard_map/all_to_all | solution.py:271
  44.9 1.3 collective-permute-start.5
  46.2 1.9 %collective-permute-start = (f32[128,32]{1,0:T(8,128)S(1)}, f32[128,32]{1,0:T(8,128)S(1)}, u32[]{:S(2)}, u32[]{:S(2)}) collective-permute-start(f32[128,32]{1,0:T(8,128)S(1)} %get-tuple-element.96.mixing_ref), channel_id=1, source_target_pairs={{0,4},{4,0},{8,12},{12,8},{16,20},{20,16},{24,28},{28,24},{32,36},... | collective-permute-start | bytes 49160 | tf_op jit(solution)/shard_map/ppermute | solution.py:195
  49.4 4.1 %collective-permute-done.6.held_ref = bf16[128,1536]{1,0:T(8,128)(2,1)S(1)} collective-permute-done((bf16[128,1536]{1,0:T(8,128)(2,1)}, bf16[128,1536]{1,0:T(8,128)(2,1)S(1)}, u32[]{:S(2)}, u32[]{:S(2)}) %collective-permute-start.6) | collective-permute-done | bytes 393248 | tf_op jit(solution)/shard_map/ppermute | solution.py:201
  54.1 1.3 collective-permute-start.8
  55.4 2.3 %collective-permute-done.5.held_ref = bf16[128,1536]{1,0:T(8,128)(2,1)S(1)} collective-permute-done((bf16[128,1536]{1,0:T(8,128)(2,1)}, bf16[128,1536]{1,0:T(8,128)(2,1)S(1)}, u32[]{:S(2)}, u32[]{:S(2)}) %collective-permute-start.5) | collective-permute-done | bytes 393248 | tf_op jit(solution)/shard_map/ppermute | solution.py:201
  58.3 1.3 collective-permute-start.7
  61.9 1.9 %collective-permute-done.8.held_ref = bf16[128,1536]{1,0:T(8,128)(2,1)S(1)} collective-permute-done((bf16[128,1536]{1,0:T(8,128)(2,1)S(1)}, bf16[128,1536]{1,0:T(8,128)(2,1)S(1)}, u32[]{:S(2)}, u32[]{:S(2)}) %collective-permute-start.8) | collective-permute-done | bytes 393248 | tf_op jit(solution)/shard_map/ppermute | solution.py:201
  63.8 1.3 shard_map.90
  66.4 1.6 collective-permute-done.7.held_ref
  68.0 1.3 shard_map.88
  72.9 2.2 %collective-permute-done.10.held_ref = bf16[128,1536]{1,0:T(8,128)(2,1)} collective-permute-done((bf16[128,1536]{1,0:T(8,128)(2,1)}, bf16[128,1536]{1,0:T(8,128)(2,1)}, u32[]{:S(2)}, u32[]{:S(2)}) %collective-permute-start.10) | collective-permute-done | bytes 393248 | tf_op jit(solution)/shard_map/ppermute | solution.py:201
  76.1 1.3 collective-permute-start.12
  77.4 1.9 %collective-permute-done.9.held_ref = bf16[128,1536]{1,0:T(8,128)(2,1)} collective-permute-done((bf16[128,1536]{1,0:T(8,128)(2,1)}, bf16[128,1536]{1,0:T(8,128)(2,1)}, u32[]{:S(2)}, u32[]{:S(2)}) %collective-permute-start.9) | collective-permute-done | bytes 393248 | tf_op jit(solution)/shard_map/ppermute | solution.py:201
  80.3 1.3 collective-permute-start.11
  81.6 1.6 shard_map.91.before_ref
  83.2 1.6 shard_map.89.before_ref
  86.4 1.3 collective-permute-start.14
  87.7 2.3 %collective-permute-done.11.held_ref = bf16[128,1536]{1,0:T(8,128)(2,1)S(1)} collective-permute-done((bf16[128,1536]{1,0:T(8,128)(2,1)S(1)}, bf16[128,1536]{1,0:T(8,128)(2,1)S(1)}, u32[]{:S(2)}, u32[]{:S(2)}) %collective-permute-start.11) | collective-permute-done | bytes 393248 | tf_op jit(solution)/shard_map/ppermute | solution.py:201
  90.6 1.3 collective-permute-start.13
  94.2 2.2 %collective-permute-done.14.held_ref = bf16[128,1536]{1,0:T(8,128)(2,1)S(1)} collective-permute-done((bf16[128,1536]{1,0:T(8,128)(2,1)S(1)}, bf16[128,1536]{1,0:T(8,128)(2,1)S(1)}, u32[]{:S(2)}, u32[]{:S(2)}) %collective-permute-start.14) | collective-permute-done | bytes 393248 | tf_op jit(solution)/shard_map/ppermute | solution.py:201
  97.0 1.3 collective-permute-start.16
  98.3 2.3 %collective-permute-done.13.held_ref = bf16[128,1536]{1,0:T(8,128)(2,1)S(1)} collective-permute-done((bf16[128,1536]{1,0:T(8,128)(2,1)S(1)}, bf16[128,1536]{1,0:T(8,128)(2,1)S(1)}, u32[]{:S(2)}, u32[]{:S(2)}) %collective-permute-start.13) | collective-permute-done | bytes 393248 | tf_op jit(solution)/shard_map/ppermute | solution.py:201
  101.2 1.3 collective-permute-start.15
  104.8 1.9 %collective-permute-done.16.held_ref = bf16[128,1536]{1,0:T(8,128)(2,1)S(1)} collective-permute-done((bf16[128,1536]{1,0:T(8,128)(2,1)S(1)}, bf16[128,1536]{1,0:T(8,128)(2,1)S(1)}, u32[]{:S(2)}, u32[]{:S(2)}) %collective-permute-start.16) | collective-permute-done | bytes 393248 | tf_op jit(solution)/shard_map/ppermute | solution.py:201
  108.1 2.8 %collective-permute-done.15.held_ref = bf16[128,1536]{1,0:T(8,128)(2,1)S(1)} collective-permute-done((bf16[128,1536]{1,0:T(8,128)(2,1)S(1)}, bf16[128,1536]{1,0:T(8,128)(2,1)S(1)}, u32[]{:S(2)}, u32[]{:S(2)}) %collective-permute-start.15) | collective-permute-done | bytes 393248 | tf_op jit(solution)/shard_map/ppermute | solution.py:201
  114.4 8.4 %all_to_all.25.parts_ref = f32[4,64,128]{2,1,0:T(8,128)S(1)} all-to-all(f32[4,64,128]{2,1,0:T(8,128)S(1)} %broadcast_in_dim.8), channel_id=1, replica_groups=mesh['pipe'=8,'dp'=16,'tensor'=4] {'tensor'}, dimensions={0} | all-to-all | bytes 262144 | tf_op jit(solution)/shard_map/all_to_all | solution.py:277
  122.8 10.7 %all_to_all.26.depth_ref = bf16[8,64,128]{2,1,0:T(8,128)(2,1)S(1)} all-to-all(bf16[8,64,128]{2,1,0:T(8,128)(2,1)S(1)} %shard_map.104), channel_id=1, replica_groups={{0,4,16,20,32,36,48,52},{8,12,24,28,40,44,56,60},{1,5,17,21,33,37,49,53..., dimensions={0} | all-to-all | bytes 262144 | tf_op jit(solution)/shard_map/all_to_all | solution.py:279
  133.5 2.2 %shard_map.105 = bf16[224,256]{1,0:T(8,128)(2,1)S(1)} custom-call(bf16[8,64,128]{2,1,0:T(8,128)(2,1)S(1)} %all_to_all.26.depth_ref, bf16[256,32]{1,0:T(8,128)(2,1)S(1)} %copy-done.10, bf16[8,704,128]{2,1,0:T(8,128)(2,1)} %all-to-all-done.1.gathered_ref), custom_call_target="tpu_custom_call" | custom-call | flops 100663296 | bytes 1048576 | tf_op jit(solution)/shard_map/pallas_call | solution.py:280
  137.7 1.4 collective-permute-start.20
  139.1 9.1 %collective-permute-start.19 = (bf16[224,256]{1,0:T(8,128)(2,1)S(1)}, bf16[224,256]{1,0:T(8,128)(2,1)S(1)}, u32[]{:S(2)}, u32[]{:S(2)}) collective-permute-start(bf16[224,256]{1,0:T(8,128)(2,1)S(1)} %shard_map.105), channel_id=1, source_target_pairs={{0,8},{4,12},{8,0},{12,4},{16,24},{20,28},{24,16},{28,20},{32,40},... | collective-permute-start | bytes 344072 | tf_op jit(solution)/shard_map/ppermute | solution.py:288
  148.2 8.5 %collective-permute-done.19 = bf16[224,256]{1,0:T(8,128)(2,1)S(1)} collective-permute-done((bf16[224,256]{1,0:T(8,128)(2,1)S(1)}, bf16[224,256]{1,0:T(8,128)(2,1)S(1)}, u32[]{:S(2)}, u32[]{:S(2)}) %collective-permute-start.19) | collective-permute-done | bytes 114720 | tf_op jit(solution)/shard_map/ppermute | solution.py:288
  158.5 6.7 %all-to-all-start.4 = ((bf16[8,192,256]{2,1,0:T(8,128)(2,1)}), bf16[8,192,256]{2,1,0:T(8,128)(2,1)}, u32[]{:S(2)}, u32[]{:S(2)}) async-start(bf16[8,192,256]{2,1,0:T(8,128)(2,1)} %broadcast_in_dim.10), calls=%async_computation.4 | async-start | bytes 1572864 | tf_op jit(solution)/shard_map/all_to_all | solution.py:296
  170.7 1.4 fusion.1
  172.1 1.7 collective-permute-done.22.given_ref
  173.8 1.8 shard_map.111
  175.6 2.8 %all-to-all-done.4 = bf16[8,192,256]{2,1,0:T(8,128)(2,1)} async-done(((bf16[8,192,256]{2,1,0:T(8,128)(2,1)}), bf16[8,192,256]{2,1,0:T(8,128)(2,1)}, u32[]{:S(2)}, u32[]{:S(2)}) %all-to-all-start.4) | async-done | bytes 786464 | tf_op jit(solution)/shard_map/all_to_all | solution.py:296
  178.4 2.4 %convert_multiply_fusion = f32[8,192,256]{2,1,0:T(8,128)} fusion(bf16[8,192,256]{2,1,0:T(8,128)(2,1)} %all-to-all-done.4), kind=kLoop, calls=%fused_computation.2 | loop fusion | flops 786432 | bytes 2359296 | tf_op jit(solution)/shard_map/div | solution.py:297
  (108 shorter events, 47.3 us)
Async XLA Ops:
  0.6 31.8 %copy-start = (bf16[4,1,128,1536]{3,2,1,0:T(8,128)(2,1)S(1)}, bf16[4,1,128,1536]{3,2,1,0:T(8,128)(2,1)}, u32[]{:S(2)}) copy-start(bf16[4,1,128,1536]{3,2,1,0:T(8,128)(2,1)} %param.6) | copy-start | bytes 4718596
  0.6 4.1 %collective-permute-start.2 = (bf16[128,1536]{1,0:T(8,128)(2,1)}, bf16[128,1536]{1,0:T(8,128)(2,1)}, u32[]{:S(2)}, u32[]{:S(2)}) collective-permute-start(bf16[128,1536]{1,0:T(8,128)(2,1)} %bitcast.36), channel_id=1, source_target_pairs={{0,4},{4,0},{8,12},{12,8},{16,20},{20,16},{24,28},{28,24},{32,36},... | collective-permute-start | bytes 1179656 | tf_op jit(solution)/shard_map/ppermute | solution.py:195
  4.7 31.4 %collective-permute-start.4 = (bf16[4,128,1536]{2,1,0:T(8,128)(2,1)}, bf16[4,128,1536]{2,1,0:T(8,128)(2,1)S(1)}, u32[]{:S(2)}, u32[]{:S(2)}) collective-permute-start(bf16[4,128,1536]{2,1,0:T(8,128)(2,1)} %bitcast.19), channel_id=1, source_target_pairs={{0,4},{4,0},{8,12},{12,8},{16,20},{20,16},{24,28},{28,24},{32,36},... | collective-permute-start | bytes 4718600 | tf_op jit(solution)/shard_map/ppermute | solution.py:195
  6.8 27.7 %collective-permute-start.1 = (bf16[128,1536]{1,0:T(8,128)(2,1)}, bf16[128,1536]{1,0:T(8,128)(2,1)}, u32[]{:S(2)}, u32[]{:S(2)}) collective-permute-start(bf16[128,1536]{1,0:T(8,128)(2,1)} %bitcast.37), channel_id=1, source_target_pairs={{0,64},{8,72},{16,80},{24,88},{32,96},{40,104},{48,112},{56,120},{... | collective-permute-start | bytes 1179656 | tf_op jit(solution)/shard_map/ppermute | solution.py:201
  8.1 29.7 %collective-permute-start.3 = (bf16[128,1536]{1,0:T(8,128)(2,1)}, bf16[128,1536]{1,0:T(8,128)(2,1)}, u32[]{:S(2)}, u32[]{:S(2)}) collective-permute-start(bf16[128,1536]{1,0:T(8,128)(2,1)} %collective-permute-done.2.held_ref), channel_id=1, source_target_pairs={{0,64},{8,72},{16,80},{24,88},{32,96},{40,104},{48,112},{56,120},{... | collective-permute-start | bytes 1179656 | tf_op jit(solution)/shard_map/ppermute | solution.py:201
  9.4 1.0 copy-start.1
  10.4 1.1 copy-start.4
  12.2 6.3 %copy-start.20 = (bf16[1,256,32]{1,2,0:T(8,128)(2,1)S(1)}, bf16[1,256,32]{1,2,0:T(8,128)(2,1)}, u32[]{:S(2)}) copy-start(bf16[1,256,32]{1,2,0:T(8,128)(2,1)} %param.9) | copy-start | bytes 49156
  14.0 13.3 %all-to-all-start = ((bf16[4,128,384]{2,1,0:T(8,128)(2,1)}), bf16[4,128,384]{2,1,0:T(8,128)(2,1)S(1)}, u32[]{:S(2)}, u32[]{:S(2)}) async-start(bf16[4,128,384]{2,1,0:T(8,128)(2,1)} %copy-done.11), calls=%async_computation | async-start | bytes 786432 | tf_op jit(solution)/shard_map/all_to_all | solution.py:217
  28.1 1.0 copy-start.7
  29.1 0.8 copy-start.9
  29.9 1.0 copy-start.13
  31.3 1.1 copy-start.8
  32.4 1.0 copy-start.2
  33.4 2.7 %copy-start.16 = (f32[128,256]{1,0:T(8,128)}, f32[128,256]{1,0:T(8,128)S(1)}, u32[]{:S(2)}) copy-start(f32[128,256]{1,0:T(8,128)S(1)} %get-tuple-element.99.slope_ref) | copy-start | bytes 393220
  33.4 2.7 %copy-start.18 = (f32[128,256]{1,0:T(8,128)}, f32[128,256]{1,0:T(8,128)S(1)}, u32[]{:S(2)}) copy-start(f32[128,256]{1,0:T(8,128)S(1)} %get-tuple-element.100.preact_ref) | copy-start | bytes 393220
  33.4 2.7 %copy-start.22 = (f32[128,128]{1,0:T(8,128)}, f32[128,128]{1,0:T(8,128)S(1)}, u32[]{:S(2)}) copy-start(f32[128,128]{1,0:T(8,128)S(1)} %get-tuple-element.101.factor_ref) | copy-start | bytes 196612
  39.3 33.6 %all-to-all-start.1 = ((bf16[8,704,128]{2,1,0:T(8,128)(2,1)}), bf16[8,704,128]{2,1,0:T(8,128)(2,1)}, u32[]{:S(2)}, u32[]{:S(2)}) async-start(bf16[8,704,128]{2,1,0:T(8,128)(2,1)} %copy-done.8), calls=%async_computation.1 | async-start | bytes 2883584 | tf_op jit(solution)/shard_map/all_to_all | solution.py:271
  43.7 9.9 %collective-permute-start.6 = (bf16[128,1536]{1,0:T(8,128)(2,1)}, bf16[128,1536]{1,0:T(8,128)(2,1)S(1)}, u32[]{:S(2)}, u32[]{:S(2)}) collective-permute-start(bf16[128,1536]{1,0:T(8,128)(2,1)} %collective-permute-done.3.held_ref), channel_id=1, source_target_pairs={{64,128},{72,136},{80,144},{88,152},{96,160},{104,168},{112,176},{... | collective-permute-start | bytes 1179656 | tf_op jit(solution)/shard_map/ppermute | solution.py:201
  44.9 12.8 %collective-permute-start.5 = (bf16[128,1536]{1,0:T(8,128)(2,1)}, bf16[128,1536]{1,0:T(8,128)(2,1)S(1)}, u32[]{:S(2)}, u32[]{:S(2)}) collective-permute-start(bf16[128,1536]{1,0:T(8,128)(2,1)} %collective-permute-done.1.held_ref), channel_id=1, source_target_pairs={{64,128},{72,136},{80,144},{88,152},{96,160},{104,168},{112,176},{... | collective-permute-start | bytes 1179656 | tf_op jit(solution)/shard_map/ppermute | solution.py:201
  46.2 3.1 %collective-permute-start = (f32[128,32]{1,0:T(8,128)S(1)}, f32[128,32]{1,0:T(8,128)S(1)}, u32[]{:S(2)}, u32[]{:S(2)}) collective-permute-start(f32[128,32]{1,0:T(8,128)S(1)} %get-tuple-element.96.mixing_ref), channel_id=1, source_target_pairs={{0,4},{4,0},{8,12},{12,8},{16,20},{20,16},{24,28},{28,24},{32,36},... | collective-permute-start | bytes 49160 | tf_op jit(solution)/shard_map/ppermute | solution.py:195
  54.1 9.7 %collective-permute-start.8 = (bf16[128,1536]{1,0:T(8,128)(2,1)S(1)}, bf16[128,1536]{1,0:T(8,128)(2,1)S(1)}, u32[]{:S(2)}, u32[]{:S(2)}) collective-permute-start(bf16[128,1536]{1,0:T(8,128)(2,1)S(1)} %shard_map.86), channel_id=1, source_target_pairs={{128,192},{136,200},{144,208},{152,216},{160,224},{168,232},{176,2... | collective-permute-start | bytes 1179656 | tf_op jit(solution)/shard_map/ppermute | solution.py:201
  58.3 9.7 %collective-permute-start.7 = (bf16[128,1536]{1,0:T(8,128)(2,1)S(1)}, bf16[128,1536]{1,0:T(8,128)(2,1)S(1)}, u32[]{:S(2)}, u32[]{:S(2)}) collective-permute-start(bf16[128,1536]{1,0:T(8,128)(2,1)S(1)} %shard_map.84), channel_id=1, source_target_pairs={{128,192},{136,200},{144,208},{152,216},{160,224},{168,232},{176,2... | collective-permute-start | bytes 1179656 | tf_op jit(solution)/shard_map/ppermute | solution.py:201
  65.1 10.0 %collective-permute-start.10 = (bf16[128,1536]{1,0:T(8,128)(2,1)}, bf16[128,1536]{1,0:T(8,128)(2,1)}, u32[]{:S(2)}, u32[]{:S(2)}) collective-permute-start(bf16[128,1536]{1,0:T(8,128)(2,1)} %shard_map.90), channel_id=1, source_target_pairs={{192,256},{200,264},{208,272},{216,280},{224,288},{232,296},{240,3... | collective-permute-start | bytes 1179656 | tf_op jit(solution)/shard_map/ppermute | solution.py:201
  69.3 10.0 %collective-permute-start.9 = (bf16[128,1536]{1,0:T(8,128)(2,1)}, bf16[128,1536]{1,0:T(8,128)(2,1)}, u32[]{:S(2)}, u32[]{:S(2)}) collective-permute-start(bf16[128,1536]{1,0:T(8,128)(2,1)} %shard_map.88), channel_id=1, source_target_pairs={{192,256},{200,264},{208,272},{216,280},{224,288},{232,296},{240,3... | collective-permute-start | bytes 1179656 | tf_op jit(solution)/shard_map/ppermute | solution.py:201
  76.1 9.7 %collective-permute-start.12 = (bf16[128,1536]{1,0:T(8,128)(2,1)S(1)}, bf16[128,1536]{1,0:T(8,128)(2,1)S(1)}, u32[]{:S(2)}, u32[]{:S(2)}) collective-permute-start(bf16[128,1536]{1,0:T(8,128)(2,1)S(1)} %shard_map.94), channel_id=1, source_target_pairs={{256,320},{264,328},{272,336},{280,344},{288,352},{296,360},{304,3... | collective-permute-start | bytes 1179656 | tf_op jit(solution)/shard_map/ppermute | solution.py:201
  80.3 9.7 %collective-permute-start.11 = (bf16[128,1536]{1,0:T(8,128)(2,1)S(1)}, bf16[128,1536]{1,0:T(8,128)(2,1)S(1)}, u32[]{:S(2)}, u32[]{:S(2)}) collective-permute-start(bf16[128,1536]{1,0:T(8,128)(2,1)S(1)} %shard_map.92), channel_id=1, source_target_pairs={{256,320},{264,328},{272,336},{280,344},{288,352},{296,360},{304,3... | collective-permute-start | bytes 1179656 | tf_op jit(solution)/shard_map/ppermute | solution.py:201
  86.4 10.0 %collective-permute-start.14 = (bf16[128,1536]{1,0:T(8,128)(2,1)S(1)}, bf16[128,1536]{1,0:T(8,128)(2,1)S(1)}, u32[]{:S(2)}, u32[]{:S(2)}) collective-permute-start(bf16[128,1536]{1,0:T(8,128)(2,1)S(1)} %shard_map.98), channel_id=1, source_target_pairs={{320,384},{328,392},{336,400},{344,408},{352,416},{360,424},{368,4... | collective-permute-start | bytes 1179656 | tf_op jit(solution)/shard_map/ppermute | solution.py:201
  90.6 10.0 %collective-permute-start.13 = (bf16[128,1536]{1,0:T(8,128)(2,1)S(1)}, bf16[128,1536]{1,0:T(8,128)(2,1)S(1)}, u32[]{:S(2)}, u32[]{:S(2)}) collective-permute-start(bf16[128,1536]{1,0:T(8,128)(2,1)S(1)} %shard_map.96), channel_id=1, source_target_pairs={{320,384},{328,392},{336,400},{344,408},{352,416},{360,424},{368,4... | collective-permute-start | bytes 1179656 | tf_op jit(solution)/shard_map/ppermute | solution.py:201
  97.0 9.7 %collective-permute-start.16 = (bf16[128,1536]{1,0:T(8,128)(2,1)S(1)}, bf16[128,1536]{1,0:T(8,128)(2,1)S(1)}, u32[]{:S(2)}, u32[]{:S(2)}) collective-permute-start(bf16[128,1536]{1,0:T(8,128)(2,1)S(1)} %shard_map.102), channel_id=1, source_target_pairs={{384,448},{392,456},{400,464},{408,472},{416,480},{424,488},{432,4... | collective-permute-start | bytes 1179656 | tf_op jit(solution)/shard_map/ppermute | solution.py:201
  101.2 9.7 %collective-permute-start.15 = (bf16[128,1536]{1,0:T(8,128)(2,1)S(1)}, bf16[128,1536]{1,0:T(8,128)(2,1)S(1)}, u32[]{:S(2)}, u32[]{:S(2)}) collective-permute-start(bf16[128,1536]{1,0:T(8,128)(2,1)S(1)} %shard_map.100), channel_id=1, source_target_pairs={{384,448},{392,456},{400,464},{408,472},{416,480},{424,488},{432,4... | collective-permute-start | bytes 1179656 | tf_op jit(solution)/shard_map/ppermute | solution.py:201
  107.4 28.4 %collective-permute-start.18 = (bf16[128,1536]{1,0:T(8,128)(2,1)S(1)}, bf16[128,1536]{1,0:T(8,128)(2,1)S(1)}, u32[]{:S(2)}, u32[]{:S(2)}) collective-permute-start(bf16[128,1536]{1,0:T(8,128)(2,1)S(1)} %shard_map.107), channel_id=1, source_target_pairs={{132,68},{140,76},{148,84},{156,92},{164,100},{172,108},{180,116},... | collective-permute-start | bytes 1179656 | tf_op jit(solution)/shard_map/ppermute | solution.py:201
  111.4 24.4 %collective-permute-start.17 = (bf16[128,1536]{1,0:T(8,128)(2,1)S(1)}, bf16[128,1536]{1,0:T(8,128)(2,1)S(1)}, u32[]{:S(2)}, u32[]{:S(2)}) collective-permute-start(bf16[128,1536]{1,0:T(8,128)(2,1)S(1)} %shard_map.106), channel_id=1, source_target_pairs={{132,68},{140,76},{148,84},{156,92},{164,100},{172,108},{180,116},... | collective-permute-start | bytes 1179656 | tf_op jit(solution)/shard_map/ppermute | solution.py:201
  113.3 20.3 %copy-start.10 = (bf16[256,32]{1,0:T(8,128)(2,1)S(1)}, bf16[256,32]{1,0:T(8,128)(2,1)}, u32[]{:S(2)}) copy-start(bf16[256,32]{1,0:T(8,128)(2,1)} %copy.10.weight_ref) | copy-start | bytes 49156
  136.4 20.4 %collective-permute-start.21 = (bf16[128,1536]{1,0:T(8,128)(2,1)S(1)}, bf16[128,1536]{1,0:T(8,128)(2,1)S(1)}, u32[]{:S(2)}, u32[]{:S(2)}) collective-permute-start(bf16[128,1536]{1,0:T(8,128)(2,1)S(1)} %shard_map.109), channel_id=1, source_target_pairs={{68,4},{76,12},{84,20},{92,28},{100,36},{108,44},{116,52},{124,60}... | collective-permute-start | bytes 1179656 | tf_op jit(solution)/shard_map/ppermute | solution.py:201
  137.7 27.5 %copy-start.25 = (bf16[1,1536]{1,0:T(2,128)(2,1)S(1)}, bf16[1,1536]{1,0:T(2,128)(2,1)}, u32[]{:S(2)}) copy-start(bf16[1,1536]{1,0:T(2,128)(2,1)} %gain_ref.1) | copy-start | bytes 9220
  137.7 27.5 %copy-start.21 = (bf16[1,256,32]{1,2,0:T(8,128)(2,1)S(1)}, bf16[1,256,32]{1,2,0:T(8,128)(2,1)}, u32[]{:S(2)}) copy-start(bf16[1,256,32]{1,2,0:T(8,128)(2,1)} %param.9) | copy-start | bytes 49156
  137.7 19.1 %collective-permute-start.20 = (bf16[128,1536]{1,0:T(8,128)(2,1)S(1)}, bf16[128,1536]{1,0:T(8,128)(2,1)}, u32[]{:S(2)}, u32[]{:S(2)}) collective-permute-start(bf16[128,1536]{1,0:T(8,128)(2,1)S(1)} %shard_map.108), channel_id=1, source_target_pairs={{68,4},{76,12},{84,20},{92,28},{100,36},{108,44},{116,52},{124,60}... | collective-permute-start | bytes 1179656 | tf_op jit(solution)/shard_map/ppermute | solution.py:201
  139.1 17.6 %collective-permute-start.19 = (bf16[224,256]{1,0:T(8,128)(2,1)S(1)}, bf16[224,256]{1,0:T(8,128)(2,1)S(1)}, u32[]{:S(2)}, u32[]{:S(2)}) collective-permute-start(bf16[224,256]{1,0:T(8,128)(2,1)S(1)} %shard_map.105), channel_id=1, source_target_pairs={{0,8},{4,12},{8,0},{12,4},{16,24},{20,28},{24,16},{28,20},{32,40},... | collective-permute-start | bytes 344072 | tf_op jit(solution)/shard_map/ppermute | solution.py:288
  157.5 1.0 copy-start.26
  157.5 12.8 %copy-start.3 = (bf16[1,128,1536]{2,1,0:T(8,128)(2,1)S(1)}, bf16[1,128,1536]{2,1,0:T(8,128)(2,1)}, u32[]{:S(2)}) copy-start(bf16[1,128,1536]{2,1,0:T(8,128)(2,1)} %param.5) | copy-start | bytes 1179652
  157.5 12.8 %copy-start.5 = (bf16[1,1536,256]{2,1,0:T(8,128)(2,1)S(1)}, bf16[1,1536,256]{2,1,0:T(8,128)(2,1)}, u32[]{:S(2)}) copy-start(bf16[1,1536,256]{2,1,0:T(8,128)(2,1)} %param.8) | copy-start | bytes 2359300
  158.5 20.0 %all-to-all-start.4 = ((bf16[8,192,256]{2,1,0:T(8,128)(2,1)}), bf16[8,192,256]{2,1,0:T(8,128)(2,1)}, u32[]{:S(2)}, u32[]{:S(2)}) async-start(bf16[8,192,256]{2,1,0:T(8,128)(2,1)} %broadcast_in_dim.10), calls=%async_computation.4 | async-start | bytes 1572864 | tf_op jit(solution)/shard_map/all_to_all | solution.py:296
  165.2 8.6 %copy-start.15 = (bf16[128,1536]{1,0:T(8,128)(2,1)S(1)}, bf16[128,1536]{1,0:T(8,128)(2,1)}, u32[]{:S(2)}) copy-start(bf16[128,1536]{1,0:T(8,128)(2,1)} %copy-done.14) | copy-start | bytes 1179652
  165.2 0.9 copy-start.17
  166.2 0.9 copy-start.19
  167.1 0.8 copy-start.23
  169.0 4.8 %collective-permute-start.22 = (bf16[128,1536]{1,0:T(8,128)(2,1)}, bf16[128,1536]{1,0:T(8,128)(2,1)S(1)}, u32[]{:S(2)}, u32[]{:S(2)}) collective-permute-start(bf16[128,1536]{1,0:T(8,128)(2,1)} %collective-permute-done.20), channel_id=1, source_target_pairs={{4,0},{12,8},{20,16},{28,24},{36,32},{44,40},{52,48},{60,56},{5,1}... | collective-permute-start | bytes 1179656 | tf_op jit(solution)/shard_map/ppermute | solution.py:310
  (5 other events, 3.7 us)

commit v3 on v2

--- a/solution.py
+++ b/solution.py
@@ -24,7 +24,7 @@
         + [pl.BlockSpec(memory_space=pltpu.VMEM)] * (count - smem),
         out_specs=[pl.BlockSpec(memory_space=pltpu.VMEM)] * len(shapes),
         scratch_shapes=list(scratch),
-        compiler_params=pltpu.CompilerParams(vmem_limit_bytes=20 * 1024 * 1024),
+        compiler_params=pltpu.CompilerParams(vmem_limit_bytes=6 * 1024 * 1024),
         cost_estimate=pl.CostEstimate(flops=flops, bytes_accessed=moved, transcendentals=0),
     )
 
@@ -56,14 +56,14 @@
     return total
 
 
-def put_products(held_ref, incoming_ref, products_ref, layer, layers):
+def put_products(held_ref, incoming_ref, products_ref, start, layers):
     tokens = held_ref.shape[0]
     same = lax.broadcasted_iota(jnp.int32, (tokens, tokens), 0) == lax.broadcasted_iota(jnp.int32, (tokens, tokens), 1)
     for s in range(4):
         every = lax.dot_general(
             incoming_ref[s], held_ref[...], (((1,), (1,)), ((), ())), preferred_element_type=f32
         )
-        products_ref[pl.ds(s * layers + layer, 1), :] = jnp.sum(jnp.where(same, every, 0.0), axis=0, keepdims=True)
+        products_ref[pl.ds(start + s * layers, 1), :] = jnp.sum(jnp.where(same, every, 0.0), axis=0, keepdims=True)
 
 
 def generate_kernel(
@@ -94,20 +94,23 @@
     mixing_ref[...] = jnp.dot(active, weight_ref[...], preferred_element_type=f32)
 
 
-def own_kernel(layers, place_ref, held_ref, incoming_ref, products_ref):
+def own_kernel(layers, place_ref, even_ref, odd_ref, even_in_ref, odd_in_ref, products_ref):
     products_ref[...] = jnp.zeros_like(products_ref)
 
     @pl.when(place_ref[1] == 0)
     def _():
-        put_products(held_ref, incoming_ref, products_ref, place_ref[0], layers)
-
-
-def depth_kernel(turn, layers, place_ref, held_ref, incoming_ref, before_ref, products_ref):
+        put_products(even_ref, even_in_ref, products_ref, place_ref[0], layers)
+        put_products(odd_ref, odd_in_ref, products_ref, 4 * layers + place_ref[0], layers)
+
+
+def depth_kernel(turn, layers, place_ref, even_ref, odd_ref, even_in_ref, odd_in_ref, before_ref, products_ref):
     products_ref[...] = before_ref[...]
 
     @pl.when(place_ref[1] == 0)
     def _():
-        put_products(held_ref, incoming_ref, products_ref, (place_ref[0] - (turn - 1)) & (layers - 1), layers)
+        layer = (place_ref[0] - (turn - 1)) & (layers - 1)
+        put_products(even_ref, even_in_ref, products_ref, layer, layers)
+        put_products(odd_ref, odd_in_ref, products_ref, 4 * layers + layer, layers)
 
 
 def tiles(shape):
@@ -200,12 +203,8 @@
             pairs += [(k * size + i, (k - 1) * size + i) for k in range(layers + LAG - turn, layers) for i in range(1, size, 2)]
         return lax.ppermute(array, ("pipe", "dp"), pairs)
 
-    swapped, incoming = lax.optimization_barrier((swap(current), incoming))
-    halves = [current, swapped]
+    halves = [current, swap(current)]
     chains = [hop(halves[h], 1) for h in range(2)]
-    across = swap(incoming)
-    rising = [incoming, across]
-    falling = [across, incoming]
 
     packed, scaled_turned = call(
         project_kernel,
@@ -215,6 +214,12 @@
         count=3,
     )(current, gains, first_weight[0])
     packed = lax.all_to_all(packed, "tensor", 0, 0, tiled=True)
+    scaled_turned, incoming, *chains = lax.optimization_barrier((scaled_turned, incoming, *chains))
+    across = swap(incoming)
+    rising = [incoming, across]
+    falling = [across, incoming]
+    early = [hop(chains[h], LAG) for h in range(2)]
+    packed, *early = lax.optimization_barrier((packed, *early))
     mixing, slope, preact, factor, payload = call(
         generate_kernel,
         [
@@ -229,21 +234,16 @@
         count=3,
     )(packed, second_weight[0], scaled_turned)
     mixings = [swap(mixing), mixing]
-    products = [
-        call(
-            functools.partial(own_kernel, layers),
-            [shape((columns, tokens), f32)],
-            8 * tokens * width,
-            10 * tokens * width,
-            smem=1,
-            count=3,
-        )(place, halves[h], rising[h])[0]
-        for h in range(2)
-    ]
+    [products] = call(
+        functools.partial(own_kernel, layers),
+        [shape((2 * columns, tokens), f32)],
+        16 * tokens * width,
+        20 * tokens * width,
+        smem=1,
+        count=5,
+    )(place, *halves, *rising)
 
     def advance(turn, h):
-        if turn <= LAG:
-            return hop(chains[h], turn)
         [sent] = call(
             functools.partial(hop_kernel, turn, layers),
             [shape((tokens, width), bf16)],
@@ -255,26 +255,24 @@
         return hop(sent, turn)
 
     for turn in range(2, layers + 1):
-        for h in range(2):
-            held = chains[h]
-            chains[h] = advance(turn, h)
-            [products[h]] = call(
-                functools.partial(depth_kernel, turn, layers),
-                [shape((columns, tokens), f32)],
-                8 * tokens * width,
-                10 * tokens * width,
-                smem=1,
-                count=4,
-            )(place, held, rising[h], products[h])
+        held = chains
+        chains = early if turn == LAG else [advance(turn, h) for h in range(2)]
+        [products] = call(
+            functools.partial(depth_kernel, turn, layers),
+            [shape((2 * columns, tokens), f32)],
+            16 * tokens * width,
+            20 * tokens * width,
+            smem=1,
+            count=6,
+        )(place, *held, *rising, products)
         if turn == LAG:
-            payload, *products = lax.optimization_barrier((payload, *products))
+            payload, products = lax.optimization_barrier((payload, products))
             gathered = lax.all_to_all(payload, "dp", 0, 0, axis_index_groups=groups, tiled=True)
         if turn == 2 * LAG:
-            gathered, *products = lax.optimization_barrier((gathered, *products))
-        *mixings, products[0], products[1] = lax.optimization_barrier((*mixings, *products))
-
-    both = jnp.concatenate(products, axis=0)
-    spread = lax.all_to_all(jnp.broadcast_to(both[None], (4, *both.shape)), "tensor", 0, 0, tiled=True)
+            gathered, products = lax.optimization_barrier((gathered, products))
+        *mixings, products = lax.optimization_barrier((*mixings, products))
+
+    spread = lax.all_to_all(jnp.broadcast_to(products[None], (4, *products.shape)), "tensor", 0, 0, tiled=True)
     [depth_grads] = call(depth_grad_kernel, [shape((members, 2 * columns, tokens), bf16)], 0, 8 * columns * tokens, count=1)(spread)
     depth_all = lax.all_to_all(depth_grads, "dp", 0, 0, axis_index_groups=groups, tiled=True)
     [mine] = call(
@@ -286,14 +284,18 @@
     )(depth_all, second_weight[0], gathered)
     mine, *chains = lax.optimization_barrier((mine, *chains))
     other = lax.ppermute(mine, "dp", [(i, i ^ 2) for i in range(size)])
-    for turn in range(layers + 1, layers + LAG):
-        chains = [advance(turn, h) for h in range(2)]
-    other, *chains = lax.optimization_barrier((other, *chains))
     total = mine.astype(f32) + other.astype(f32)
     divisor = tokens * size
     second_grads = total[chunk:].T / divisor
-    spread = jnp.broadcast_to(total[None, :chunk].astype(bf16), (members, chunk, hidden))
-    summed = lax.all_to_all(spread, "dp", 0, 0, axis_index_groups=groups, tiled=True)
+    spread = jnp.broadcast_to(total[None, :chunk].astype(bf16), (size // 4, chunk, hidden))
+    along = [[x * 4 + rest for x in range(size // 4)] for rest in range(4)]
+    for turn in range(layers + 1, layers + LAG):
+        chains = [advance(turn, h) for h in range(2)]
+    own = lax.all_to_all(spread, "dp", 0, 0, axis_index_groups=along, tiled=True)
+    own, *chains = lax.optimization_barrier((own, *chains))
+    far = swap(own)
+    near = (index & 1) == 0
+    summed = jnp.stack([jnp.where(near, own, far), jnp.where(near, far, own)], axis=1)
     first_grads = summed.astype(f32).reshape(width, hidden) / divisor
 
     scaled_grad, back = call(

time: 183 us -> 182 us (level)
  the two profiles are of different devices: /device:TPU:224 before, /device:TPU:225 now
where the time goes in v3:
time: 182 us; the launch traced here: 180 us
  starting transfers between devices  92.2 us (51%)
  Pallas kernels  31.1 us (17%)
  waiting for transfers between devices  19.3 us (11%)
  blocking collectives  18.6 us (10%)
  local copies, waits for them, and re-layouts  12.7 us (7%)
  other arithmetic  4.53 us (2%)
    ppermute x18, starting transfers between devices, hop(): return lax.ppermute(array, ('pipe', 'dp'), pairs)  49.2 us
    pallas_call x14, Pallas kernels, advance(): call(functools.partial(hop_kernel, turn, layers), [shape((tokens, width),...  18.8 us
    ppermute x4, starting transfers between devices, swap(): return lax.ppermute(array, 'dp', [(i, i ^ 1) for i in range(size)])  17.7 us
    all_to_all x1, blocking collectives, on_device(): lax.all_to_all(depth_grads, 'dp', 0, 0, axis_index_groups=groups, tiled=T...  11.4 us
    unnamed x48, local copies, waits for them, and re-layouts  10.1 us
    ppermute x1, starting transfers between devices, on_device(): other = lax.ppermute(mine, 'dp', [(i, i ^ 2) for i in range(size)])  7.93 us
    all_to_all x1, waiting for transfers between devices, on_device(): packed = lax.all_to_all(packed, 'tensor', 0, 0, tiled=True)  7.38 us
    all_to_all x1, blocking collectives, on_device(): lax.all_to_all(jnp.broadcast_to(products[None], (4, *products.shape)), 't...  7.21 us
  transfers between devices with their start and end apart: 27, of which 6 were waited for; matrix products, arithmetic and copies ran while one was open for 4% of the time, Pallas kernels for 15%

profile of v3, /device:TPU:225, one launch (start us, length us, event | category | flops | bytes accessed | tf_op | source)
XLA Modules:
  0.0 180.0 jit_solution(11996955091469434522)
XLA Ops:
  0.6 2.7 %collective-permute-start.1 = (bf16[128,1536]{1,0:T(8,128)(2,1)}, bf16[128,1536]{1,0:T(8,128)(2,1)S(1)}, u32[]{:S(2)}, u32[]{:S(2)}) collective-permute-start(bf16[128,1536]{1,0:T(8,128)(2,1)} %bitcast.42), channel_id=1, source_target_pairs={{0,4},{4,0},{8,12},{12,8},{16,20},{20,16},{24,28},{28,24},{32,36},... | collective-permute-start | bytes 1179656 | tf_op jit(solution)/shard_map/ppermute | solution.py:198
  3.4 1.4 collective-permute-start
  4.9 1.4 collective-permute-start.2
  10.3 9.2 %collective-permute-start.6 = (bf16[4,128,1536]{2,1,0:T(8,128)(2,1)}, bf16[4,128,1536]{2,1,0:T(8,128)(2,1)S(1)}, u32[]{:S(2)}, u32[]{:S(2)}) collective-permute-start(bf16[4,128,1536]{2,1,0:T(8,128)(2,1)} %bitcast.25), channel_id=1, source_target_pairs={{0,4},{4,0},{8,12},{12,8},{16,20},{20,16},{24,28},{28,24},{32,36},... | collective-permute-start | bytes 4718600 | tf_op jit(solution)/shard_map/ppermute | solution.py:198
  19.5 1.4 collective-permute-start.3
  20.9 1.4 collective-permute-start.4
  22.3 4.2 %all-to-all-start = ((bf16[4,128,384]{2,1,0:T(8,128)(2,1)}), bf16[4,128,384]{2,1,0:T(8,128)(2,1)S(1)}, u32[]{:S(2)}, u32[]{:S(2)}) async-start(bf16[4,128,384]{2,1,0:T(8,128)(2,1)} %copy-done.13), calls=%async_computation | async-start | bytes 786432 | tf_op jit(solution)/shard_map/all_to_all | solution.py:216
  27.3 7.4 %all-to-all-done.parts_ref = bf16[4,128,384]{2,1,0:T(8,128)(2,1)S(1)} async-done(((bf16[4,128,384]{2,1,0:T(8,128)(2,1)}), bf16[4,128,384]{2,1,0:T(8,128)(2,1)S(1)}, u32[]{:S(2)}, u32[]{:S(2)}) %all-to-all-start) | async-done | bytes 393248 | tf_op jit(solution)/shard_map/all_to_all | solution.py:216
  39.3 1.3 copy-done.2
  42.2 1.1 shard_map.79.before_ref
  43.3 7.1 %all-to-all-start.1 = ((bf16[8,704,128]{2,1,0:T(8,128)(2,1)}), bf16[8,704,128]{2,1,0:T(8,128)(2,1)}, u32[]{:S(2)}, u32[]{:S(2)}) async-start(bf16[8,704,128]{2,1,0:T(8,128)(2,1)} %copy-done.8), calls=%async_computation.1 | async-start | bytes 2883584 | tf_op jit(solution)/shard_map/all_to_all | solution.py:270
  50.5 1.9 %collective-permute-start.5 = (f32[128,32]{1,0:T(8,128)S(1)}, f32[128,32]{1,0:T(8,128)S(1)}, u32[]{:S(2)}, u32[]{:S(2)}) collective-permute-start(f32[128,32]{1,0:T(8,128)S(1)} %get-tuple-element.88.mixing_ref), channel_id=1, source_target_pairs={{0,4},{4,0},{8,12},{12,8},{16,20},{20,16},{24,28},{28,24},{32,36},... | collective-permute-start | bytes 49160 | tf_op jit(solution)/shard_map/ppermute | solution.py:198
  52.4 1.2 collective-permute-done.5.mixing_ref
  53.6 1.4 shard_map.82
  55.0 3.3 %collective-permute-start.8 = (bf16[128,1536]{1,0:T(8,128)(2,1)S(1)}, bf16[128,1536]{1,0:T(8,128)(2,1)S(1)}, u32[]{:S(2)}, u32[]{:S(2)}) collective-permute-start(bf16[128,1536]{1,0:T(8,128)(2,1)S(1)} %shard_map.82), channel_id=1, source_target_pairs={{128,192},{136,200},{144,208},{152,216},{160,224},{168,232},{176,2... | collective-permute-start | bytes 1179656 | tf_op jit(solution)/shard_map/ppermute | solution.py:204
  58.4 1.4 shard_map.81
  59.8 1.3 collective-permute-start.7
  63.1 1.8 shard_map.85
  64.8 5.0 %collective-permute-start.10 = (bf16[128,1536]{1,0:T(8,128)(2,1)}, bf16[128,1536]{1,0:T(8,128)(2,1)}, u32[]{:S(2)}, u32[]{:S(2)}) collective-permute-start(bf16[128,1536]{1,0:T(8,128)(2,1)} %shard_map.85), channel_id=1, source_target_pairs={{192,256},{200,264},{208,272},{216,280},{224,288},{232,296},{240,3... | collective-permute-start | bytes 1179656 | tf_op jit(solution)/shard_map/ppermute | solution.py:204
  69.8 1.7 shard_map.84
  71.5 2.4 %collective-permute-start.9 = (bf16[128,1536]{1,0:T(8,128)(2,1)}, bf16[128,1536]{1,0:T(8,128)(2,1)}, u32[]{:S(2)}, u32[]{:S(2)}) collective-permute-start(bf16[128,1536]{1,0:T(8,128)(2,1)} %shard_map.84), channel_id=1, source_target_pairs={{192,256},{200,264},{208,272},{216,280},{224,288},{232,296},{240,3... | collective-permute-start | bytes 1179656 | tf_op jit(solution)/shard_map/ppermute | solution.py:204
  74.5 1.4 shard_map.88
  76.0 3.6 %collective-permute-start.12 = (bf16[128,1536]{1,0:T(8,128)(2,1)S(1)}, bf16[128,1536]{1,0:T(8,128)(2,1)S(1)}, u32[]{:S(2)}, u32[]{:S(2)}) collective-permute-start(bf16[128,1536]{1,0:T(8,128)(2,1)S(1)} %shard_map.88), channel_id=1, source_target_pairs={{256,320},{264,328},{272,336},{280,344},{288,352},{296,360},{304,3... | collective-permute-start | bytes 1179656 | tf_op jit(solution)/shard_map/ppermute | solution.py:204
  79.6 1.4 shard_map.87
  81.1 2.7 %collective-permute-start.11 = (bf16[128,1536]{1,0:T(8,128)(2,1)S(1)}, bf16[128,1536]{1,0:T(8,128)(2,1)S(1)}, u32[]{:S(2)}, u32[]{:S(2)}) collective-permute-start(bf16[128,1536]{1,0:T(8,128)(2,1)S(1)} %shard_map.87), channel_id=1, source_target_pairs={{256,320},{264,328},{272,336},{280,344},{288,352},{296,360},{304,3... | collective-permute-start | bytes 1179656 | tf_op jit(solution)/shard_map/ppermute | solution.py:204
  86.0 3.4 %collective-permute-start.14 = (bf16[128,1536]{1,0:T(8,128)(2,1)S(1)}, bf16[128,1536]{1,0:T(8,128)(2,1)S(1)}, u32[]{:S(2)}, u32[]{:S(2)}) collective-permute-start(bf16[128,1536]{1,0:T(8,128)(2,1)S(1)} %shard_map.91), channel_id=1, source_target_pairs={{320,384},{328,392},{336,400},{344,408},{352,416},{360,424},{368,4... | collective-permute-start | bytes 1179656 | tf_op jit(solution)/shard_map/ppermute | solution.py:204
  90.4 3.2 %collective-permute-start.13 = (bf16[128,1536]{1,0:T(8,128)(2,1)S(1)}, bf16[128,1536]{1,0:T(8,128)(2,1)S(1)}, u32[]{:S(2)}, u32[]{:S(2)}) collective-permute-start(bf16[128,1536]{1,0:T(8,128)(2,1)S(1)} %shard_map.90), channel_id=1, source_target_pairs={{320,384},{328,392},{336,400},{344,408},{352,416},{360,424},{368,4... | collective-permute-start | bytes 1179656 | tf_op jit(solution)/shard_map/ppermute | solution.py:204
  95.2 4.0 %collective-permute-start.16 = (bf16[128,1536]{1,0:T(8,128)(2,1)S(1)}, bf16[128,1536]{1,0:T(8,128)(2,1)S(1)}, u32[]{:S(2)}, u32[]{:S(2)}) collective-permute-start(bf16[128,1536]{1,0:T(8,128)(2,1)S(1)} %shard_map.94), channel_id=1, source_target_pairs={{384,448},{392,456},{400,464},{408,472},{416,480},{424,488},{432,4... | collective-permute-start | bytes 1179656 | tf_op jit(solution)/shard_map/ppermute | solution.py:204
  100.2 3.2 %collective-permute-start.15 = (bf16[128,1536]{1,0:T(8,128)(2,1)S(1)}, bf16[128,1536]{1,0:T(8,128)(2,1)S(1)}, u32[]{:S(2)}, u32[]{:S(2)}) collective-permute-start(bf16[128,1536]{1,0:T(8,128)(2,1)S(1)} %shard_map.93), channel_id=1, source_target_pairs={{384,448},{392,456},{400,464},{408,472},{416,480},{424,488},{432,4... | collective-permute-start | bytes 1179656 | tf_op jit(solution)/shard_map/ppermute | solution.py:204
  104.0 1.2 shard_map.99
  105.2 3.7 %collective-permute-start.18 = (bf16[128,1536]{1,0:T(8,128)(2,1)S(1)}, bf16[128,1536]{1,0:T(8,128)(2,1)S(1)}, u32[]{:S(2)}, u32[]{:S(2)}) collective-permute-start(bf16[128,1536]{1,0:T(8,128)(2,1)S(1)} %shard_map.99), channel_id=1, source_target_pairs={{132,68},{140,76},{148,84},{156,92},{164,100},{172,108},{180,116},... | collective-permute-start | bytes 1179656 | tf_op jit(solution)/shard_map/ppermute | solution.py:204
  109.9 3.2 %collective-permute-start.17 = (bf16[128,1536]{1,0:T(8,128)(2,1)S(1)}, bf16[128,1536]{1,0:T(8,128)(2,1)S(1)}, u32[]{:S(2)}, u32[]{:S(2)}) collective-permute-start(bf16[128,1536]{1,0:T(8,128)(2,1)S(1)} %shard_map.98), channel_id=1, source_target_pairs={{132,68},{140,76},{148,84},{156,92},{164,100},{172,108},{180,116},... | collective-permute-start | bytes 1179656 | tf_op jit(solution)/shard_map/ppermute | solution.py:204
  113.7 7.2 %all_to_all.25.parts_ref = f32[4,64,128]{2,1,0:T(8,128)S(1)} all-to-all(f32[4,64,128]{2,1,0:T(8,128)S(1)} %broadcast_in_dim.8), channel_id=1, replica_groups=mesh['pipe'=8,'dp'=16,'tensor'=4] {'tensor'}, dimensions={0} | all-to-all | bytes 262144 | tf_op jit(solution)/shard_map/all_to_all | solution.py:275
  120.9 11.4 %all_to_all.26.depth_ref = bf16[8,64,128]{2,1,0:T(8,128)(2,1)S(1)} all-to-all(bf16[8,64,128]{2,1,0:T(8,128)(2,1)S(1)} %shard_map.96), channel_id=1, replica_groups={{0,4,16,20,32,36,48,52},{8,12,24,28,40,44,56,60},{1,5,17,21,33,37,49,53..., dimensions={0} | all-to-all | bytes 262144 | tf_op jit(solution)/shard_map/all_to_all | solution.py:277
  132.3 2.2 %shard_map.97 = bf16[224,256]{1,0:T(8,128)(2,1)S(1)} custom-call(bf16[8,64,128]{2,1,0:T(8,128)(2,1)S(1)} %all_to_all.26.depth_ref, bf16[256,32]{1,0:T(8,128)(2,1)S(1)} %copy-done.10, bf16[8,704,128]{2,1,0:T(8,128)(2,1)} %all-to-all-done.1.gathered_ref), custom_call_target="tpu_custom_call" | custom-call | flops 100663296 | bytes 1048576 | tf_op jit(solution)/shard_map/pallas_call | solution.py:278
  134.6 7.9 %collective-permute-start.19 = (bf16[224,256]{1,0:T(8,128)(2,1)S(1)}, bf16[224,256]{1,0:T(8,128)(2,1)S(1)}, u32[]{:S(2)}, u32[]{:S(2)}) collective-permute-start(bf16[224,256]{1,0:T(8,128)(2,1)S(1)} %shard_map.97), channel_id=1, source_target_pairs={{0,8},{4,12},{8,0},{12,4},{16,24},{20,28},{24,16},{28,20},{32,40},... | collective-permute-start | bytes 344072 | tf_op jit(solution)/shard_map/ppermute | solution.py:286
  142.5 1.7 shard_map.101
  144.3 2.2 %collective-permute-start.21 = (bf16[128,1536]{1,0:T(8,128)(2,1)}, bf16[128,1536]{1,0:T(8,128)(2,1)}, u32[]{:S(2)}, u32[]{:S(2)}) collective-permute-start(bf16[128,1536]{1,0:T(8,128)(2,1)} %shard_map.101), channel_id=1, source_target_pairs={{68,4},{76,12},{84,20},{92,28},{100,36},{108,44},{116,52},{124,60}... | collective-permute-start | bytes 1179656 | tf_op jit(solution)/shard_map/ppermute | solution.py:204
  146.4 1.7 shard_map.100
  148.2 2.2 %collective-permute-start.20 = (bf16[128,1536]{1,0:T(8,128)(2,1)}, bf16[128,1536]{1,0:T(8,128)(2,1)}, u32[]{:S(2)}, u32[]{:S(2)}) collective-permute-start(bf16[128,1536]{1,0:T(8,128)(2,1)} %shard_map.100), channel_id=1, source_target_pairs={{68,4},{76,12},{84,20},{92,28},{100,36},{108,44},{116,52},{124,60}... | collective-permute-start | bytes 1179656 | tf_op jit(solution)/shard_map/ppermute | solution.py:204
  150.4 3.8 %collective-permute-done.19 = bf16[224,256]{1,0:T(8,128)(2,1)S(1)} collective-permute-done((bf16[224,256]{1,0:T(8,128)(2,1)S(1)}, bf16[224,256]{1,0:T(8,128)(2,1)S(1)}, u32[]{:S(2)}, u32[]{:S(2)}) %collective-permute-start.19) | collective-permute-done | bytes 114720 | tf_op jit(solution)/shard_map/ppermute | solution.py:286
  156.6 4.1 %all-to-all-start.4 = ((bf16[4,192,256]{2,1,0:T(8,128)(2,1)}), bf16[4,192,256]{2,1,0:T(8,128)(2,1)}, u32[]{:S(2)}, u32[]{:S(2)}) async-start(bf16[4,192,256]{2,1,0:T(8,128)(2,1)} %broadcast_in_dim.9), calls=%async_computation.4 | async-start | bytes 786432 | tf_op jit(solution)/shard_map/all_to_all | solution.py:294
  161.9 6.0 %all-to-all-done.4 = bf16[4,192,256]{2,1,0:T(8,128)(2,1)} async-done(((bf16[4,192,256]{2,1,0:T(8,128)(2,1)}), bf16[4,192,256]{2,1,0:T(8,128)(2,1)}, u32[]{:S(2)}, u32[]{:S(2)}) %all-to-all-start.4) | async-done | bytes 393248 | tf_op jit(solution)/shard_map/all_to_all | solution.py:294
  167.9 3.9 %collective-permute-start.23 = (bf16[4,192,256]{2,1,0:T(8,128)(2,1)}, bf16[4,192,256]{2,1,0:T(8,128)(2,1)S(1)}, u32[]{:S(2)}, u32[]{:S(2)}) collective-permute-start(bf16[4,192,256]{2,1,0:T(8,128)(2,1)} %all-to-all-done.4), channel_id=1, source_target_pairs={{0,4},{4,0},{8,12},{12,8},{16,20},{20,16},{24,28},{28,24},{32,36},... | collective-permute-start | bytes 1179656 | tf_op jit(solution)/shard_map/ppermute | solution.py:198
  172.2 1.4 fusion.1
  173.5 1.9 %collective-permute-start.22 = (bf16[128,1536]{1,0:T(8,128)(2,1)}, bf16[128,1536]{1,0:T(8,128)(2,1)S(1)}, u32[]{:S(2)}, u32[]{:S(2)}) collective-permute-start(bf16[128,1536]{1,0:T(8,128)(2,1)} %collective-permute-done.20), channel_id=1, source_target_pairs={{4,0},{12,8},{20,16},{28,24},{36,32},{44,40},{52,48},{60,56},{5,1}... | collective-permute-start | bytes 1179656 | tf_op jit(solution)/shard_map/ppermute | solution.py:312
  176.5 1.3 convert_multiply_fusion
  177.8 2.2 %shard_map.103 = bf16[128,1536]{1,0:T(8,128)(2,1)} custom-call(s32[3]{0:T(128)S(1)} %pad_add_fusion.place_ref, bf16[128,1536]{1,0:T(8,128)(2,1)S(1)} %collective-permute-done.22.given_ref, bf16[128,1536]{1,0:T(8,128)(2,1)} %collective-permute-done.21.kept_ref, bf16[4,128,1536]{2,1,0:T(8,128)(2,1)S(1)} %bitcast.41, ...), custom_call_target="tpu_custom_call" | custom-call | flops 1572864 | bytes 3145728 | tf_op jit(solution)/shard_map/pallas_call | solution.py:313
  (96 shorter events, 26.2 us)
Async XLA Ops:
  0.6 38.7 %copy-start = (bf16[4,1,128,1536]{3,2,1,0:T(8,128)(2,1)S(1)}, bf16[4,1,128,1536]{3,2,1,0:T(8,128)(2,1)}, u32[]{:S(2)}) copy-start(bf16[4,1,128,1536]{3,2,1,0:T(8,128)(2,1)} %param.6) | copy-start | bytes 4718596
  0.6 4.3 %collective-permute-start.1 = (bf16[128,1536]{1,0:T(8,128)(2,1)}, bf16[128,1536]{1,0:T(8,128)(2,1)S(1)}, u32[]{:S(2)}, u32[]{:S(2)}) collective-permute-start(bf16[128,1536]{1,0:T(8,128)(2,1)} %bitcast.42), channel_id=1, source_target_pairs={{0,4},{4,0},{8,12},{12,8},{16,20},{20,16},{24,28},{28,24},{32,36},... | collective-permute-start | bytes 1179656 | tf_op jit(solution)/shard_map/ppermute | solution.py:198
  3.4 6.9 %collective-permute-start = (bf16[128,1536]{1,0:T(8,128)(2,1)}, bf16[128,1536]{1,0:T(8,128)(2,1)}, u32[]{:S(2)}, u32[]{:S(2)}) collective-permute-start(bf16[128,1536]{1,0:T(8,128)(2,1)} %bitcast.43), channel_id=1, source_target_pairs={{0,64},{8,72},{16,80},{24,88},{32,96},{40,104},{48,112},{56,120},{... | collective-permute-start | bytes 1179656 | tf_op jit(solution)/shard_map/ppermute | solution.py:204
  4.9 5.3 %copy-start.11 = (bf16[128,1536]{1,0:T(8,128)(2,1)}, bf16[128,1536]{1,0:T(8,128)(2,1)S(1)}, u32[]{:S(2)}) copy-start(bf16[128,1536]{1,0:T(8,128)(2,1)S(1)} %collective-permute-done.1.odd_ref) | copy-start | bytes 1179652
  4.9 5.3 %collective-permute-start.2 = (bf16[128,1536]{1,0:T(8,128)(2,1)S(1)}, bf16[128,1536]{1,0:T(8,128)(2,1)}, u32[]{:S(2)}, u32[]{:S(2)}) collective-permute-start(bf16[128,1536]{1,0:T(8,128)(2,1)S(1)} %collective-permute-done.1.odd_ref), channel_id=1, source_target_pairs={{0,64},{8,72},{16,80},{24,88},{32,96},{40,104},{48,112},{56,120},{... | collective-permute-start | bytes 1179656 | tf_op jit(solution)/shard_map/ppermute | solution.py:204
  6.3 1.0 copy-start.1
  7.3 1.1 copy-start.4
  9.2 17.4 %copy-start.18 = (bf16[1,256,32]{1,2,0:T(8,128)(2,1)S(1)}, bf16[1,256,32]{1,2,0:T(8,128)(2,1)}, u32[]{:S(2)}) copy-start(bf16[1,256,32]{1,2,0:T(8,128)(2,1)} %param.9) | copy-start | bytes 49156
  9.5 0.7 copy-start.14
  10.2 12.1 %copy-start.13 = (bf16[4,128,384]{2,1,0:T(8,128)(2,1)}, bf16[4,128,384]{2,1,0:T(8,128)(2,1)S(1)}, u32[]{:S(2)}) copy-start(bf16[4,128,384]{2,1,0:T(8,128)(2,1)S(1)} %get-tuple-element.50) | copy-start | bytes 1179652
  10.3 29.1 %collective-permute-start.6 = (bf16[4,128,1536]{2,1,0:T(8,128)(2,1)}, bf16[4,128,1536]{2,1,0:T(8,128)(2,1)S(1)}, u32[]{:S(2)}, u32[]{:S(2)}) collective-permute-start(bf16[4,128,1536]{2,1,0:T(8,128)(2,1)} %bitcast.25), channel_id=1, source_target_pairs={{0,4},{4,0},{8,12},{12,8},{16,20},{20,16},{24,28},{28,24},{32,36},... | collective-permute-start | bytes 4718600 | tf_op jit(solution)/shard_map/ppermute | solution.py:198
  19.5 16.0 %collective-permute-start.3 = (bf16[128,1536]{1,0:T(8,128)(2,1)}, bf16[128,1536]{1,0:T(8,128)(2,1)}, u32[]{:S(2)}, u32[]{:S(2)}) collective-permute-start(bf16[128,1536]{1,0:T(8,128)(2,1)} %collective-permute-done.even_ref), channel_id=1, source_target_pairs={{64,128},{72,136},{80,144},{88,152},{96,160},{104,168},{112,176},{... | collective-permute-start | bytes 1179656 | tf_op jit(solution)/shard_map/ppermute | solution.py:204
  20.9 14.6 %collective-permute-start.4 = (bf16[128,1536]{1,0:T(8,128)(2,1)}, bf16[128,1536]{1,0:T(8,128)(2,1)}, u32[]{:S(2)}, u32[]{:S(2)}) collective-permute-start(bf16[128,1536]{1,0:T(8,128)(2,1)} %collective-permute-done.2.odd_ref), channel_id=1, source_target_pairs={{64,128},{72,136},{80,144},{88,152},{96,160},{104,168},{112,176},{... | collective-permute-start | bytes 1179656 | tf_op jit(solution)/shard_map/ppermute | solution.py:204
  22.3 12.4 %all-to-all-start = ((bf16[4,128,384]{2,1,0:T(8,128)(2,1)}), bf16[4,128,384]{2,1,0:T(8,128)(2,1)S(1)}, u32[]{:S(2)}, u32[]{:S(2)}) async-start(bf16[4,128,384]{2,1,0:T(8,128)(2,1)} %copy-done.13), calls=%async_computation | async-start | bytes 786432 | tf_op jit(solution)/shard_map/all_to_all | solution.py:216
  35.5 1.0 copy-start.7
  36.5 0.8 copy-start.9
  37.3 1.0 copy-start.15
  39.3 2.9 %copy-start.20 = (f32[128,128]{1,0:T(8,128)}, f32[128,128]{1,0:T(8,128)S(1)}, u32[]{:S(2)}) copy-start(f32[128,128]{1,0:T(8,128)S(1)} %get-tuple-element.93.factor_ref) | copy-start | bytes 196612
  39.3 4.0 %copy-start.8 = (bf16[8,704,128]{2,1,0:T(8,128)(2,1)}, bf16[8,704,128]{2,1,0:T(8,128)(2,1)S(1)}, u32[]{:S(2)}) copy-start(bf16[8,704,128]{2,1,0:T(8,128)(2,1)S(1)} %get-tuple-element.67) | copy-start | bytes 4325380
  39.3 1.3 copy-start.2
  40.6 1.0 copy-start.12
  43.3 31.2 %all-to-all-start.1 = ((bf16[8,704,128]{2,1,0:T(8,128)(2,1)}), bf16[8,704,128]{2,1,0:T(8,128)(2,1)}, u32[]{:S(2)}, u32[]{:S(2)}) async-start(bf16[8,704,128]{2,1,0:T(8,128)(2,1)} %copy-done.8), calls=%async_computation.1 | async-start | bytes 2883584 | tf_op jit(solution)/shard_map/all_to_all | solution.py:270
  50.5 3.1 %collective-permute-start.5 = (f32[128,32]{1,0:T(8,128)S(1)}, f32[128,32]{1,0:T(8,128)S(1)}, u32[]{:S(2)}, u32[]{:S(2)}) collective-permute-start(f32[128,32]{1,0:T(8,128)S(1)} %get-tuple-element.88.mixing_ref), channel_id=1, source_target_pairs={{0,4},{4,0},{8,12},{12,8},{16,20},{20,16},{24,28},{28,24},{32,36},... | collective-permute-start | bytes 49160 | tf_op jit(solution)/shard_map/ppermute | solution.py:198
  55.0 8.0 %collective-permute-start.8 = (bf16[128,1536]{1,0:T(8,128)(2,1)S(1)}, bf16[128,1536]{1,0:T(8,128)(2,1)S(1)}, u32[]{:S(2)}, u32[]{:S(2)}) collective-permute-start(bf16[128,1536]{1,0:T(8,128)(2,1)S(1)} %shard_map.82), channel_id=1, source_target_pairs={{128,192},{136,200},{144,208},{152,216},{160,224},{168,232},{176,2... | collective-permute-start | bytes 1179656 | tf_op jit(solution)/shard_map/ppermute | solution.py:204
  59.8 9.9 %collective-permute-start.7 = (bf16[128,1536]{1,0:T(8,128)(2,1)S(1)}, bf16[128,1536]{1,0:T(8,128)(2,1)S(1)}, u32[]{:S(2)}, u32[]{:S(2)}) collective-permute-start(bf16[128,1536]{1,0:T(8,128)(2,1)S(1)} %shard_map.81), channel_id=1, source_target_pairs={{128,192},{136,200},{144,208},{152,216},{160,224},{168,232},{176,2... | collective-permute-start | bytes 1179656 | tf_op jit(solution)/shard_map/ppermute | solution.py:204
  64.8 9.7 %collective-permute-start.10 = (bf16[128,1536]{1,0:T(8,128)(2,1)}, bf16[128,1536]{1,0:T(8,128)(2,1)}, u32[]{:S(2)}, u32[]{:S(2)}) collective-permute-start(bf16[128,1536]{1,0:T(8,128)(2,1)} %shard_map.85), channel_id=1, source_target_pairs={{192,256},{200,264},{208,272},{216,280},{224,288},{232,296},{240,3... | collective-permute-start | bytes 1179656 | tf_op jit(solution)/shard_map/ppermute | solution.py:204
  71.5 8.1 %collective-permute-start.9 = (bf16[128,1536]{1,0:T(8,128)(2,1)}, bf16[128,1536]{1,0:T(8,128)(2,1)}, u32[]{:S(2)}, u32[]{:S(2)}) collective-permute-start(bf16[128,1536]{1,0:T(8,128)(2,1)} %shard_map.84), channel_id=1, source_target_pairs={{192,256},{200,264},{208,272},{216,280},{224,288},{232,296},{240,3... | collective-permute-start | bytes 1179656 | tf_op jit(solution)/shard_map/ppermute | solution.py:204
  76.0 9.0 %collective-permute-start.12 = (bf16[128,1536]{1,0:T(8,128)(2,1)S(1)}, bf16[128,1536]{1,0:T(8,128)(2,1)S(1)}, u32[]{:S(2)}, u32[]{:S(2)}) collective-permute-start(bf16[128,1536]{1,0:T(8,128)(2,1)S(1)} %shard_map.88), channel_id=1, source_target_pairs={{256,320},{264,328},{272,336},{280,344},{288,352},{296,360},{304,3... | collective-permute-start | bytes 1179656 | tf_op jit(solution)/shard_map/ppermute | solution.py:204
  81.1 8.3 %collective-permute-start.11 = (bf16[128,1536]{1,0:T(8,128)(2,1)S(1)}, bf16[128,1536]{1,0:T(8,128)(2,1)S(1)}, u32[]{:S(2)}, u32[]{:S(2)}) collective-permute-start(bf16[128,1536]{1,0:T(8,128)(2,1)S(1)} %shard_map.87), channel_id=1, source_target_pairs={{256,320},{264,328},{272,336},{280,344},{288,352},{296,360},{304,3... | collective-permute-start | bytes 1179656 | tf_op jit(solution)/shard_map/ppermute | solution.py:204
  86.0 8.2 %collective-permute-start.14 = (bf16[128,1536]{1,0:T(8,128)(2,1)S(1)}, bf16[128,1536]{1,0:T(8,128)(2,1)S(1)}, u32[]{:S(2)}, u32[]{:S(2)}) collective-permute-start(bf16[128,1536]{1,0:T(8,128)(2,1)S(1)} %shard_map.91), channel_id=1, source_target_pairs={{320,384},{328,392},{336,400},{344,408},{352,416},{360,424},{368,4... | collective-permute-start | bytes 1179656 | tf_op jit(solution)/shard_map/ppermute | solution.py:204
  90.4 8.8 %collective-permute-start.13 = (bf16[128,1536]{1,0:T(8,128)(2,1)S(1)}, bf16[128,1536]{1,0:T(8,128)(2,1)S(1)}, u32[]{:S(2)}, u32[]{:S(2)}) collective-permute-start(bf16[128,1536]{1,0:T(8,128)(2,1)S(1)} %shard_map.90), channel_id=1, source_target_pairs={{320,384},{328,392},{336,400},{344,408},{352,416},{360,424},{368,4... | collective-permute-start | bytes 1179656 | tf_op jit(solution)/shard_map/ppermute | solution.py:204
  95.2 8.8 %collective-permute-start.16 = (bf16[128,1536]{1,0:T(8,128)(2,1)S(1)}, bf16[128,1536]{1,0:T(8,128)(2,1)S(1)}, u32[]{:S(2)}, u32[]{:S(2)}) collective-permute-start(bf16[128,1536]{1,0:T(8,128)(2,1)S(1)} %shard_map.94), channel_id=1, source_target_pairs={{384,448},{392,456},{400,464},{408,472},{416,480},{424,488},{432,4... | collective-permute-start | bytes 1179656 | tf_op jit(solution)/shard_map/ppermute | solution.py:204
  100.2 8.7 %collective-permute-start.15 = (bf16[128,1536]{1,0:T(8,128)(2,1)S(1)}, bf16[128,1536]{1,0:T(8,128)(2,1)S(1)}, u32[]{:S(2)}, u32[]{:S(2)}) collective-permute-start(bf16[128,1536]{1,0:T(8,128)(2,1)S(1)} %shard_map.93), channel_id=1, source_target_pairs={{384,448},{392,456},{400,464},{408,472},{416,480},{424,488},{432,4... | collective-permute-start | bytes 1179656 | tf_op jit(solution)/shard_map/ppermute | solution.py:204
  105.2 29.4 %collective-permute-start.18 = (bf16[128,1536]{1,0:T(8,128)(2,1)S(1)}, bf16[128,1536]{1,0:T(8,128)(2,1)S(1)}, u32[]{:S(2)}, u32[]{:S(2)}) collective-permute-start(bf16[128,1536]{1,0:T(8,128)(2,1)S(1)} %shard_map.99), channel_id=1, source_target_pairs={{132,68},{140,76},{148,84},{156,92},{164,100},{172,108},{180,116},... | collective-permute-start | bytes 1179656 | tf_op jit(solution)/shard_map/ppermute | solution.py:204
  109.9 22.4 %copy-start.10 = (bf16[256,32]{1,0:T(8,128)(2,1)S(1)}, bf16[256,32]{1,0:T(8,128)(2,1)}, u32[]{:S(2)}) copy-start(bf16[256,32]{1,0:T(8,128)(2,1)} %copy.11.weight_ref) | copy-start | bytes 49156
  109.9 24.6 %collective-permute-start.17 = (bf16[128,1536]{1,0:T(8,128)(2,1)S(1)}, bf16[128,1536]{1,0:T(8,128)(2,1)S(1)}, u32[]{:S(2)}, u32[]{:S(2)}) collective-permute-start(bf16[128,1536]{1,0:T(8,128)(2,1)S(1)} %shard_map.98), channel_id=1, source_target_pairs={{132,68},{140,76},{148,84},{156,92},{164,100},{172,108},{180,116},... | collective-permute-start | bytes 1179656 | tf_op jit(solution)/shard_map/ppermute | solution.py:204
  134.6 19.6 %collective-permute-start.19 = (bf16[224,256]{1,0:T(8,128)(2,1)S(1)}, bf16[224,256]{1,0:T(8,128)(2,1)S(1)}, u32[]{:S(2)}, u32[]{:S(2)}) collective-permute-start(bf16[224,256]{1,0:T(8,128)(2,1)S(1)} %shard_map.97), channel_id=1, source_target_pairs={{0,8},{4,12},{8,0},{12,4},{16,24},{20,28},{24,16},{28,20},{32,40},... | collective-permute-start | bytes 344072 | tf_op jit(solution)/shard_map/ppermute | solution.py:286
  144.3 17.6 %collective-permute-start.21 = (bf16[128,1536]{1,0:T(8,128)(2,1)}, bf16[128,1536]{1,0:T(8,128)(2,1)}, u32[]{:S(2)}, u32[]{:S(2)}) collective-permute-start(bf16[128,1536]{1,0:T(8,128)(2,1)} %shard_map.101), channel_id=1, source_target_pairs={{68,4},{76,12},{84,20},{92,28},{100,36},{108,44},{116,52},{124,60}... | collective-permute-start | bytes 1179656 | tf_op jit(solution)/shard_map/ppermute | solution.py:204
  148.1 12.6 %copy-start.23 = (bf16[1,1536]{1,0:T(2,128)(2,1)S(1)}, bf16[1,1536]{1,0:T(2,128)(2,1)}, u32[]{:S(2)}) copy-start(bf16[1,1536]{1,0:T(2,128)(2,1)} %gain_ref.1) | copy-start | bytes 9220
  148.2 12.6 %copy-start.17 = (f32[128,256]{1,0:T(8,128)S(1)}, f32[128,256]{1,0:T(8,128)}, u32[]{:S(2)}) copy-start(f32[128,256]{1,0:T(8,128)} %copy-done.16) | copy-start | bytes 393220
  148.2 12.6 %copy-start.19 = (bf16[1,256,32]{1,2,0:T(8,128)(2,1)S(1)}, bf16[1,256,32]{1,2,0:T(8,128)(2,1)}, u32[]{:S(2)}) copy-start(bf16[1,256,32]{1,2,0:T(8,128)(2,1)} %param.9) | copy-start | bytes 49156
  148.2 12.7 %copy-start.21 = (f32[128,128]{1,0:T(8,128)S(1)}, f32[128,128]{1,0:T(8,128)}, u32[]{:S(2)}) copy-start(f32[128,128]{1,0:T(8,128)} %copy-done.20) | copy-start | bytes 196612
  148.2 23.6 %copy-start.3 = (bf16[1,128,1536]{2,1,0:T(8,128)(2,1)S(1)}, bf16[1,128,1536]{2,1,0:T(8,128)(2,1)}, u32[]{:S(2)}) copy-start(bf16[1,128,1536]{2,1,0:T(8,128)(2,1)} %param.5) | copy-start | bytes 1179652
  148.2 23.6 %copy-start.5 = (bf16[1,1536,256]{2,1,0:T(8,128)(2,1)S(1)}, bf16[1,1536,256]{2,1,0:T(8,128)(2,1)}, u32[]{:S(2)}) copy-start(bf16[1,1536,256]{2,1,0:T(8,128)(2,1)} %param.8) | copy-start | bytes 2359300
  148.2 13.7 %collective-permute-start.20 = (bf16[128,1536]{1,0:T(8,128)(2,1)}, bf16[128,1536]{1,0:T(8,128)(2,1)}, u32[]{:S(2)}, u32[]{:S(2)}) collective-permute-start(bf16[128,1536]{1,0:T(8,128)(2,1)} %shard_map.100), channel_id=1, source_target_pairs={{68,4},{76,12},{84,20},{92,28},{100,36},{108,44},{116,52},{124,60}... | collective-permute-start | bytes 1179656 | tf_op jit(solution)/shard_map/ppermute | solution.py:204
  156.6 11.2 %all-to-all-start.4 = ((bf16[4,192,256]{2,1,0:T(8,128)(2,1)}), bf16[4,192,256]{2,1,0:T(8,128)(2,1)}, u32[]{:S(2)}, u32[]{:S(2)}) async-start(bf16[4,192,256]{2,1,0:T(8,128)(2,1)} %broadcast_in_dim.9), calls=%async_computation.4 | async-start | bytes 786432 | tf_op jit(solution)/shard_map/all_to_all | solution.py:294
  167.9 7.6 %collective-permute-start.23 = (bf16[4,192,256]{2,1,0:T(8,128)(2,1)}, bf16[4,192,256]{2,1,0:T(8,128)(2,1)S(1)}, u32[]{:S(2)}, u32[]{:S(2)}) collective-permute-start(bf16[4,192,256]{2,1,0:T(8,128)(2,1)} %all-to-all-done.4), channel_id=1, source_target_pairs={{0,4},{4,0},{8,12},{12,8},{16,20},{20,16},{24,28},{28,24},{32,36},... | collective-permute-start | bytes 1179656 | tf_op jit(solution)/shard_map/ppermute | solution.py:198
  173.5 4.3 %collective-permute-start.22 = (bf16[128,1536]{1,0:T(8,128)(2,1)}, bf16[128,1536]{1,0:T(8,128)(2,1)S(1)}, u32[]{:S(2)}, u32[]{:S(2)}) collective-permute-start(bf16[128,1536]{1,0:T(8,128)(2,1)} %collective-permute-done.20), channel_id=1, source_target_pairs={{4,0},{12,8},{20,16},{28,24},{36,32},{44,40},{52,48},{60,56},{5,1}... | collective-permute-start | bytes 1179656 | tf_op jit(solution)/shard_map/ppermute | solution.py:312
  (3 other events, 2.1 us)

commit v4 on v3

--- a/solution.py
+++ b/solution.py
@@ -24,7 +24,7 @@
         + [pl.BlockSpec(memory_space=pltpu.VMEM)] * (count - smem),
         out_specs=[pl.BlockSpec(memory_space=pltpu.VMEM)] * len(shapes),
         scratch_shapes=list(scratch),
-        compiler_params=pltpu.CompilerParams(vmem_limit_bytes=6 * 1024 * 1024),
+        compiler_params=pltpu.CompilerParams(vmem_limit_bytes=20 * 1024 * 1024),
         cost_estimate=pl.CostEstimate(flops=flops, bytes_accessed=moved, transcendentals=0),
     )
 
@@ -56,14 +56,14 @@
     return total
 
 
-def put_products(held_ref, incoming_ref, products_ref, start, layers):
+def put_products(held_ref, incoming_ref, products_ref, layer, layers):
     tokens = held_ref.shape[0]
     same = lax.broadcasted_iota(jnp.int32, (tokens, tokens), 0) == lax.broadcasted_iota(jnp.int32, (tokens, tokens), 1)
     for s in range(4):
         every = lax.dot_general(
             incoming_ref[s], held_ref[...], (((1,), (1,)), ((), ())), preferred_element_type=f32
         )
-        products_ref[pl.ds(start + s * layers, 1), :] = jnp.sum(jnp.where(same, every, 0.0), axis=0, keepdims=True)
+        products_ref[pl.ds(s * layers + layer, 1), :] = jnp.sum(jnp.where(same, every, 0.0), axis=0, keepdims=True)
 
 
 def generate_kernel(
@@ -94,31 +94,27 @@
     mixing_ref[...] = jnp.dot(active, weight_ref[...], preferred_element_type=f32)
 
 
-def own_kernel(layers, place_ref, even_ref, odd_ref, even_in_ref, odd_in_ref, products_ref):
+def own_kernel(layers, place_ref, held_ref, incoming_ref, products_ref):
     products_ref[...] = jnp.zeros_like(products_ref)
-
-    @pl.when(place_ref[1] == 0)
-    def _():
-        put_products(even_ref, even_in_ref, products_ref, place_ref[0], layers)
-        put_products(odd_ref, odd_in_ref, products_ref, 4 * layers + place_ref[0], layers)
-
-
-def depth_kernel(turn, layers, place_ref, even_ref, odd_ref, even_in_ref, odd_in_ref, before_ref, products_ref):
+    put_products(held_ref, incoming_ref, products_ref, place_ref[0], layers)
+
+
+def depth_kernel(turn, layers, place_ref, even_ref, odd_ref, incoming_ref, before_ref, products_ref):
     products_ref[...] = before_ref[...]
-
-    @pl.when(place_ref[1] == 0)
-    def _():
-        layer = (place_ref[0] - (turn - 1)) & (layers - 1)
-        put_products(even_ref, even_in_ref, products_ref, layer, layers)
-        put_products(odd_ref, odd_in_ref, products_ref, 4 * layers + layer, layers)
+    layer = (place_ref[0] - (turn - 1)) & (layers - 1)
+    for chain, held_ref in enumerate((even_ref, odd_ref)):
+
+        @pl.when(place_ref[1] == chain)
+        def _():
+            put_products(held_ref, incoming_ref, products_ref, layer, layers)
 
 
 def tiles(shape):
     return [(slice(r, r + 16), slice(at, at + LANES)) for r in range(0, shape[0], 16) for at in range(0, shape[1], LANES)]
 
 
-def hop_kernel(turn, layers, place_ref, held_ref, incoming_ref, mixing_ref, sent_ref):
-    rising = place_ref[1] == 0
+def hop_kernel(turn, chain, layers, place_ref, held_ref, incoming_ref, mixing_ref, sent_ref):
+    rising = place_ref[1] == chain
 
     @pl.when(rising)
     def _():
@@ -132,11 +128,11 @@
             sent_ref[rows, lanes] = total.astype(bf16)
 
 
-def finish_kernel(layers, place_ref, given_ref, kept_ref, incoming_ref, mixing_ref, generated_ref, out_ref):
+def finish_kernel(layers, place_ref, even_ref, odd_ref, incoming_ref, mixing_ref, generated_ref, out_ref):
     even = place_ref[1] == 0
     weights = weights_of(mixing_ref[...], place_ref[0], layers)
     for rows, lanes in tiles(out_ref.shape):
-        came = jnp.where(even, given_ref[rows, lanes].astype(f32), kept_ref[rows, lanes].astype(f32))
+        came = jnp.where(even, odd_ref[rows, lanes].astype(f32), even_ref[rows, lanes].astype(f32))
         total = add_term(rows, lanes, weights, incoming_ref, came)
         out_ref[rows, lanes] = (total + generated_ref[rows, lanes]).astype(bf16)
 
@@ -149,13 +145,13 @@
 
 
 def chunk_kernel(depth_ref, weight_ref, gathered_ref, mine_ref):
-    hidden, columns = weight_ref.shape
+    hidden = weight_ref.shape[0]
     members, rows = gathered_ref.shape[0], gathered_ref.shape[1] - 2 * hidden
     first = jnp.zeros((rows, hidden), f32)
-    second = jnp.zeros((columns, hidden), f32)
+    second = jnp.zeros((depth_ref.shape[1], hidden), f32)
     across = (((1,), (1,)), ((), ()))
     for m in range(members):
-        depth = depth_ref[m // 2 * 2, m % 2 * columns : (m % 2 + 1) * columns]
+        depth = depth_ref[m]
         dactive = jnp.dot(weight_ref[...], depth, preferred_element_type=f32)
         scaled_grad = (dactive * gathered_ref[m, rows : rows + hidden].astype(f32)).astype(bf16)
         first = first + lax.dot_general(gathered_ref[m, :rows], scaled_grad, across, preferred_element_type=f32)
@@ -164,10 +160,8 @@
     mine_ref[rows:] = second.astype(bf16)
 
 
-def gradient_kernel(place_ref, depth_ref, weight_ref, slope_ref, preact_ref, factor_ref, scaled_grad_ref, back_ref):
-    both = depth_ref[place_ref[2]].astype(f32)
-    columns = weight_ref.shape[0]
-    depth_grads = jnp.where(place_ref[1] == 0, both[:columns], both[columns:]).T.astype(bf16)
+def gradient_kernel(depth_ref, weight_ref, slope_ref, preact_ref, factor_ref, scaled_grad_ref, back_ref):
+    depth_grads = depth_ref[0].astype(f32).T.astype(bf16)
     dactive = jnp.dot(depth_grads, weight_ref[...], preferred_element_type=f32)
     dpreact = dactive * slope_ref[...]
     factor = factor_ref[...][:, :1]
@@ -187,24 +181,20 @@
     hidden = first_weight.shape[2]
     columns = 4 * layers
     shape = jax.ShapeDtypeStruct
+    place = jnp.stack([section, lax.axis_index("dp") & 1]).astype(jnp.int32)
+
+    def hop(array, turn, chain):
+        pairs = [(k * size + i, (k + 1) * size + i) for k in range(turn - 1, last) for i in range(chain, size, 2)]
+        if turn > LAG:
+            pairs += [
+                (k * size + i, (k - 1) * size + i) for k in range(layers + LAG - turn, layers) for i in range(1 - chain, size, 2)
+            ]
+        return lax.ppermute(array, ("pipe", "dp"), pairs)
+
+    groups = [[x * 4 + z * 2 + core for x in range(size // 4) for core in range(2)] for z in range(2)]
+    members = size // 2
     index = lax.axis_index("dp")
-    even = lax.shift_right_logical(index, 2) * 2
-    place = jnp.stack([section, index & 1, even]).astype(jnp.int32)
-    members = size // 2
     chunk = width // members
-    groups = [[x * 4 + z * 2 + core for x in range(size // 4) for core in range(2)] for z in range(2)]
-
-    def swap(array):
-        return lax.ppermute(array, "dp", [(i, i ^ 1) for i in range(size)])
-
-    def hop(array, turn):
-        pairs = [(k * size + i, (k + 1) * size + i) for k in range(turn - 1, last) for i in range(0, size, 2)]
-        if turn > LAG:
-            pairs += [(k * size + i, (k - 1) * size + i) for k in range(layers + LAG - turn, layers) for i in range(1, size, 2)]
-        return lax.ppermute(array, ("pipe", "dp"), pairs)
-
-    halves = [current, swap(current)]
-    chains = [hop(halves[h], 1) for h in range(2)]
 
     packed, scaled_turned = call(
         project_kernel,
@@ -214,12 +204,8 @@
         count=3,
     )(current, gains, first_weight[0])
     packed = lax.all_to_all(packed, "tensor", 0, 0, tiled=True)
-    scaled_turned, incoming, *chains = lax.optimization_barrier((scaled_turned, incoming, *chains))
-    across = swap(incoming)
-    rising = [incoming, across]
-    falling = [across, incoming]
-    early = [hop(chains[h], LAG) for h in range(2)]
-    packed, *early = lax.optimization_barrier((packed, *early))
+    chains = [hop(current, 1, chain) for chain in range(2)]
+    packed, *chains = lax.optimization_barrier((packed, *chains))
     mixing, slope, preact, factor, payload = call(
         generate_kernel,
         [
@@ -233,47 +219,48 @@
         20 * tokens * hidden,
         count=3,
     )(packed, second_weight[0], scaled_turned)
-    mixings = [swap(mixing), mixing]
     [products] = call(
         functools.partial(own_kernel, layers),
-        [shape((2 * columns, tokens), f32)],
-        16 * tokens * width,
-        20 * tokens * width,
+        [shape((columns, tokens), f32)],
+        8 * tokens * width,
+        10 * tokens * width,
         smem=1,
-        count=5,
-    )(place, *halves, *rising)
-
-    def advance(turn, h):
+        count=3,
+    )(place, current, incoming)
+
+    def advance(turn, chain):
+        if turn <= LAG:
+            return hop(chains[chain], turn, chain)
         [sent] = call(
-            functools.partial(hop_kernel, turn, layers),
+            functools.partial(hop_kernel, turn, chain, layers),
             [shape((tokens, width), bf16)],
             8 * tokens * width,
             12 * tokens * width,
             smem=1,
             count=4,
-        )(place, chains[h], falling[h], mixings[h])
-        return hop(sent, turn)
+        )(place, chains[chain], incoming, mixing)
+        return hop(sent, turn, chain)
 
     for turn in range(2, layers + 1):
         held = chains
-        chains = early if turn == LAG else [advance(turn, h) for h in range(2)]
+        chains = [advance(turn, chain) for chain in range(2)]
         [products] = call(
             functools.partial(depth_kernel, turn, layers),
-            [shape((2 * columns, tokens), f32)],
-            16 * tokens * width,
-            20 * tokens * width,
+            [shape((columns, tokens), f32)],
+            8 * tokens * width,
+            10 * tokens * width,
             smem=1,
-            count=6,
-        )(place, *held, *rising, products)
+            count=5,
+        )(place, *held, incoming, products)
         if turn == LAG:
             payload, products = lax.optimization_barrier((payload, products))
             gathered = lax.all_to_all(payload, "dp", 0, 0, axis_index_groups=groups, tiled=True)
         if turn == 2 * LAG:
             gathered, products = lax.optimization_barrier((gathered, products))
-        *mixings, products = lax.optimization_barrier((*mixings, products))
-
-    spread = lax.all_to_all(jnp.broadcast_to(products[None], (4, *products.shape)), "tensor", 0, 0, tiled=True)
-    [depth_grads] = call(depth_grad_kernel, [shape((members, 2 * columns, tokens), bf16)], 0, 8 * columns * tokens, count=1)(spread)
+        mixing, products = lax.optimization_barrier((mixing, products))
+
+    spread = lax.all_to_all(jnp.broadcast_to(products[None], (4, columns, tokens)), "tensor", 0, 0, tiled=True)
+    [depth_grads] = call(depth_grad_kernel, [shape((members, columns, tokens), bf16)], 0, 8 * columns * tokens, count=1)(spread)
     depth_all = lax.all_to_all(depth_grads, "dp", 0, 0, axis_index_groups=groups, tiled=True)
     [mine] = call(
         chunk_kernel,
@@ -290,10 +277,10 @@
     spread = jnp.broadcast_to(total[None, :chunk].astype(bf16), (size // 4, chunk, hidden))
     along = [[x * 4 + rest for x in range(size // 4)] for rest in range(4)]
     for turn in range(layers + 1, layers + LAG):
-        chains = [advance(turn, h) for h in range(2)]
+        chains = [advance(turn, chain) for chain in range(2)]
     own = lax.all_to_all(spread, "dp", 0, 0, axis_index_groups=along, tiled=True)
     own, *chains = lax.optimization_barrier((own, *chains))
-    far = swap(own)
+    far = lax.ppermute(own, "dp", [(i, i ^ 1) for i in range(size)])
     near = (index & 1) == 0
     summed = jnp.stack([jnp.where(near, own, far), jnp.where(near, far, own)], axis=1)
     first_grads = summed.astype(f32).reshape(width, hidden) / divisor
@@ -303,13 +290,11 @@
         [shape((tokens, hidden), bf16), shape((tokens, 128), f32)],
         2 * tokens * hidden * columns,
         16 * tokens * hidden,
-        smem=1,
-        count=6,
-    )(place, depth_all, second_weight[0].T, slope, preact, factor)
+        count=5,
+    )(depth_grads, second_weight[0].T, slope, preact, factor)
 
     weighted = lax.dot_general(scaled_grad, first_weight[0], (((1,), (1,)), ((), ())), preferred_element_type=f32)
     generated = weighted * gains[0].astype(f32)[None] - current.astype(f32) * back[:, :1]
-    given = lax.ppermute(chains[0], "dp", [(i, i ^ 1) for i in range(1, size, 2)])
     [output_grads] = call(
         functools.partial(finish_kernel, layers),
         [shape((tokens, width), bf16)],
@@ -317,7 +302,7 @@
         16 * tokens * width,
         smem=1,
         count=6,
-    )(place, given, chains[1], incoming, mixing, generated)
+    )(place, chains[0], chains[1], incoming, mixing, generated)
     return (output_grads[None], first_grads[None], second_grads[None])
 
 

time: 182 us -> 170 us (0.934)
  the two profiles are of different devices: /device:TPU:225 before, /device:TPU:97 now
where the time goes in v4:
time: 170 us; the launch traced here: 168 us
  starting transfers between devices  68 us (40%)
  waiting for transfers between devices  42.3 us (25%)
  Pallas kernels  30.4 us (18%)
  blocking collectives  15.2 us (9%)
  local copies, waits for them, and re-layouts  6.96 us (4%)
  other arithmetic  3.85 us (2%)
    ppermute x18, waiting for transfers between devices, hop(): return lax.ppermute(array, ('pipe', 'dp'), pairs)  37.4 us
    ppermute x18, starting transfers between devices, hop(): return lax.ppermute(array, ('pipe', 'dp'), pairs)  34.9 us
    pallas_call x14, Pallas kernels, advance(): call(functools.partial(hop_kernel, turn, chain, layers), [shape((tokens,...  15 us
    ppermute x1, starting transfers between devices, on_device(): other = lax.ppermute(mine, 'dp', [(i, i ^ 2) for i in range(size)])  9.74 us
    pallas_call x7, Pallas kernels, on_device(): call(functools.partial(depth_kernel, turn, layers), [shape((columns, toke...  9.15 us
    all_to_all x1, blocking collectives, on_device(): lax.all_to_all(depth_grads, 'dp', 0, 0, axis_index_groups=groups, tiled=T...  8.41 us
    ppermute x1, starting transfers between devices, on_device(): far = lax.ppermute(own, 'dp', [(i, i ^ 1) for i in range(size)])  7.68 us
    all_to_all x1, starting transfers between devices, on_device(): lax.all_to_all(payload, 'dp', 0, 0, axis_index_groups=groups, tiled=True)  7.41 us
  transfers between devices with their start and end apart: 23, of which 7 were waited for; matrix products, arithmetic and copies ran while one was open for 2% of the time, Pallas kernels for 17%

profile of v4, /device:TPU:97, one launch (start us, length us, event | category | flops | bytes accessed | tf_op | source)
XLA Modules:
  0.0 168.3 jit_solution(3500489949584298665)
XLA Ops:
  1.5 4.8 %collective-permute-start.1 = (bf16[128,1536]{1,0:T(8,128)(2,1)}, bf16[128,1536]{1,0:T(8,128)(2,1)}, u32[]{:S(2)}, u32[]{:S(2)}) collective-permute-start(bf16[128,1536]{1,0:T(8,128)(2,1)} %bitcast.48), channel_id=1, source_target_pairs={{4,68},{12,76},{20,84},{28,92},{36,100},{44,108},{52,116},{60,124}... | collective-permute-start | bytes 1179656 | tf_op jit(solution)/shard_map/ppermute | solution.py:192
  6.2 1.0 copy-done.1
  7.2 1.1 copy-done.3
  9.1 1.1 shard_map.76
  10.1 4.2 %all-to-all-start = ((bf16[4,128,384]{2,1,0:T(8,128)(2,1)}), bf16[4,128,384]{2,1,0:T(8,128)(2,1)S(1)}, u32[]{:S(2)}, u32[]{:S(2)}) async-start(bf16[4,128,384]{2,1,0:T(8,128)(2,1)} %get-tuple-element.39), calls=%async_computation | async-start | bytes 786432 | tf_op jit(solution)/shard_map/all_to_all | solution.py:206
  14.5 1.1 shard_map.78.before_ref
  15.6 4.9 %all-to-all-done.parts_ref = bf16[4,128,384]{2,1,0:T(8,128)(2,1)S(1)} async-done(((bf16[4,128,384]{2,1,0:T(8,128)(2,1)}), bf16[4,128,384]{2,1,0:T(8,128)(2,1)S(1)}, u32[]{:S(2)}, u32[]{:S(2)}) %all-to-all-start) | async-done | bytes 393248 | tf_op jit(solution)/shard_map/all_to_all | solution.py:206
  20.6 1.7 %shard_map.79.before_ref = f32[32,128]{1,0:T(8,128)S(1)} custom-call(s32[2]{0:T(128)S(1)} %pad_add_fusion.place_ref, bf16[128,1536]{1,0:T(8,128)(2,1)S(1)} %collective-permute-done.even_ref, bf16[128,1536]{1,0:T(8,128)(2,1)} %collective-permute-done.1.odd_ref, bf16[4,128,1536]{2,1,0:T(8,128)(2,1)S(1)} %bitcast.25, f32[32,128]{1,0:T(8,128)S(1)} %shard_map.78.before_ref), custom_call_target="tpu_custom_call" | custom-call | flops 1572864 | bytes 1966080 | tf_op jit(solution)/shard_map/pallas_call | solution.py:247
  22.7 1.1 copy-done.5
  25.7 7.4 %all-to-all-start.1 = ((bf16[8,704,128]{2,1,0:T(8,128)(2,1)}), bf16[8,704,128]{2,1,0:T(8,128)(2,1)S(1)}, u32[]{:S(2)}, u32[]{:S(2)}) async-start(bf16[8,704,128]{2,1,0:T(8,128)(2,1)} %copy-done.5), calls=%async_computation.1 | async-start | bytes 2883584 | tf_op jit(solution)/shard_map/all_to_all | solution.py:257
  33.1 3.5 %collective-permute-start.3 = (bf16[128,1536]{1,0:T(8,128)(2,1)}, bf16[128,1536]{1,0:T(8,128)(2,1)S(1)}, u32[]{:S(2)}, u32[]{:S(2)}) collective-permute-start(bf16[128,1536]{1,0:T(8,128)(2,1)} %collective-permute-done.1.odd_ref), channel_id=1, source_target_pairs={{68,132},{76,140},{84,148},{92,156},{100,164},{108,172},{116,180},... | collective-permute-start | bytes 1179656 | tf_op jit(solution)/shard_map/ppermute | solution.py:192
  37.4 7.8 %collective-permute-done.3.odd_ref.held_ref = bf16[128,1536]{1,0:T(8,128)(2,1)S(1)} collective-permute-done((bf16[128,1536]{1,0:T(8,128)(2,1)}, bf16[128,1536]{1,0:T(8,128)(2,1)S(1)}, u32[]{:S(2)}, u32[]{:S(2)}) %collective-permute-start.3) | collective-permute-done | bytes 393248 | tf_op jit(solution)/shard_map/ppermute | solution.py:192
  45.8 4.8 %collective-permute-start.5 = (bf16[128,1536]{1,0:T(8,128)(2,1)S(1)}, bf16[128,1536]{1,0:T(8,128)(2,1)S(1)}, u32[]{:S(2)}, u32[]{:S(2)}) collective-permute-start(bf16[128,1536]{1,0:T(8,128)(2,1)S(1)} %shard_map.82), channel_id=1, source_target_pairs={{132,196},{140,204},{148,212},{156,220},{164,228},{172,236},{180,2... | collective-permute-start | bytes 1179656 | tf_op jit(solution)/shard_map/ppermute | solution.py:192
  50.5 1.0 shard_map.81
  52.2 1.1 shard_map.80.before_ref
  53.4 4.0 %collective-permute-done.5.odd_ref.held_ref = bf16[128,1536]{1,0:T(8,128)(2,1)S(1)} collective-permute-done((bf16[128,1536]{1,0:T(8,128)(2,1)S(1)}, bf16[128,1536]{1,0:T(8,128)(2,1)S(1)}, u32[]{:S(2)}, u32[]{:S(2)}) %collective-permute-start.5) | collective-permute-done | bytes 393248 | tf_op jit(solution)/shard_map/ppermute | solution.py:192
  57.3 1.3 shard_map.85
  58.7 6.1 %collective-permute-start.7 = (bf16[128,1536]{1,0:T(8,128)(2,1)}, bf16[128,1536]{1,0:T(8,128)(2,1)}, u32[]{:S(2)}, u32[]{:S(2)}) collective-permute-start(bf16[128,1536]{1,0:T(8,128)(2,1)} %shard_map.85), channel_id=1, source_target_pairs={{196,260},{204,268},{212,276},{220,284},{228,292},{236,300},{244,3... | collective-permute-start | bytes 1179656 | tf_op jit(solution)/shard_map/ppermute | solution.py:192
  64.7 1.7 %shard_map.84 = bf16[128,1536]{1,0:T(8,128)(2,1)} custom-call(s32[2]{0:T(128)S(1)} %pad_add_fusion.place_ref, bf16[128,1536]{1,0:T(8,128)(2,1)S(1)} %collective-permute-done.4.even_ref.held_ref, bf16[4,128,1536]{2,1,0:T(8,128)(2,1)S(1)} %bitcast.30, f32[128,32]{1,0:T(8,128)S(1)} %get-tuple-element.65.mixing_ref), custom_call_target="tpu_custom_call" | custom-call | flops 1572864 | bytes 2359296 | tf_op jit(solution)/shard_map/pallas_call | solution.py:234
  66.5 1.4 collective-permute-start.6
  67.9 1.1 shard_map.83.before_ref
  69.0 1.2 collective-permute-done.7.odd_ref.held_ref
  70.2 1.0 shard_map.88
  72.0 1.4 shard_map.87
  74.1 1.7 %shard_map.86.before_ref = f32[32,128]{1,0:T(8,128)S(1)} custom-call(s32[2]{0:T(128)S(1)} %pad_add_fusion.place_ref, bf16[128,1536]{1,0:T(8,128)(2,1)} %collective-permute-done.6.even_ref.held_ref, bf16[128,1536]{1,0:T(8,128)(2,1)} %collective-permute-done.7.odd_ref.held_ref, bf16[4,128,1536]{2,1,0:T(8,128)(2,1)S(1)} %bitcast.34, ...), custom_call_target="tpu_custom_call" | custom-call | flops 1572864 | bytes 1966080 | tf_op jit(solution)/shard_map/pallas_call | solution.py:247
  78.1 1.3 collective-permute-start.10
  79.4 1.1 shard_map.89.before_ref
  81.9 12.2 %collective-permute-done.10.even_ref.held_ref = bf16[128,1536]{1,0:T(8,128)(2,1)S(1)} collective-permute-done((bf16[128,1536]{1,0:T(8,128)(2,1)S(1)}, bf16[128,1536]{1,0:T(8,128)(2,1)S(1)}, u32[]{:S(2)}, u32[]{:S(2)}) %collective-permute-start.10) | collective-permute-done | bytes 393248 | tf_op jit(solution)/shard_map/ppermute | solution.py:192
  95.0 1.9 %collective-permute-start.12 = (bf16[128,1536]{1,0:T(8,128)(2,1)S(1)}, bf16[128,1536]{1,0:T(8,128)(2,1)S(1)}, u32[]{:S(2)}, u32[]{:S(2)}) collective-permute-start(bf16[128,1536]{1,0:T(8,128)(2,1)S(1)} %shard_map.93), channel_id=1, source_target_pairs={{384,448},{392,456},{400,464},{408,472},{416,480},{424,488},{432,4... | collective-permute-start | bytes 1179656 | tf_op jit(solution)/shard_map/ppermute | solution.py:192
  97.0 1.1 shard_map.92.before_ref
  99.4 6.0 %collective-permute-done.12.even_ref.held_ref = bf16[128,1536]{1,0:T(8,128)(2,1)S(1)} collective-permute-done((bf16[128,1536]{1,0:T(8,128)(2,1)S(1)}, bf16[128,1536]{1,0:T(8,128)(2,1)S(1)}, u32[]{:S(2)}, u32[]{:S(2)}) %collective-permute-start.12) | collective-permute-done | bytes 393248 | tf_op jit(solution)/shard_map/ppermute | solution.py:192
  105.4 1.2 shard_map.98
  106.6 2.1 %collective-permute-start.14 = (bf16[128,1536]{1,0:T(8,128)(2,1)S(1)}, bf16[128,1536]{1,0:T(8,128)(2,1)S(1)}, u32[]{:S(2)}, u32[]{:S(2)}) collective-permute-start(bf16[128,1536]{1,0:T(8,128)(2,1)S(1)} %shard_map.98), channel_id=1, source_target_pairs={{132,68},{140,76},{148,84},{156,92},{164,100},{172,108},{180,116},... | collective-permute-start | bytes 1179656 | tf_op jit(solution)/shard_map/ppermute | solution.py:192
  108.7 1.1 shard_map.95
  109.8 6.8 %all_to_all.25.parts_ref = f32[4,32,128]{2,1,0:T(8,128)S(1)} all-to-all(f32[4,32,128]{2,1,0:T(8,128)S(1)} %broadcast_in_dim.8), channel_id=1, replica_groups=mesh['pipe'=8,'dp'=16,'tensor'=4] {'tensor'}, dimensions={0} | all-to-all | bytes 131072 | tf_op jit(solution)/shard_map/all_to_all | solution.py:262
  116.7 8.4 %all_to_all.26.depth_ref = bf16[8,32,128]{2,1,0:T(8,128)(2,1)S(1)} all-to-all(bf16[8,32,128]{2,1,0:T(8,128)(2,1)S(1)} %shard_map.96.depth_ref), channel_id=1, replica_groups={{0,4,16,20,32,36,48,52},{8,12,24,28,40,44,56,60},{1,5,17,21,33,37,49,53..., dimensions={0} | all-to-all | bytes 131072 | tf_op jit(solution)/shard_map/all_to_all | solution.py:264
  126.0 9.7 %collective-permute-start.16 = (bf16[224,256]{1,0:T(8,128)(2,1)S(1)}, bf16[224,256]{1,0:T(8,128)(2,1)S(1)}, u32[]{:S(2)}, u32[]{:S(2)}) collective-permute-start(bf16[224,256]{1,0:T(8,128)(2,1)S(1)} %shard_map.97), channel_id=1, source_target_pairs={{0,8},{4,12},{8,0},{12,4},{16,24},{20,28},{24,16},{28,20},{32,40},... | collective-permute-start | bytes 344072 | tf_op jit(solution)/shard_map/ppermute | solution.py:273
  135.7 1.3 shard_map.101
  137.1 1.4 collective-permute-start.18
  138.5 1.7 %shard_map.100 = bf16[128,1536]{1,0:T(8,128)(2,1)} custom-call(s32[2]{0:T(128)S(1)} %pad_add_fusion.place_ref, bf16[128,1536]{1,0:T(8,128)(2,1)S(1)} %collective-permute-done.14.held_ref, bf16[4,128,1536]{2,1,0:T(8,128)(2,1)S(1)} %bitcast.45, f32[128,32]{1,0:T(8,128)S(1)} %get-tuple-element.65.mixing_ref), custom_call_target="tpu_custom_call" | custom-call | flops 1572864 | bytes 2359296 | tf_op jit(solution)/shard_map/pallas_call | solution.py:234
  140.3 2.1 %collective-permute-start.17 = (bf16[128,1536]{1,0:T(8,128)(2,1)}, bf16[128,1536]{1,0:T(8,128)(2,1)}, u32[]{:S(2)}, u32[]{:S(2)}) collective-permute-start(bf16[128,1536]{1,0:T(8,128)(2,1)} %shard_map.100), channel_id=1, source_target_pairs={{68,4},{76,12},{84,20},{92,28},{100,36},{108,44},{116,52},{124,60}... | collective-permute-start | bytes 1179656 | tf_op jit(solution)/shard_map/ppermute | solution.py:192
  143.2 4.1 %all-to-all-start.4 = ((bf16[4,192,256]{2,1,0:T(8,128)(2,1)}), bf16[4,192,256]{2,1,0:T(8,128)(2,1)}, u32[]{:S(2)}, u32[]{:S(2)}) async-start(bf16[4,192,256]{2,1,0:T(8,128)(2,1)} %broadcast_in_dim.9), calls=%async_computation.4 | async-start | bytes 786432 | tf_op jit(solution)/shard_map/all_to_all | solution.py:281
  148.0 6.2 %collective-permute-done.17.even_ref = bf16[128,1536]{1,0:T(8,128)(2,1)} collective-permute-done((bf16[128,1536]{1,0:T(8,128)(2,1)}, bf16[128,1536]{1,0:T(8,128)(2,1)}, u32[]{:S(2)}, u32[]{:S(2)}) %collective-permute-start.17) | collective-permute-done | bytes 393248 | tf_op jit(solution)/shard_map/ppermute | solution.py:192
  154.1 7.7 %collective-permute-start.19 = (bf16[4,192,256]{2,1,0:T(8,128)(2,1)}, bf16[4,192,256]{2,1,0:T(8,128)(2,1)S(1)}, u32[]{:S(2)}, u32[]{:S(2)}) collective-permute-start(bf16[4,192,256]{2,1,0:T(8,128)(2,1)} %all-to-all-done.4), channel_id=1, source_target_pairs={{0,4},{4,0},{8,12},{12,8},{16,20},{20,16},{24,28},{28,24},{32,36},... | collective-permute-start | bytes 1179656 | tf_op jit(solution)/shard_map/ppermute | solution.py:283
  162.2 1.4 fusion.1
  163.6 2.3 %shard_map.103 = bf16[128,1536]{1,0:T(8,128)(2,1)} custom-call(s32[2]{0:T(128)S(1)} %pad_add_fusion.place_ref, bf16[128,1536]{1,0:T(8,128)(2,1)} %collective-permute-done.17.even_ref, bf16[128,1536]{1,0:T(8,128)(2,1)} %collective-permute-done.18.odd_ref, bf16[4,128,1536]{2,1,0:T(8,128)(2,1)S(1)} %bitcast.46, f32[128,32]{1,0:T(8,128)S(1)} %get-tuple-element.65.mixing_ref, ...), custom_call_target="tpu_custom_call" | custom-call | flops 1572864 | bytes 3145728 | tf_op jit(solution)/shard_map/pallas_call | solution.py:298
  166.0 1.1 select_bitcast_fusion.1
  167.0 1.3 convert_multiply_fusion
  (80 shorter events, 15.9 us)
Async XLA Ops:
  0.6 13.9 %copy-start = (bf16[4,1,128,1536]{3,2,1,0:T(8,128)(2,1)S(1)}, bf16[4,1,128,1536]{3,2,1,0:T(8,128)(2,1)}, u32[]{:S(2)}) copy-start(bf16[4,1,128,1536]{3,2,1,0:T(8,128)(2,1)} %param.6) | copy-start | bytes 4718596
  0.6 19.9 %collective-permute-start = (bf16[128,1536]{1,0:T(8,128)(2,1)}, bf16[128,1536]{1,0:T(8,128)(2,1)S(1)}, u32[]{:S(2)}, u32[]{:S(2)}) collective-permute-start(bf16[128,1536]{1,0:T(8,128)(2,1)} %bitcast.47), channel_id=1, source_target_pairs={{0,64},{8,72},{16,80},{24,88},{32,96},{40,104},{48,112},{56,120},{... | collective-permute-start | bytes 1179656 | tf_op jit(solution)/shard_map/ppermute | solution.py:192
  1.5 19.1 %collective-permute-start.1 = (bf16[128,1536]{1,0:T(8,128)(2,1)}, bf16[128,1536]{1,0:T(8,128)(2,1)}, u32[]{:S(2)}, u32[]{:S(2)}) collective-permute-start(bf16[128,1536]{1,0:T(8,128)(2,1)} %bitcast.48), channel_id=1, source_target_pairs={{4,68},{12,76},{20,84},{28,92},{36,100},{44,108},{52,116},{60,124}... | collective-permute-start | bytes 1179656 | tf_op jit(solution)/shard_map/ppermute | solution.py:192
  6.2 1.0 copy-start.1
  7.2 1.1 copy-start.3
  8.4 0.7 copy-start.17
  9.1 5.3 %copy-start.15 = (bf16[1,256,32]{1,2,0:T(8,128)(2,1)S(1)}, bf16[1,256,32]{1,2,0:T(8,128)(2,1)}, u32[]{:S(2)}) copy-start(bf16[1,256,32]{1,2,0:T(8,128)(2,1)} %param.9) | copy-start | bytes 49156
  9.1 5.5 %copy-start.2 = (bf16[1,128,1536]{2,1,0:T(8,128)(2,1)S(1)}, bf16[1,128,1536]{2,1,0:T(8,128)(2,1)}, u32[]{:S(2)}) copy-start(bf16[1,128,1536]{2,1,0:T(8,128)(2,1)} %param.5) | copy-start | bytes 1179652
  10.1 10.4 %all-to-all-start = ((bf16[4,128,384]{2,1,0:T(8,128)(2,1)}), bf16[4,128,384]{2,1,0:T(8,128)(2,1)S(1)}, u32[]{:S(2)}, u32[]{:S(2)}) async-start(bf16[4,128,384]{2,1,0:T(8,128)(2,1)} %get-tuple-element.39), calls=%async_computation | async-start | bytes 786432 | tf_op jit(solution)/shard_map/all_to_all | solution.py:206
  14.4 7.9 %copy-start.6 = (bf16[256,32]{1,0:T(8,128)(2,1)}, bf16[256,32]{1,0:T(8,128)(2,1)S(1)}, u32[]{:S(2)}) copy-start(bf16[256,32]{1,0:T(8,128)(2,1)S(1)} %copy.11.weight_ref) | copy-start | bytes 49156
  20.5 2.1 %copy-start.8 = (bf16[128,1536]{1,0:T(8,128)(2,1)}, bf16[128,1536]{1,0:T(8,128)(2,1)S(1)}, u32[]{:S(2)}) copy-start(bf16[128,1536]{1,0:T(8,128)(2,1)S(1)} %collective-permute-done.even_ref) | copy-start | bytes 1179652
  22.7 1.1 copy-start.5
  23.8 0.7 copy-start.9
  24.4 0.7 copy-start.11
  25.1 0.6 copy-start.13
  25.7 43.3 %all-to-all-start.1 = ((bf16[8,704,128]{2,1,0:T(8,128)(2,1)}), bf16[8,704,128]{2,1,0:T(8,128)(2,1)S(1)}, u32[]{:S(2)}, u32[]{:S(2)}) async-start(bf16[8,704,128]{2,1,0:T(8,128)(2,1)} %copy-done.5), calls=%async_computation.1 | async-start | bytes 2883584 | tf_op jit(solution)/shard_map/all_to_all | solution.py:257
  33.1 12.0 %collective-permute-start.3 = (bf16[128,1536]{1,0:T(8,128)(2,1)}, bf16[128,1536]{1,0:T(8,128)(2,1)S(1)}, u32[]{:S(2)}, u32[]{:S(2)}) collective-permute-start(bf16[128,1536]{1,0:T(8,128)(2,1)} %collective-permute-done.1.odd_ref), channel_id=1, source_target_pairs={{68,132},{76,140},{84,148},{92,156},{100,164},{108,172},{116,180},... | collective-permute-start | bytes 1179656 | tf_op jit(solution)/shard_map/ppermute | solution.py:192
  36.7 13.8 %collective-permute-start.2 = (bf16[128,1536]{1,0:T(8,128)(2,1)}, bf16[128,1536]{1,0:T(8,128)(2,1)S(1)}, u32[]{:S(2)}, u32[]{:S(2)}) collective-permute-start(bf16[128,1536]{1,0:T(8,128)(2,1)} %copy-done.8), channel_id=1, source_target_pairs={{64,128},{72,136},{80,144},{88,152},{96,160},{104,168},{112,176},{... | collective-permute-start | bytes 1179656 | tf_op jit(solution)/shard_map/ppermute | solution.py:192
  45.8 11.6 %collective-permute-start.5 = (bf16[128,1536]{1,0:T(8,128)(2,1)S(1)}, bf16[128,1536]{1,0:T(8,128)(2,1)S(1)}, u32[]{:S(2)}, u32[]{:S(2)}) collective-permute-start(bf16[128,1536]{1,0:T(8,128)(2,1)S(1)} %shard_map.82), channel_id=1, source_target_pairs={{132,196},{140,204},{148,212},{156,220},{164,228},{172,236},{180,2... | collective-permute-start | bytes 1179656 | tf_op jit(solution)/shard_map/ppermute | solution.py:192
  51.5 13.2 %collective-permute-start.4 = (bf16[128,1536]{1,0:T(8,128)(2,1)S(1)}, bf16[128,1536]{1,0:T(8,128)(2,1)S(1)}, u32[]{:S(2)}, u32[]{:S(2)}) collective-permute-start(bf16[128,1536]{1,0:T(8,128)(2,1)S(1)} %shard_map.81), channel_id=1, source_target_pairs={{128,192},{136,200},{144,208},{152,216},{160,224},{168,232},{176,2... | collective-permute-start | bytes 1179656 | tf_op jit(solution)/shard_map/ppermute | solution.py:192
  58.7 11.5 %collective-permute-start.7 = (bf16[128,1536]{1,0:T(8,128)(2,1)}, bf16[128,1536]{1,0:T(8,128)(2,1)}, u32[]{:S(2)}, u32[]{:S(2)}) collective-permute-start(bf16[128,1536]{1,0:T(8,128)(2,1)} %shard_map.85), channel_id=1, source_target_pairs={{196,260},{204,268},{212,276},{220,284},{228,292},{236,300},{244,3... | collective-permute-start | bytes 1179656 | tf_op jit(solution)/shard_map/ppermute | solution.py:192
  66.5 5.5 %collective-permute-start.6 = (bf16[128,1536]{1,0:T(8,128)(2,1)}, bf16[128,1536]{1,0:T(8,128)(2,1)}, u32[]{:S(2)}, u32[]{:S(2)}) collective-permute-start(bf16[128,1536]{1,0:T(8,128)(2,1)} %shard_map.84), channel_id=1, source_target_pairs={{192,256},{200,264},{208,272},{216,280},{224,288},{232,296},{240,3... | collective-permute-start | bytes 1179656 | tf_op jit(solution)/shard_map/ppermute | solution.py:192
  71.3 4.6 %collective-permute-start.9 = (bf16[128,1536]{1,0:T(8,128)(2,1)S(1)}, bf16[128,1536]{1,0:T(8,128)(2,1)S(1)}, u32[]{:S(2)}, u32[]{:S(2)}) collective-permute-start(bf16[128,1536]{1,0:T(8,128)(2,1)S(1)} %shard_map.88), channel_id=1, source_target_pairs={{260,324},{268,332},{276,340},{284,348},{292,356},{300,364},{308,3... | collective-permute-start | bytes 1179656 | tf_op jit(solution)/shard_map/ppermute | solution.py:192
  73.4 3.7 %collective-permute-start.8 = (bf16[128,1536]{1,0:T(8,128)(2,1)S(1)}, bf16[128,1536]{1,0:T(8,128)(2,1)S(1)}, u32[]{:S(2)}, u32[]{:S(2)}) collective-permute-start(bf16[128,1536]{1,0:T(8,128)(2,1)S(1)} %shard_map.87), channel_id=1, source_target_pairs={{256,320},{264,328},{272,336},{280,344},{288,352},{296,360},{304,3... | collective-permute-start | bytes 1179656 | tf_op jit(solution)/shard_map/ppermute | solution.py:192
  76.4 4.1 %collective-permute-start.11 = (bf16[128,1536]{1,0:T(8,128)(2,1)S(1)}, bf16[128,1536]{1,0:T(8,128)(2,1)S(1)}, u32[]{:S(2)}, u32[]{:S(2)}) collective-permute-start(bf16[128,1536]{1,0:T(8,128)(2,1)S(1)} %shard_map.91), channel_id=1, source_target_pairs={{324,388},{332,396},{340,404},{348,412},{356,420},{364,428},{372,4... | collective-permute-start | bytes 1179656 | tf_op jit(solution)/shard_map/ppermute | solution.py:192
  78.1 15.9 %collective-permute-start.10 = (bf16[128,1536]{1,0:T(8,128)(2,1)S(1)}, bf16[128,1536]{1,0:T(8,128)(2,1)S(1)}, u32[]{:S(2)}, u32[]{:S(2)}) collective-permute-start(bf16[128,1536]{1,0:T(8,128)(2,1)S(1)} %shard_map.90), channel_id=1, source_target_pairs={{320,384},{328,392},{336,400},{344,408},{352,416},{360,424},{368,4... | collective-permute-start | bytes 1179656 | tf_op jit(solution)/shard_map/ppermute | solution.py:192
  81.2 16.9 %collective-permute-start.13 = (bf16[128,1536]{1,0:T(8,128)(2,1)S(1)}, bf16[128,1536]{1,0:T(8,128)(2,1)S(1)}, u32[]{:S(2)}, u32[]{:S(2)}) collective-permute-start(bf16[128,1536]{1,0:T(8,128)(2,1)S(1)} %shard_map.94), channel_id=1, source_target_pairs={{388,452},{396,460},{404,468},{412,476},{420,484},{428,492},{436,5... | collective-permute-start | bytes 1179656 | tf_op jit(solution)/shard_map/ppermute | solution.py:192
  95.0 10.4 %collective-permute-start.12 = (bf16[128,1536]{1,0:T(8,128)(2,1)S(1)}, bf16[128,1536]{1,0:T(8,128)(2,1)S(1)}, u32[]{:S(2)}, u32[]{:S(2)}) collective-permute-start(bf16[128,1536]{1,0:T(8,128)(2,1)S(1)} %shard_map.93), channel_id=1, source_target_pairs={{384,448},{392,456},{400,464},{408,472},{416,480},{424,488},{432,4... | collective-permute-start | bytes 1179656 | tf_op jit(solution)/shard_map/ppermute | solution.py:192
  98.7 27.3 %collective-permute-start.15 = (bf16[128,1536]{1,0:T(8,128)(2,1)S(1)}, bf16[128,1536]{1,0:T(8,128)(2,1)S(1)}, u32[]{:S(2)}, u32[]{:S(2)}) collective-permute-start(bf16[128,1536]{1,0:T(8,128)(2,1)S(1)} %shard_map.99), channel_id=1, source_target_pairs={{128,64},{136,72},{144,80},{152,88},{160,96},{168,104},{176,112},{... | collective-permute-start | bytes 1179656 | tf_op jit(solution)/shard_map/ppermute | solution.py:192
  106.6 18.5 %copy-start.7 = (bf16[256,32]{1,0:T(8,128)(2,1)S(1)}, bf16[256,32]{1,0:T(8,128)(2,1)}, u32[]{:S(2)}) copy-start(bf16[256,32]{1,0:T(8,128)(2,1)} %copy-done.6) | copy-start | bytes 49156
  106.6 19.4 %collective-permute-start.14 = (bf16[128,1536]{1,0:T(8,128)(2,1)S(1)}, bf16[128,1536]{1,0:T(8,128)(2,1)S(1)}, u32[]{:S(2)}, u32[]{:S(2)}) collective-permute-start(bf16[128,1536]{1,0:T(8,128)(2,1)S(1)} %shard_map.98), channel_id=1, source_target_pairs={{132,68},{140,76},{148,84},{156,92},{164,100},{172,108},{180,116},... | collective-permute-start | bytes 1179656 | tf_op jit(solution)/shard_map/ppermute | solution.py:192
  126.0 16.3 %collective-permute-start.16 = (bf16[224,256]{1,0:T(8,128)(2,1)S(1)}, bf16[224,256]{1,0:T(8,128)(2,1)S(1)}, u32[]{:S(2)}, u32[]{:S(2)}) collective-permute-start(bf16[224,256]{1,0:T(8,128)(2,1)S(1)} %shard_map.97), channel_id=1, source_target_pairs={{0,8},{4,12},{8,0},{12,4},{16,24},{20,28},{24,16},{28,20},{32,40},... | collective-permute-start | bytes 344072 | tf_op jit(solution)/shard_map/ppermute | solution.py:273
  137.1 10.9 %collective-permute-start.18 = (bf16[128,1536]{1,0:T(8,128)(2,1)}, bf16[128,1536]{1,0:T(8,128)(2,1)}, u32[]{:S(2)}, u32[]{:S(2)}) collective-permute-start(bf16[128,1536]{1,0:T(8,128)(2,1)} %shard_map.101), channel_id=1, source_target_pairs={{64,0},{72,8},{80,16},{88,24},{96,32},{104,40},{112,48},{120,56},{... | collective-permute-start | bytes 1179656 | tf_op jit(solution)/shard_map/ppermute | solution.py:192
  140.2 7.1 %copy-start.18 = (bf16[1,1536]{1,0:T(2,128)(2,1)S(1)}, bf16[1,1536]{1,0:T(2,128)(2,1)}, u32[]{:S(2)}) copy-start(bf16[1,1536]{1,0:T(2,128)(2,1)} %gain_ref.1) | copy-start | bytes 9220
  140.2 7.1 %copy-start.10 = (f32[128,256]{1,0:T(8,128)S(1)}, f32[128,256]{1,0:T(8,128)}, u32[]{:S(2)}) copy-start(f32[128,256]{1,0:T(8,128)} %copy-done.9) | copy-start | bytes 393220
  140.2 7.2 %copy-start.12 = (f32[128,256]{1,0:T(8,128)S(1)}, f32[128,256]{1,0:T(8,128)}, u32[]{:S(2)}) copy-start(f32[128,256]{1,0:T(8,128)} %copy-done.11) | copy-start | bytes 393220
  140.2 7.2 %copy-start.14 = (f32[128,128]{1,0:T(8,128)S(1)}, f32[128,128]{1,0:T(8,128)}, u32[]{:S(2)}) copy-start(f32[128,128]{1,0:T(8,128)} %copy-done.13) | copy-start | bytes 196612
  140.2 7.2 %copy-start.16 = (bf16[1,256,32]{1,2,0:T(8,128)(2,1)S(1)}, bf16[1,256,32]{1,2,0:T(8,128)(2,1)}, u32[]{:S(2)}) copy-start(bf16[1,256,32]{1,2,0:T(8,128)(2,1)} %param.9) | copy-start | bytes 49156
  140.3 21.6 %copy-start.4 = (bf16[1,1536,256]{2,1,0:T(8,128)(2,1)S(1)}, bf16[1,1536,256]{2,1,0:T(8,128)(2,1)}, u32[]{:S(2)}) copy-start(bf16[1,1536,256]{2,1,0:T(8,128)(2,1)} %param.8) | copy-start | bytes 2359300
  140.3 13.9 %collective-permute-start.17 = (bf16[128,1536]{1,0:T(8,128)(2,1)}, bf16[128,1536]{1,0:T(8,128)(2,1)}, u32[]{:S(2)}, u32[]{:S(2)}) collective-permute-start(bf16[128,1536]{1,0:T(8,128)(2,1)} %shard_map.100), channel_id=1, source_target_pairs={{68,4},{76,12},{84,20},{92,28},{100,36},{108,44},{116,52},{124,60}... | collective-permute-start | bytes 1179656 | tf_op jit(solution)/shard_map/ppermute | solution.py:192
  142.4 5.0 %copy-start.19 = (f32[224,256]{1,0:T(8,128)}, f32[224,256]{1,0:T(8,128)S(1)}, u32[]{:S(2)}) copy-start(f32[224,256]{1,0:T(8,128)S(1)} %convert_add_fusion) | copy-start | bytes 688132
  143.2 10.9 %all-to-all-start.4 = ((bf16[4,192,256]{2,1,0:T(8,128)(2,1)}), bf16[4,192,256]{2,1,0:T(8,128)(2,1)}, u32[]{:S(2)}, u32[]{:S(2)}) async-start(bf16[4,192,256]{2,1,0:T(8,128)(2,1)} %broadcast_in_dim.9), calls=%async_computation.4 | async-start | bytes 786432 | tf_op jit(solution)/shard_map/all_to_all | solution.py:281
  154.1 11.8 %collective-permute-start.19 = (bf16[4,192,256]{2,1,0:T(8,128)(2,1)}, bf16[4,192,256]{2,1,0:T(8,128)(2,1)S(1)}, u32[]{:S(2)}, u32[]{:S(2)}) collective-permute-start(bf16[4,192,256]{2,1,0:T(8,128)(2,1)} %all-to-all-done.4), channel_id=1, source_target_pairs={{0,4},{4,0},{8,12},{12,8},{16,20},{20,16},{24,28},{28,24},{32,36},... | collective-permute-start | bytes 1179656 | tf_op jit(solution)/shard_map/ppermute | solution.py:283

commit v5 on v4

--- a/solution.py
+++ b/solution.py
@@ -252,10 +252,10 @@
             smem=1,
             count=5,
         )(place, *held, incoming, products)
-        if turn == LAG:
+        if turn == LAG + 1:
             payload, products = lax.optimization_barrier((payload, products))
             gathered = lax.all_to_all(payload, "dp", 0, 0, axis_index_groups=groups, tiled=True)
-        if turn == 2 * LAG:
+        if turn == 2 * LAG + 1:
             gathered, products = lax.optimization_barrier((gathered, products))
         mixing, products = lax.optimization_barrier((mixing, products))
 
@@ -279,12 +279,7 @@
     for turn in range(layers + 1, layers + LAG):
         chains = [advance(turn, chain) for chain in range(2)]
     own = lax.all_to_all(spread, "dp", 0, 0, axis_index_groups=along, tiled=True)
-    own, *chains = lax.optimization_barrier((own, *chains))
     far = lax.ppermute(own, "dp", [(i, i ^ 1) for i in range(size)])
-    near = (index & 1) == 0
-    summed = jnp.stack([jnp.where(near, own, far), jnp.where(near, far, own)], axis=1)
-    first_grads = summed.astype(f32).reshape(width, hidden) / divisor
-
     scaled_grad, back = call(
         gradient_kernel,
         [shape((tokens, hidden), bf16), shape((tokens, 128), f32)],
@@ -303,6 +298,10 @@
         smem=1,
         count=6,
     )(place, chains[0], chains[1], incoming, mixing, generated)
+    far, output_grads = lax.optimization_barrier((far, output_grads))
+    near = (index & 1) == 0
+    summed = jnp.stack([jnp.where(near, own, far), jnp.where(near, far, own)], axis=1)
+    first_grads = summed.astype(f32).reshape(width, hidden) / divisor
     return (output_grads[None], first_grads[None], second_grads[None])
 
 

time: 170 us -> 185 us (1.088)
  the two profiles are of different devices: /device:TPU:97 before, /device:TPU:98 now
where the time goes in v5:
time: 185 us; the launch traced here: 184 us
  starting transfers between devices  55.8 us (30%)
  waiting for transfers between devices  54.9 us (30%)
  Pallas kernels  29.3 us (16%)
  blocking collectives  28.8 us (16%)
  local copies, waits for them, and re-layouts  8.58 us (5%)
  other arithmetic  4.44 us (2%)
    ppermute x18, waiting for transfers between devices, hop(): return lax.ppermute(array, ('pipe', 'dp'), pairs)  43.4 us
    ppermute x18, starting transfers between devices, hop(): return lax.ppermute(array, ('pipe', 'dp'), pairs)  36 us
    pallas_call x14, Pallas kernels, advance(): call(functools.partial(hop_kernel, turn, chain, layers), [shape((tokens,...  15 us
    all_to_all x1, blocking collectives, on_device(): packed = lax.all_to_all(packed, 'tensor', 0, 0, tiled=True)  12.1 us
    ppermute x1, waiting for transfers between devices, on_device(): other = lax.ppermute(mine, 'dp', [(i, i ^ 2) for i in range(size)])  11.4 us
    pallas_call x7, Pallas kernels, on_device(): call(functools.partial(depth_kernel, turn, layers), [shape((columns, toke...  9.06 us
    all_to_all x1, blocking collectives, on_device(): lax.all_to_all(depth_grads, 'dp', 0, 0, axis_index_groups=groups, tiled=T...  8.77 us
    all_to_all x1, blocking collectives, on_device(): lax.all_to_all(jnp.broadcast_to(products[None], (4, columns, tokens)), 't...  7.99 us
  transfers between devices with their start and end apart: 22, of which 7 were waited for; matrix products, arithmetic and copies ran while one was open for 1% of the time, Pallas kernels for 15%

profile of v5, /device:TPU:98, one launch (start us, length us, event | category | flops | bytes accessed | tf_op | source)
XLA Modules:
  0.0 183.5 jit_solution(15955958757301686858)
XLA Ops:
  0.6 5.2 %collective-permute-start = (bf16[128,1536]{1,0:T(8,128)(2,1)}, bf16[128,1536]{1,0:T(8,128)(2,1)}, u32[]{:S(2)}, u32[]{:S(2)}) collective-permute-start(bf16[128,1536]{1,0:T(8,128)(2,1)} %bitcast.47), channel_id=1, source_target_pairs={{0,64},{8,72},{16,80},{24,88},{32,96},{40,104},{48,112},{56,120},{... | collective-permute-start | bytes 1179656 | tf_op jit(solution)/shard_map/ppermute | solution.py:192
  5.8 1.4 collective-permute-start.1
  7.2 1.0 copy-done.1
  8.2 1.1 copy-done.3
  10.4 12.1 %all_to_all.25.parts_ref = bf16[4,128,384]{2,1,0:T(8,128)(2,1)S(1)} all-to-all(bf16[4,128,384]{2,1,0:T(8,128)(2,1)S(1)} %get-tuple-element.38), channel_id=1, replica_groups=mesh['pipe'=8,'dp'=16,'tensor'=4] {'tensor'}, dimensions={0} | all-to-all | bytes 786432 | tf_op jit(solution)/shard_map/all_to_all | solution.py:206
  23.2 3.8 %collective-permute-start.2 = (bf16[128,1536]{1,0:T(8,128)(2,1)}, bf16[128,1536]{1,0:T(8,128)(2,1)S(1)}, u32[]{:S(2)}, u32[]{:S(2)}) collective-permute-start(bf16[128,1536]{1,0:T(8,128)(2,1)} %collective-permute-done.even_ref), channel_id=1, source_target_pairs={{64,128},{72,136},{80,144},{88,152},{96,160},{104,168},{112,176},{... | collective-permute-start | bytes 1179656 | tf_op jit(solution)/shard_map/ppermute | solution.py:192
  27.2 1.1 shard_map.78.before_ref
  28.4 1.8 shard_map.79.before_ref
  30.5 1.1 copy-done.9
  33.7 1.1 shard_map.80.before_ref
  34.8 4.8 %all-to-all-start.1 = ((bf16[8,704,128]{2,1,0:T(8,128)(2,1)}), bf16[8,704,128]{2,1,0:T(8,128)(2,1)S(1)}, u32[]{:S(2)}, u32[]{:S(2)}) async-start(bf16[8,704,128]{2,1,0:T(8,128)(2,1)} %copy-done.9), calls=%async_computation.1 | async-start | bytes 2883584 | tf_op jit(solution)/shard_map/all_to_all | solution.py:257
  39.7 1.0 copy-done.8
  42.9 5.0 %collective-permute-start.4 = (bf16[128,1536]{1,0:T(8,128)(2,1)S(1)}, bf16[128,1536]{1,0:T(8,128)(2,1)S(1)}, u32[]{:S(2)}, u32[]{:S(2)}) collective-permute-start(bf16[128,1536]{1,0:T(8,128)(2,1)S(1)} %shard_map.81), channel_id=1, source_target_pairs={{128,192},{136,200},{144,208},{152,216},{160,224},{168,232},{176,2... | collective-permute-start | bytes 1179656 | tf_op jit(solution)/shard_map/ppermute | solution.py:192
  48.0 1.0 shard_map.85
  49.7 5.3 %collective-permute-done.4.even_ref.held_ref = bf16[128,1536]{1,0:T(8,128)(2,1)S(1)} collective-permute-done((bf16[128,1536]{1,0:T(8,128)(2,1)S(1)}, bf16[128,1536]{1,0:T(8,128)(2,1)S(1)}, u32[]{:S(2)}, u32[]{:S(2)}) %collective-permute-start.4) | collective-permute-done | bytes 393248 | tf_op jit(solution)/shard_map/ppermute | solution.py:192
  55.5 5.6 %collective-permute-start.6 = (bf16[128,1536]{1,0:T(8,128)(2,1)S(1)}, bf16[128,1536]{1,0:T(8,128)(2,1)S(1)}, u32[]{:S(2)}, u32[]{:S(2)}) collective-permute-start(bf16[128,1536]{1,0:T(8,128)(2,1)S(1)} %shard_map.84), channel_id=1, source_target_pairs={{192,256},{200,264},{208,272},{216,280},{224,288},{232,296},{240,3... | collective-permute-start | bytes 1179656 | tf_op jit(solution)/shard_map/ppermute | solution.py:192
  61.2 1.1 shard_map.83.before_ref
  62.3 1.7 shard_map.88
  64.0 1.4 collective-permute-start.9
  65.5 1.7 collective-permute-done.6.even_ref.held_ref
  67.2 1.3 shard_map.87
  68.5 1.4 collective-permute-start.8
  69.9 1.1 shard_map.86.before_ref
  71.1 1.4 shard_map.91
  72.5 1.3 collective-permute-start.11
  73.8 1.0 shard_map.90
  75.6 1.7 shard_map.89.before_ref
  77.3 20.2 %collective-permute-done.11.odd_ref.held_ref = bf16[128,1536]{1,0:T(8,128)(2,1)S(1)} collective-permute-done((bf16[128,1536]{1,0:T(8,128)(2,1)S(1)}, bf16[128,1536]{1,0:T(8,128)(2,1)S(1)}, u32[]{:S(2)}, u32[]{:S(2)}) %collective-permute-start.11) | collective-permute-done | bytes 393248 | tf_op jit(solution)/shard_map/ppermute | solution.py:192
  97.5 1.0 shard_map.94
  98.5 1.9 %collective-permute-start.13 = (bf16[128,1536]{1,0:T(8,128)(2,1)S(1)}, bf16[128,1536]{1,0:T(8,128)(2,1)S(1)}, u32[]{:S(2)}, u32[]{:S(2)}) collective-permute-start(bf16[128,1536]{1,0:T(8,128)(2,1)S(1)} %shard_map.94), channel_id=1, source_target_pairs={{388,452},{396,460},{404,468},{412,476},{420,484},{428,492},{436,5... | collective-permute-start | bytes 1179656 | tf_op jit(solution)/shard_map/ppermute | solution.py:192
  101.7 1.1 shard_map.92.before_ref
  102.8 9.8 %collective-permute-done.13.odd_ref.held_ref = bf16[128,1536]{1,0:T(8,128)(2,1)S(1)} collective-permute-done((bf16[128,1536]{1,0:T(8,128)(2,1)S(1)}, bf16[128,1536]{1,0:T(8,128)(2,1)S(1)}, u32[]{:S(2)}, u32[]{:S(2)}) %collective-permute-start.13) | collective-permute-done | bytes 393248 | tf_op jit(solution)/shard_map/ppermute | solution.py:192
  113.6 1.9 %collective-permute-start.15 = (bf16[128,1536]{1,0:T(8,128)(2,1)S(1)}, bf16[128,1536]{1,0:T(8,128)(2,1)S(1)}, u32[]{:S(2)}, u32[]{:S(2)}) collective-permute-start(bf16[128,1536]{1,0:T(8,128)(2,1)S(1)} %shard_map.99), channel_id=1, source_target_pairs={{128,64},{136,72},{144,80},{152,88},{160,96},{168,104},{176,112},{... | collective-permute-start | bytes 1179656 | tf_op jit(solution)/shard_map/ppermute | solution.py:192
  117.1 1.1 shard_map.95
  118.3 8.0 %all_to_all.26.parts_ref = f32[4,32,128]{2,1,0:T(8,128)S(1)} all-to-all(f32[4,32,128]{2,1,0:T(8,128)S(1)} %broadcast_in_dim.8), channel_id=1, replica_groups=mesh['pipe'=8,'dp'=16,'tensor'=4] {'tensor'}, dimensions={0} | all-to-all | bytes 131072 | tf_op jit(solution)/shard_map/all_to_all | solution.py:262
  126.3 8.8 %all_to_all.27.depth_ref = bf16[8,32,128]{2,1,0:T(8,128)(2,1)S(1)} all-to-all(bf16[8,32,128]{2,1,0:T(8,128)(2,1)S(1)} %shard_map.96.depth_ref), channel_id=1, replica_groups={{0,4,16,20,32,36,48,52},{8,12,24,28,40,44,56,60},{1,5,17,21,33,37,49,53..., dimensions={0} | all-to-all | bytes 131072 | tf_op jit(solution)/shard_map/all_to_all | solution.py:264
  136.7 7.5 %collective-permute-start.16 = (bf16[224,256]{1,0:T(8,128)(2,1)S(1)}, bf16[224,256]{1,0:T(8,128)(2,1)S(1)}, u32[]{:S(2)}, u32[]{:S(2)}) collective-permute-start(bf16[224,256]{1,0:T(8,128)(2,1)S(1)} %shard_map.97), channel_id=1, source_target_pairs={{0,8},{4,12},{8,0},{12,4},{16,24},{20,28},{24,16},{28,20},{32,40},... | collective-permute-start | bytes 344072 | tf_op jit(solution)/shard_map/ppermute | solution.py:273
  144.2 11.4 %collective-permute-done.16 = bf16[224,256]{1,0:T(8,128)(2,1)S(1)} collective-permute-done((bf16[224,256]{1,0:T(8,128)(2,1)S(1)}, bf16[224,256]{1,0:T(8,128)(2,1)S(1)}, u32[]{:S(2)}, u32[]{:S(2)}) %collective-permute-start.16) | collective-permute-done | bytes 114720 | tf_op jit(solution)/shard_map/ppermute | solution.py:273
  156.5 5.5 %all-to-all-start.4 = ((bf16[4,192,256]{2,1,0:T(8,128)(2,1)}), bf16[4,192,256]{2,1,0:T(8,128)(2,1)}, u32[]{:S(2)}, u32[]{:S(2)}) async-start(bf16[4,192,256]{2,1,0:T(8,128)(2,1)} %broadcast_in_dim.9), calls=%async_computation.4 | async-start | bytes 786432 | tf_op jit(solution)/shard_map/all_to_all | solution.py:281
  163.7 1.7 shard_map.101
  165.5 2.0 %collective-permute-start.19 = (bf16[128,1536]{1,0:T(8,128)(2,1)}, bf16[128,1536]{1,0:T(8,128)(2,1)}, u32[]{:S(2)}, u32[]{:S(2)}) collective-permute-start(bf16[128,1536]{1,0:T(8,128)(2,1)} %shard_map.101), channel_id=1, source_target_pairs={{64,0},{72,8},{80,16},{88,24},{96,32},{104,40},{112,48},{120,56},{... | collective-permute-start | bytes 1179656 | tf_op jit(solution)/shard_map/ppermute | solution.py:192
  167.5 1.3 shard_map.100
  169.5 1.9 %collective-permute-start.17 = (bf16[4,192,256]{2,1,0:T(8,128)(2,1)}, bf16[4,192,256]{2,1,0:T(8,128)(2,1)S(1)}, u32[]{:S(2)}, u32[]{:S(2)}) collective-permute-start(bf16[4,192,256]{2,1,0:T(8,128)(2,1)} %all-to-all-done.4), channel_id=1, source_target_pairs={{0,4},{4,0},{8,12},{12,8},{16,20},{20,16},{24,28},{28,24},{32,36},... | collective-permute-start | bytes 1179656 | tf_op jit(solution)/shard_map/ppermute | solution.py:282
  171.9 1.4 fusion.1
  173.3 5.7 %collective-permute-done.19.odd_ref = bf16[128,1536]{1,0:T(8,128)(2,1)} collective-permute-done((bf16[128,1536]{1,0:T(8,128)(2,1)}, bf16[128,1536]{1,0:T(8,128)(2,1)}, u32[]{:S(2)}, u32[]{:S(2)}) %collective-permute-start.19) | collective-permute-done | bytes 393248 | tf_op jit(solution)/shard_map/ppermute | solution.py:192
  179.0 2.2 %shard_map.103 = bf16[128,1536]{1,0:T(8,128)(2,1)} custom-call(s32[2]{0:T(128)S(1)} %pad_add_fusion.place_ref, bf16[128,1536]{1,0:T(8,128)(2,1)S(1)} %collective-permute-done.18.even_ref, bf16[128,1536]{1,0:T(8,128)(2,1)} %collective-permute-done.19.odd_ref, bf16[4,128,1536]{2,1,0:T(8,128)(2,1)S(1)} %bitcast.46, f32[128,32]{1,0:T(8,128)S(1)} %get-tuple-element.64.mixing_ref, ...), custom_call_target="tpu_custom_call" | custom-call | flops 1572864 | bytes 3145728 | tf_op jit(solution)/shard_map/pallas_call | solution.py:293
  181.2 1.1 select_bitcast_fusion.1
  182.2 1.3 convert_multiply_fusion
  (103 shorter events, 17.6 us)
Async XLA Ops:
  0.6 26.6 %copy-start = (bf16[4,1,128,1536]{3,2,1,0:T(8,128)(2,1)S(1)}, bf16[4,1,128,1536]{3,2,1,0:T(8,128)(2,1)}, u32[]{:S(2)}) copy-start(bf16[4,1,128,1536]{3,2,1,0:T(8,128)(2,1)} %param.6) | copy-start | bytes 4718596
  0.6 21.8 %collective-permute-start = (bf16[128,1536]{1,0:T(8,128)(2,1)}, bf16[128,1536]{1,0:T(8,128)(2,1)}, u32[]{:S(2)}, u32[]{:S(2)}) collective-permute-start(bf16[128,1536]{1,0:T(8,128)(2,1)} %bitcast.47), channel_id=1, source_target_pairs={{0,64},{8,72},{16,80},{24,88},{32,96},{40,104},{48,112},{56,120},{... | collective-permute-start | bytes 1179656 | tf_op jit(solution)/shard_map/ppermute | solution.py:192
  5.8 16.6 %collective-permute-start.1 = (bf16[128,1536]{1,0:T(8,128)(2,1)}, bf16[128,1536]{1,0:T(8,128)(2,1)}, u32[]{:S(2)}, u32[]{:S(2)}) collective-permute-start(bf16[128,1536]{1,0:T(8,128)(2,1)} %bitcast.48), channel_id=1, source_target_pairs={{4,68},{12,76},{20,84},{28,92},{36,100},{44,108},{52,116},{60,124}... | collective-permute-start | bytes 1179656 | tf_op jit(solution)/shard_map/ppermute | solution.py:192
  8.2 1.1 copy-start.3
  10.1 16.9 %copy-start.26 = (bf16[1,256,32]{1,2,0:T(8,128)(2,1)S(1)}, bf16[1,256,32]{1,2,0:T(8,128)(2,1)}, u32[]{:S(2)}) copy-start(bf16[1,256,32]{1,2,0:T(8,128)(2,1)} %param.9) | copy-start | bytes 49156
  10.1 17.2 %copy-start.2 = (bf16[1,128,1536]{2,1,0:T(8,128)(2,1)S(1)}, bf16[1,128,1536]{2,1,0:T(8,128)(2,1)}, u32[]{:S(2)}) copy-start(bf16[1,128,1536]{2,1,0:T(8,128)(2,1)} %param.5) | copy-start | bytes 1179652
  10.4 12.1 %copy-start.12 = (bf16[1536,128]{1,0:T(8,128)(2,1)}, bf16[1536,128]{1,0:T(8,128)(2,1)S(1)}, u32[]{:S(2)}) copy-start(bf16[1536,128]{1,0:T(8,128)(2,1)S(1)} %get-tuple-element.40.scaled_ref) | copy-start | bytes 1179652
  22.5 10.4 %collective-permute-start.3 = (bf16[128,1536]{1,0:T(8,128)(2,1)}, bf16[128,1536]{1,0:T(8,128)(2,1)S(1)}, u32[]{:S(2)}, u32[]{:S(2)}) collective-permute-start(bf16[128,1536]{1,0:T(8,128)(2,1)} %collective-permute-done.1.odd_ref), channel_id=1, source_target_pairs={{68,132},{76,140},{84,148},{92,156},{100,164},{108,172},{116,180},... | collective-permute-start | bytes 1179656 | tf_op jit(solution)/shard_map/ppermute | solution.py:192
  23.2 10.5 %collective-permute-start.2 = (bf16[128,1536]{1,0:T(8,128)(2,1)}, bf16[128,1536]{1,0:T(8,128)(2,1)S(1)}, u32[]{:S(2)}, u32[]{:S(2)}) collective-permute-start(bf16[128,1536]{1,0:T(8,128)(2,1)} %collective-permute-done.even_ref), channel_id=1, source_target_pairs={{64,128},{72,136},{80,144},{88,152},{96,160},{104,168},{112,176},{... | collective-permute-start | bytes 1179656 | tf_op jit(solution)/shard_map/ppermute | solution.py:192
  27.1 3.0 %copy-start.10 = (bf16[256,32]{1,0:T(8,128)(2,1)}, bf16[256,32]{1,0:T(8,128)(2,1)S(1)}, u32[]{:S(2)}) copy-start(bf16[256,32]{1,0:T(8,128)(2,1)S(1)} %copy.11.weight_ref) | copy-start | bytes 49156
  28.3 1.8 copy-start.13
  30.5 1.1 copy-start.9
  32.9 1.9 %copy-start.22 = (f32[128,128]{1,0:T(8,128)}, f32[128,128]{1,0:T(8,128)S(1)}, u32[]{:S(2)}) copy-start(f32[128,128]{1,0:T(8,128)S(1)} %get-tuple-element.68.factor_ref) | copy-start | bytes 196612
  32.9 1.9 %copy-start.7 = (bf16[128,1536]{1,0:T(8,128)(2,1)}, bf16[128,1536]{1,0:T(8,128)(2,1)S(1)}, u32[]{:S(2)}) copy-start(bf16[128,1536]{1,0:T(8,128)(2,1)S(1)} %collective-permute-done.3.odd_ref.held_ref) | copy-start | bytes 1179652
  33.7 1.2 copy-start.5
  34.8 36.3 %all-to-all-start.1 = ((bf16[8,704,128]{2,1,0:T(8,128)(2,1)}), bf16[8,704,128]{2,1,0:T(8,128)(2,1)S(1)}, u32[]{:S(2)}, u32[]{:S(2)}) async-start(bf16[8,704,128]{2,1,0:T(8,128)(2,1)} %copy-done.9), calls=%async_computation.1 | async-start | bytes 2883584 | tf_op jit(solution)/shard_map/all_to_all | solution.py:257
  39.7 1.0 copy-start.8
  40.7 1.7 copy-start.6
  41.6 6.3 %collective-permute-start.5 = (bf16[128,1536]{1,0:T(8,128)(2,1)S(1)}, bf16[128,1536]{1,0:T(8,128)(2,1)S(1)}, u32[]{:S(2)}, u32[]{:S(2)}) collective-permute-start(bf16[128,1536]{1,0:T(8,128)(2,1)S(1)} %shard_map.82), channel_id=1, source_target_pairs={{132,196},{140,204},{148,212},{156,220},{164,228},{172,236},{180,2... | collective-permute-start | bytes 1179656 | tf_op jit(solution)/shard_map/ppermute | solution.py:192
  42.9 12.0 %collective-permute-start.4 = (bf16[128,1536]{1,0:T(8,128)(2,1)S(1)}, bf16[128,1536]{1,0:T(8,128)(2,1)S(1)}, u32[]{:S(2)}, u32[]{:S(2)}) collective-permute-start(bf16[128,1536]{1,0:T(8,128)(2,1)S(1)} %shard_map.81), channel_id=1, source_target_pairs={{128,192},{136,200},{144,208},{152,216},{160,224},{168,232},{176,2... | collective-permute-start | bytes 1179656 | tf_op jit(solution)/shard_map/ppermute | solution.py:192
  49.0 13.3 %collective-permute-start.7 = (bf16[128,1536]{1,0:T(8,128)(2,1)S(1)}, bf16[128,1536]{1,0:T(8,128)(2,1)S(1)}, u32[]{:S(2)}, u32[]{:S(2)}) collective-permute-start(bf16[128,1536]{1,0:T(8,128)(2,1)S(1)} %shard_map.85), channel_id=1, source_target_pairs={{196,260},{204,268},{212,276},{220,284},{228,292},{236,300},{244,3... | collective-permute-start | bytes 1179656 | tf_op jit(solution)/shard_map/ppermute | solution.py:192
  55.5 11.7 %collective-permute-start.6 = (bf16[128,1536]{1,0:T(8,128)(2,1)S(1)}, bf16[128,1536]{1,0:T(8,128)(2,1)S(1)}, u32[]{:S(2)}, u32[]{:S(2)}) collective-permute-start(bf16[128,1536]{1,0:T(8,128)(2,1)S(1)} %shard_map.84), channel_id=1, source_target_pairs={{192,256},{200,264},{208,272},{216,280},{224,288},{232,296},{240,3... | collective-permute-start | bytes 1179656 | tf_op jit(solution)/shard_map/ppermute | solution.py:192
  64.0 7.0 %collective-permute-start.9 = (bf16[128,1536]{1,0:T(8,128)(2,1)}, bf16[128,1536]{1,0:T(8,128)(2,1)}, u32[]{:S(2)}, u32[]{:S(2)}) collective-permute-start(bf16[128,1536]{1,0:T(8,128)(2,1)} %shard_map.88), channel_id=1, source_target_pairs={{260,324},{268,332},{276,340},{284,348},{292,356},{300,364},{308,3... | collective-permute-start | bytes 1179656 | tf_op jit(solution)/shard_map/ppermute | solution.py:192
  68.5 5.3 %collective-permute-start.8 = (bf16[128,1536]{1,0:T(8,128)(2,1)}, bf16[128,1536]{1,0:T(8,128)(2,1)}, u32[]{:S(2)}, u32[]{:S(2)}) collective-permute-start(bf16[128,1536]{1,0:T(8,128)(2,1)} %shard_map.87), channel_id=1, source_target_pairs={{256,320},{264,328},{272,336},{280,344},{288,352},{296,360},{304,3... | collective-permute-start | bytes 1179656 | tf_op jit(solution)/shard_map/ppermute | solution.py:192
  72.5 25.0 %collective-permute-start.11 = (bf16[128,1536]{1,0:T(8,128)(2,1)S(1)}, bf16[128,1536]{1,0:T(8,128)(2,1)S(1)}, u32[]{:S(2)}, u32[]{:S(2)}) collective-permute-start(bf16[128,1536]{1,0:T(8,128)(2,1)S(1)} %shard_map.91), channel_id=1, source_target_pairs={{324,388},{332,396},{340,404},{348,412},{356,420},{364,428},{372,4... | collective-permute-start | bytes 1179656 | tf_op jit(solution)/shard_map/ppermute | solution.py:192
  74.9 25.5 %collective-permute-start.10 = (bf16[128,1536]{1,0:T(8,128)(2,1)S(1)}, bf16[128,1536]{1,0:T(8,128)(2,1)S(1)}, u32[]{:S(2)}, u32[]{:S(2)}) collective-permute-start(bf16[128,1536]{1,0:T(8,128)(2,1)S(1)} %shard_map.90), channel_id=1, source_target_pairs={{320,384},{328,392},{336,400},{344,408},{352,416},{360,424},{368,4... | collective-permute-start | bytes 1179656 | tf_op jit(solution)/shard_map/ppermute | solution.py:192
  98.5 14.1 %collective-permute-start.13 = (bf16[128,1536]{1,0:T(8,128)(2,1)S(1)}, bf16[128,1536]{1,0:T(8,128)(2,1)S(1)}, u32[]{:S(2)}, u32[]{:S(2)}) collective-permute-start(bf16[128,1536]{1,0:T(8,128)(2,1)S(1)} %shard_map.94), channel_id=1, source_target_pairs={{388,452},{396,460},{404,468},{412,476},{420,484},{428,492},{436,5... | collective-permute-start | bytes 1179656 | tf_op jit(solution)/shard_map/ppermute | solution.py:192
  101.0 14.5 %collective-permute-start.12 = (bf16[128,1536]{1,0:T(8,128)(2,1)S(1)}, bf16[128,1536]{1,0:T(8,128)(2,1)S(1)}, u32[]{:S(2)}, u32[]{:S(2)}) collective-permute-start(bf16[128,1536]{1,0:T(8,128)(2,1)S(1)} %shard_map.93), channel_id=1, source_target_pairs={{384,448},{392,456},{400,464},{408,472},{416,480},{424,488},{432,4... | collective-permute-start | bytes 1179656 | tf_op jit(solution)/shard_map/ppermute | solution.py:192
  113.6 22.4 %collective-permute-start.15 = (bf16[128,1536]{1,0:T(8,128)(2,1)S(1)}, bf16[128,1536]{1,0:T(8,128)(2,1)S(1)}, u32[]{:S(2)}, u32[]{:S(2)}) collective-permute-start(bf16[128,1536]{1,0:T(8,128)(2,1)S(1)} %shard_map.99), channel_id=1, source_target_pairs={{128,64},{136,72},{144,80},{152,88},{160,96},{168,104},{176,112},{... | collective-permute-start | bytes 1179656 | tf_op jit(solution)/shard_map/ppermute | solution.py:192
  116.3 18.8 %copy-start.11 = (bf16[256,32]{1,0:T(8,128)(2,1)S(1)}, bf16[256,32]{1,0:T(8,128)(2,1)}, u32[]{:S(2)}) copy-start(bf16[256,32]{1,0:T(8,128)(2,1)} %copy-done.10) | copy-start | bytes 49156
  116.3 19.7 %collective-permute-start.14 = (bf16[128,1536]{1,0:T(8,128)(2,1)S(1)}, bf16[128,1536]{1,0:T(8,128)(2,1)S(1)}, u32[]{:S(2)}, u32[]{:S(2)}) collective-permute-start(bf16[128,1536]{1,0:T(8,128)(2,1)S(1)} %shard_map.98), channel_id=1, source_target_pairs={{132,68},{140,76},{148,84},{156,92},{164,100},{172,108},{180,116},... | collective-permute-start | bytes 1179656 | tf_op jit(solution)/shard_map/ppermute | solution.py:192
  135.0 27.0 %copy-start.29 = (bf16[1,1536]{1,0:T(2,128)(2,1)S(1)}, bf16[1,1536]{1,0:T(2,128)(2,1)}, u32[]{:S(2)}) copy-start(bf16[1,1536]{1,0:T(2,128)(2,1)} %gain_ref.1) | copy-start | bytes 9220
  135.9 26.8 %copy-start.19 = (f32[128,256]{1,0:T(8,128)S(1)}, f32[128,256]{1,0:T(8,128)}, u32[]{:S(2)}) copy-start(f32[128,256]{1,0:T(8,128)} %copy-done.18) | copy-start | bytes 393220
  135.9 26.8 %copy-start.21 = (f32[128,256]{1,0:T(8,128)S(1)}, f32[128,256]{1,0:T(8,128)}, u32[]{:S(2)}) copy-start(f32[128,256]{1,0:T(8,128)} %copy-done.20) | copy-start | bytes 393220
  135.9 26.8 %copy-start.23 = (f32[128,128]{1,0:T(8,128)S(1)}, f32[128,128]{1,0:T(8,128)}, u32[]{:S(2)}) copy-start(f32[128,128]{1,0:T(8,128)} %copy-done.22) | copy-start | bytes 196612
  135.9 26.7 %copy-start.27 = (bf16[1,256,32]{1,2,0:T(8,128)(2,1)S(1)}, bf16[1,256,32]{1,2,0:T(8,128)(2,1)}, u32[]{:S(2)}) copy-start(bf16[1,256,32]{1,2,0:T(8,128)(2,1)} %param.9) | copy-start | bytes 49156
  136.0 19.7 %copy-start.14 = (bf16[128,1536]{1,0:T(8,128)(2,1)}, bf16[128,1536]{1,0:T(8,128)(2,1)S(1)}, u32[]{:S(2)}) copy-start(bf16[128,1536]{1,0:T(8,128)(2,1)S(1)} %collective-permute-done.15.held_ref) | copy-start | bytes 1179652
  136.7 18.9 %collective-permute-start.16 = (bf16[224,256]{1,0:T(8,128)(2,1)S(1)}, bf16[224,256]{1,0:T(8,128)(2,1)S(1)}, u32[]{:S(2)}, u32[]{:S(2)}) collective-permute-start(bf16[224,256]{1,0:T(8,128)(2,1)S(1)} %shard_map.97), channel_id=1, source_target_pairs={{0,8},{4,12},{8,0},{12,4},{16,24},{20,28},{24,16},{28,20},{32,40},... | collective-permute-start | bytes 344072 | tf_op jit(solution)/shard_map/ppermute | solution.py:273
  155.7 7.0 %copy-start.30 = (f32[224,256]{1,0:T(8,128)}, f32[224,256]{1,0:T(8,128)S(1)}, u32[]{:S(2)}) copy-start(f32[224,256]{1,0:T(8,128)S(1)} %convert_add_fusion) | copy-start | bytes 688132
  155.7 8.0 %copy-start.15 = (bf16[128,1536]{1,0:T(8,128)(2,1)S(1)}, bf16[128,1536]{1,0:T(8,128)(2,1)}, u32[]{:S(2)}) copy-start(bf16[128,1536]{1,0:T(8,128)(2,1)} %copy-done.14) | copy-start | bytes 1179652
  156.5 13.0 %all-to-all-start.4 = ((bf16[4,192,256]{2,1,0:T(8,128)(2,1)}), bf16[4,192,256]{2,1,0:T(8,128)(2,1)}, u32[]{:S(2)}, u32[]{:S(2)}) async-start(bf16[4,192,256]{2,1,0:T(8,128)(2,1)} %broadcast_in_dim.9), calls=%async_computation.4 | async-start | bytes 786432 | tf_op jit(solution)/shard_map/all_to_all | solution.py:281
  162.1 5.5 %copy-start.17 = (bf16[128,1536]{1,0:T(8,128)(2,1)S(1)}, bf16[128,1536]{1,0:T(8,128)(2,1)}, u32[]{:S(2)}) copy-start(bf16[128,1536]{1,0:T(8,128)(2,1)} %copy-done.16) | copy-start | bytes 1179652
  165.5 6.0 %copy-start.4 = (bf16[1,1536,256]{2,1,0:T(8,128)(2,1)S(1)}, bf16[1,1536,256]{2,1,0:T(8,128)(2,1)}, u32[]{:S(2)}) copy-start(bf16[1,1536,256]{2,1,0:T(8,128)(2,1)} %param.8) | copy-start | bytes 2359300
  165.5 6.0 %copy-start.25 = (bf16[128,256]{1,0:T(8,128)(2,1)S(1)}, bf16[128,256]{1,0:T(8,128)(2,1)}, u32[]{:S(2)}) copy-start(bf16[128,256]{1,0:T(8,128)(2,1)} %copy-done.24) | copy-start | bytes 196612
  165.5 6.0 %copy-start.31 = (f32[1536]{0:T(1024)S(1)}, f32[1536]{0:T(1024)}, u32[]{:S(2)}) copy-start(f32[1536]{0:T(1024)} %convert_reduce_fusion) | copy-start | bytes 18436
  165.5 13.5 %collective-permute-start.19 = (bf16[128,1536]{1,0:T(8,128)(2,1)}, bf16[128,1536]{1,0:T(8,128)(2,1)}, u32[]{:S(2)}, u32[]{:S(2)}) collective-permute-start(bf16[128,1536]{1,0:T(8,128)(2,1)} %shard_map.101), channel_id=1, source_target_pairs={{64,0},{72,8},{80,16},{88,24},{96,32},{104,40},{112,48},{120,56},{... | collective-permute-start | bytes 1179656 | tf_op jit(solution)/shard_map/ppermute | solution.py:192
  168.9 10.1 %collective-permute-start.18 = (bf16[128,1536]{1,0:T(8,128)(2,1)}, bf16[128,1536]{1,0:T(8,128)(2,1)S(1)}, u32[]{:S(2)}, u32[]{:S(2)}) collective-permute-start(bf16[128,1536]{1,0:T(8,128)(2,1)} %shard_map.100), channel_id=1, source_target_pairs={{68,4},{76,12},{84,20},{92,28},{100,36},{108,44},{116,52},{124,60}... | collective-permute-start | bytes 1179656 | tf_op jit(solution)/shard_map/ppermute | solution.py:192
  169.5 11.6 %collective-permute-start.17 = (bf16[4,192,256]{2,1,0:T(8,128)(2,1)}, bf16[4,192,256]{2,1,0:T(8,128)(2,1)S(1)}, u32[]{:S(2)}, u32[]{:S(2)}) collective-permute-start(bf16[4,192,256]{2,1,0:T(8,128)(2,1)} %all-to-all-done.4), channel_id=1, source_target_pairs={{0,4},{4,0},{8,12},{12,8},{16,20},{20,16},{24,28},{28,24},{32,36},... | collective-permute-start | bytes 1179656 | tf_op jit(solution)/shard_map/ppermute | solution.py:282
  (6 other events, 4.4 us)

commit v6 on v4

--- a/solution.py
+++ b/solution.py
@@ -9,7 +9,7 @@
 
 D = 6144
 epsilon = 1e-06
-LAG = 2
+LAG = 3
 LANES = 512
 
 f32 = jnp.float32
@@ -252,10 +252,10 @@
             smem=1,
             count=5,
         )(place, *held, incoming, products)
-        if turn == LAG:
+        if turn == 2:
             payload, products = lax.optimization_barrier((payload, products))
             gathered = lax.all_to_all(payload, "dp", 0, 0, axis_index_groups=groups, tiled=True)
-        if turn == 2 * LAG:
+        if turn == LAG + 2:
             gathered, products = lax.optimization_barrier((gathered, products))
         mixing, products = lax.optimization_barrier((mixing, products))
 
@@ -276,10 +276,11 @@
     second_grads = total[chunk:].T / divisor
     spread = jnp.broadcast_to(total[None, :chunk].astype(bf16), (size // 4, chunk, hidden))
     along = [[x * 4 + rest for x in range(size // 4)] for rest in range(4)]
+    own = lax.all_to_all(spread, "dp", 0, 0, axis_index_groups=along, tiled=True)
     for turn in range(layers + 1, layers + LAG):
         chains = [advance(turn, chain) for chain in range(2)]
-    own = lax.all_to_all(spread, "dp", 0, 0, axis_index_groups=along, tiled=True)
-    own, *chains = lax.optimization_barrier((own, *chains))
+        if turn == layers + 1:
+            own, *chains = lax.optimization_barrier((own, *chains))
     far = lax.ppermute(own, "dp", [(i, i ^ 1) for i in range(size)])
     near = (index & 1) == 0
     summed = jnp.stack([jnp.where(near, own, far), jnp.where(near, far, own)], axis=1)

time: 170 us -> 176 us (1.035)
  the two profiles are of different devices: /device:TPU:97 before, /device:TPU:161 now
where the time goes in v6:
time: 176 us; the launch traced here: 175 us
  starting transfers between devices  63 us (36%)
  waiting for transfers between devices  39.7 us (23%)
  Pallas kernels  29.9 us (17%)
  blocking collectives  25.8 us (15%)
  local copies, waits for them, and re-layouts  9.62 us (5%)
  other arithmetic  4.45 us (3%)
    ppermute x20, waiting for transfers between devices, hop(): return lax.ppermute(array, ('pipe', 'dp'), pairs)  36.1 us
    ppermute x20, starting transfers between devices, hop(): return lax.ppermute(array, ('pipe', 'dp'), pairs)  35.5 us
    pallas_call x14, Pallas kernels, advance(): call(functools.partial(hop_kernel, turn, chain, layers), [shape((tokens,...  15.3 us
    all_to_all x1, blocking collectives, on_device(): packed = lax.all_to_all(packed, 'tensor', 0, 0, tiled=True)  10.5 us
    ppermute x1, starting transfers between devices, on_device(): far = lax.ppermute(own, 'dp', [(i, i ^ 1) for i in range(size)])  10.2 us
    pallas_call x7, Pallas kernels, on_device(): call(functools.partial(depth_kernel, turn, layers), [shape((columns, toke...  9.71 us
    unnamed x40, local copies, waits for them, and re-layouts  8.61 us
    all_to_all x1, blocking collectives, on_device(): lax.all_to_all(depth_grads, 'dp', 0, 0, axis_index_groups=groups, tiled=T...  8.22 us
  transfers between devices with their start and end apart: 24, of which 10 were waited for; matrix products, arithmetic and copies ran while one was open for 4% of the time, Pallas kernels for 16%

profile of v6, /device:TPU:161, one launch (start us, length us, event | category | flops | bytes accessed | tf_op | source)
XLA Modules:
  0.0 174.8 jit_solution(9256349129518110549)
XLA Ops:
  0.6 1.5 collective-permute-start
  2.2 3.5 %collective-permute-start.1 = (bf16[128,1536]{1,0:T(8,128)(2,1)}, bf16[128,1536]{1,0:T(8,128)(2,1)}, u32[]{:S(2)}, u32[]{:S(2)}) collective-permute-start(bf16[128,1536]{1,0:T(8,128)(2,1)} %bitcast.48), channel_id=1, source_target_pairs={{4,68},{12,76},{20,84},{28,92},{36,100},{44,108},{52,116},{60,124}... | collective-permute-start | bytes 1179656 | tf_op jit(solution)/shard_map/ppermute | solution.py:192
  6.7 1.1 copy-done.3
  8.9 10.5 %all_to_all.25.parts_ref = bf16[4,128,384]{2,1,0:T(8,128)(2,1)S(1)} all-to-all(bf16[4,128,384]{2,1,0:T(8,128)(2,1)S(1)} %get-tuple-element.39), channel_id=1, replica_groups=mesh['pipe'=8,'dp'=16,'tensor'=4] {'tensor'}, dimensions={0} | all-to-all | bytes 786432 | tf_op jit(solution)/shard_map/all_to_all | solution.py:206
  19.4 3.5 %collective-permute-start.3 = (bf16[128,1536]{1,0:T(8,128)(2,1)}, bf16[128,1536]{1,0:T(8,128)(2,1)}, u32[]{:S(2)}, u32[]{:S(2)}) collective-permute-start(bf16[128,1536]{1,0:T(8,128)(2,1)} %collective-permute-done.1.odd_ref), channel_id=1, source_target_pairs={{68,132},{76,140},{84,148},{92,156},{100,164},{108,172},{116,180},... | collective-permute-start | bytes 1179656 | tf_op jit(solution)/shard_map/ppermute | solution.py:192
  23.0 1.4 collective-permute-start.2
  24.6 1.1 shard_map.78.before_ref
  25.7 1.7 shard_map.79.before_ref
  30.9 7.0 %all-to-all-start.1 = ((bf16[8,704,128]{2,1,0:T(8,128)(2,1)}), bf16[8,704,128]{2,1,0:T(8,128)(2,1)S(1)}, u32[]{:S(2)}, u32[]{:S(2)}) async-start(bf16[8,704,128]{2,1,0:T(8,128)(2,1)} %copy-done.5), calls=%async_computation.1 | async-start | bytes 2883584 | tf_op jit(solution)/shard_map/all_to_all | solution.py:257
  37.9 1.9 %collective-permute-start.5 = (bf16[128,1536]{1,0:T(8,128)(2,1)}, bf16[128,1536]{1,0:T(8,128)(2,1)S(1)}, u32[]{:S(2)}, u32[]{:S(2)}) collective-permute-start(bf16[128,1536]{1,0:T(8,128)(2,1)} %collective-permute-done.3.odd_ref), channel_id=1, source_target_pairs={{132,196},{140,204},{148,212},{156,220},{164,228},{172,236},{180,2... | collective-permute-start | bytes 1179656 | tf_op jit(solution)/shard_map/ppermute | solution.py:192
  40.5 1.7 shard_map.80.before_ref
  42.2 7.7 %collective-permute-done.5.odd_ref.held_ref = bf16[128,1536]{1,0:T(8,128)(2,1)S(1)} collective-permute-done((bf16[128,1536]{1,0:T(8,128)(2,1)}, bf16[128,1536]{1,0:T(8,128)(2,1)S(1)}, u32[]{:S(2)}, u32[]{:S(2)}) %collective-permute-start.5) | collective-permute-done | bytes 393248 | tf_op jit(solution)/shard_map/ppermute | solution.py:192
  50.5 2.2 %collective-permute-start.7 = (bf16[128,1536]{1,0:T(8,128)(2,1)S(1)}, bf16[128,1536]{1,0:T(8,128)(2,1)S(1)}, u32[]{:S(2)}, u32[]{:S(2)}) collective-permute-start(bf16[128,1536]{1,0:T(8,128)(2,1)S(1)} %shard_map.83), channel_id=1, source_target_pairs={{196,260},{204,268},{212,276},{220,284},{228,292},{236,300},{244,3... | collective-permute-start | bytes 1179656 | tf_op jit(solution)/shard_map/ppermute | solution.py:192
  54.4 1.1 shard_map.81.before_ref
  55.6 5.8 %collective-permute-done.7.odd_ref.held_ref = bf16[128,1536]{1,0:T(8,128)(2,1)S(1)} collective-permute-done((bf16[128,1536]{1,0:T(8,128)(2,1)S(1)}, bf16[128,1536]{1,0:T(8,128)(2,1)S(1)}, u32[]{:S(2)}, u32[]{:S(2)}) %collective-permute-start.7) | collective-permute-done | bytes 393248 | tf_op jit(solution)/shard_map/ppermute | solution.py:192
  61.4 1.3 shard_map.86
  62.7 2.5 %collective-permute-start.9 = (bf16[128,1536]{1,0:T(8,128)(2,1)}, bf16[128,1536]{1,0:T(8,128)(2,1)}, u32[]{:S(2)}, u32[]{:S(2)}) collective-permute-start(bf16[128,1536]{1,0:T(8,128)(2,1)} %shard_map.86), channel_id=1, source_target_pairs={{260,324},{268,332},{276,340},{284,348},{292,356},{300,364},{308,3... | collective-permute-start | bytes 1179656 | tf_op jit(solution)/shard_map/ppermute | solution.py:192
  65.3 1.7 shard_map.85
  67.0 1.3 collective-permute-start.8
  68.3 1.1 shard_map.84.before_ref
  69.5 3.9 %collective-permute-done.9.odd_ref.held_ref = bf16[128,1536]{1,0:T(8,128)(2,1)} collective-permute-done((bf16[128,1536]{1,0:T(8,128)(2,1)}, bf16[128,1536]{1,0:T(8,128)(2,1)}, u32[]{:S(2)}, u32[]{:S(2)}) %collective-permute-start.9) | collective-permute-done | bytes 393248 | tf_op jit(solution)/shard_map/ppermute | solution.py:192
  74.4 2.6 %collective-permute-start.11 = (bf16[128,1536]{1,0:T(8,128)(2,1)S(1)}, bf16[128,1536]{1,0:T(8,128)(2,1)S(1)}, u32[]{:S(2)}, u32[]{:S(2)}) collective-permute-start(bf16[128,1536]{1,0:T(8,128)(2,1)S(1)} %shard_map.89), channel_id=1, source_target_pairs={{324,388},{332,396},{340,404},{348,412},{356,420},{364,428},{372,4... | collective-permute-start | bytes 1179656 | tf_op jit(solution)/shard_map/ppermute | solution.py:192
  77.0 1.4 shard_map.88
  78.5 1.9 %collective-permute-start.10 = (bf16[128,1536]{1,0:T(8,128)(2,1)S(1)}, bf16[128,1536]{1,0:T(8,128)(2,1)S(1)}, u32[]{:S(2)}, u32[]{:S(2)}) collective-permute-start(bf16[128,1536]{1,0:T(8,128)(2,1)S(1)} %shard_map.88), channel_id=1, source_target_pairs={{320,384},{328,392},{336,400},{344,408},{352,416},{360,424},{368,4... | collective-permute-start | bytes 1179656 | tf_op jit(solution)/shard_map/ppermute | solution.py:192
  80.4 1.7 shard_map.87.before_ref
  83.5 3.4 %collective-permute-done.10.even_ref.held_ref = bf16[128,1536]{1,0:T(8,128)(2,1)S(1)} collective-permute-done((bf16[128,1536]{1,0:T(8,128)(2,1)S(1)}, bf16[128,1536]{1,0:T(8,128)(2,1)S(1)}, u32[]{:S(2)}, u32[]{:S(2)}) %collective-permute-start.10) | collective-permute-done | bytes 393248 | tf_op jit(solution)/shard_map/ppermute | solution.py:192
  88.0 1.9 %collective-permute-start.12 = (bf16[128,1536]{1,0:T(8,128)(2,1)S(1)}, bf16[128,1536]{1,0:T(8,128)(2,1)S(1)}, u32[]{:S(2)}, u32[]{:S(2)}) collective-permute-start(bf16[128,1536]{1,0:T(8,128)(2,1)S(1)} %shard_map.91), channel_id=1, source_target_pairs={{384,448},{392,456},{400,464},{408,472},{416,480},{424,488},{432,4... | collective-permute-start | bytes 1179656 | tf_op jit(solution)/shard_map/ppermute | solution.py:192
  89.9 1.1 shard_map.90.before_ref
  92.3 7.0 %collective-permute-done.12.even_ref.held_ref = bf16[128,1536]{1,0:T(8,128)(2,1)S(1)} collective-permute-done((bf16[128,1536]{1,0:T(8,128)(2,1)S(1)}, bf16[128,1536]{1,0:T(8,128)(2,1)S(1)}, u32[]{:S(2)}, u32[]{:S(2)}) %collective-permute-start.12) | collective-permute-done | bytes 393248 | tf_op jit(solution)/shard_map/ppermute | solution.py:192
  100.3 2.1 %collective-permute-start.14 = (bf16[128,1536]{1,0:T(8,128)(2,1)S(1)}, bf16[128,1536]{1,0:T(8,128)(2,1)S(1)}, u32[]{:S(2)}, u32[]{:S(2)}) collective-permute-start(bf16[128,1536]{1,0:T(8,128)(2,1)S(1)} %shard_map.96), channel_id=1, source_target_pairs={{196,132},{204,140},{212,148},{220,156},{228,164},{236,172},{244,1... | collective-permute-start | bytes 1179656 | tf_op jit(solution)/shard_map/ppermute | solution.py:192
  102.3 1.1 shard_map.93
  103.5 7.0 %all_to_all.26.parts_ref = f32[4,32,128]{2,1,0:T(8,128)S(1)} all-to-all(f32[4,32,128]{2,1,0:T(8,128)S(1)} %broadcast_in_dim.8), channel_id=1, replica_groups=mesh['pipe'=8,'dp'=16,'tensor'=4] {'tensor'}, dimensions={0} | all-to-all | bytes 131072 | tf_op jit(solution)/shard_map/all_to_all | solution.py:262
  110.5 8.2 %all_to_all.27.depth_ref = bf16[8,32,128]{2,1,0:T(8,128)(2,1)S(1)} all-to-all(bf16[8,32,128]{2,1,0:T(8,128)(2,1)S(1)} %shard_map.94.depth_ref), channel_id=1, replica_groups={{0,4,16,20,32,36,48,52},{8,12,24,28,40,44,56,60},{1,5,17,21,33,37,49,53..., dimensions={0} | all-to-all | bytes 131072 | tf_op jit(solution)/shard_map/all_to_all | solution.py:264
  119.7 6.1 %collective-permute-start.16 = (bf16[224,256]{1,0:T(8,128)(2,1)S(1)}, bf16[224,256]{1,0:T(8,128)(2,1)S(1)}, u32[]{:S(2)}, u32[]{:S(2)}) collective-permute-start(bf16[224,256]{1,0:T(8,128)(2,1)S(1)} %shard_map.95), channel_id=1, source_target_pairs={{0,8},{4,12},{8,0},{12,4},{16,24},{20,28},{24,16},{28,20},{32,40},... | collective-permute-start | bytes 344072 | tf_op jit(solution)/shard_map/ppermute | solution.py:273
  125.8 1.3 shard_map.99
  127.8 1.7 shard_map.98
  129.5 3.0 %collective-permute-start.17 = (bf16[128,1536]{1,0:T(8,128)(2,1)}, bf16[128,1536]{1,0:T(8,128)(2,1)}, u32[]{:S(2)}, u32[]{:S(2)}) collective-permute-start(bf16[128,1536]{1,0:T(8,128)(2,1)} %shard_map.98), channel_id=1, source_target_pairs={{132,68},{140,76},{148,84},{156,92},{164,100},{172,108},{180,116},... | collective-permute-start | bytes 1179656 | tf_op jit(solution)/shard_map/ppermute | solution.py:192
  132.5 1.5 collective-permute-done.16
  135.5 4.1 %all-to-all-start.4 = ((bf16[4,192,256]{2,1,0:T(8,128)(2,1)}), bf16[4,192,256]{2,1,0:T(8,128)(2,1)}, u32[]{:S(2)}, u32[]{:S(2)}) async-start(bf16[4,192,256]{2,1,0:T(8,128)(2,1)} %broadcast_in_dim.9), calls=%async_computation.4 | async-start | bytes 786432 | tf_op jit(solution)/shard_map/all_to_all | solution.py:279
  143.9 2.1 %all-to-all-done.4 = bf16[4,192,256]{2,1,0:T(8,128)(2,1)} async-done(((bf16[4,192,256]{2,1,0:T(8,128)(2,1)}), bf16[4,192,256]{2,1,0:T(8,128)(2,1)}, u32[]{:S(2)}, u32[]{:S(2)}) %all-to-all-start.4) | async-done | bytes 393248 | tf_op jit(solution)/shard_map/all_to_all | solution.py:279
  146.0 10.2 %collective-permute-start.21 = (bf16[4,192,256]{2,1,0:T(8,128)(2,1)}, bf16[4,192,256]{2,1,0:T(8,128)(2,1)S(1)}, u32[]{:S(2)}, u32[]{:S(2)}) collective-permute-start(bf16[4,192,256]{2,1,0:T(8,128)(2,1)} %all-to-all-done.4), channel_id=1, source_target_pairs={{0,4},{4,0},{8,12},{12,8},{16,20},{20,16},{24,28},{28,24},{32,36},... | collective-permute-start | bytes 1179656 | tf_op jit(solution)/shard_map/ppermute | solution.py:284
  156.2 1.2 fusion.generated_ref
  157.4 1.4 fusion.1
  160.1 1.4 shard_map.100
  161.5 1.9 %collective-permute-start.19 = (bf16[128,1536]{1,0:T(8,128)(2,1)S(1)}, bf16[128,1536]{1,0:T(8,128)(2,1)S(1)}, u32[]{:S(2)}, u32[]{:S(2)}) collective-permute-start(bf16[128,1536]{1,0:T(8,128)(2,1)S(1)} %shard_map.100), channel_id=1, source_target_pairs={{68,4},{76,12},{84,20},{92,28},{100,36},{108,44},{116,52},{124,60}... | collective-permute-start | bytes 1179656 | tf_op jit(solution)/shard_map/ppermute | solution.py:192
  164.5 1.3 convert_multiply_fusion
  165.8 7.2 %collective-permute-done.19.even_ref = bf16[128,1536]{1,0:T(8,128)(2,1)S(1)} collective-permute-done((bf16[128,1536]{1,0:T(8,128)(2,1)S(1)}, bf16[128,1536]{1,0:T(8,128)(2,1)S(1)}, u32[]{:S(2)}, u32[]{:S(2)}) %collective-permute-start.19) | collective-permute-done | bytes 393248 | tf_op jit(solution)/shard_map/ppermute | solution.py:192
  173.0 1.8 %shard_map.103 = bf16[128,1536]{1,0:T(8,128)(2,1)} custom-call(s32[2]{0:T(128)S(1)} %pad_add_fusion.place_ref, bf16[128,1536]{1,0:T(8,128)(2,1)S(1)} %collective-permute-done.19.even_ref, bf16[128,1536]{1,0:T(8,128)(2,1)S(1)} %collective-permute-done.20.odd_ref, bf16[4,128,1536]{2,1,0:T(8,128)(2,1)S(1)} %bitcast.46, ...), custom_call_target="tpu_custom_call" | custom-call | flops 1572864 | bytes 3145728 | tf_op jit(solution)/shard_map/pallas_call | solution.py:299
  (83 shorter events, 23.8 us)
Async XLA Ops:
  0.6 24.0 %copy-start = (bf16[4,1,128,1536]{3,2,1,0:T(8,128)(2,1)S(1)}, bf16[4,1,128,1536]{3,2,1,0:T(8,128)(2,1)}, u32[]{:S(2)}) copy-start(bf16[4,1,128,1536]{3,2,1,0:T(8,128)(2,1)} %param.6) | copy-start | bytes 4718596
  0.6 18.8 %collective-permute-start = (bf16[128,1536]{1,0:T(8,128)(2,1)}, bf16[128,1536]{1,0:T(8,128)(2,1)}, u32[]{:S(2)}, u32[]{:S(2)}) collective-permute-start(bf16[128,1536]{1,0:T(8,128)(2,1)} %bitcast.47), channel_id=1, source_target_pairs={{0,64},{8,72},{16,80},{24,88},{32,96},{40,104},{48,112},{56,120},{... | collective-permute-start | bytes 1179656 | tf_op jit(solution)/shard_map/ppermute | solution.py:192
  2.2 17.2 %collective-permute-start.1 = (bf16[128,1536]{1,0:T(8,128)(2,1)}, bf16[128,1536]{1,0:T(8,128)(2,1)}, u32[]{:S(2)}, u32[]{:S(2)}) collective-permute-start(bf16[128,1536]{1,0:T(8,128)(2,1)} %bitcast.48), channel_id=1, source_target_pairs={{4,68},{12,76},{20,84},{28,92},{36,100},{44,108},{52,116},{60,124}... | collective-permute-start | bytes 1179656 | tf_op jit(solution)/shard_map/ppermute | solution.py:192
  5.7 1.0 copy-start.1
  6.7 1.1 copy-start.3
  7.9 0.7 copy-start.17
  8.6 15.9 %copy-start.15 = (bf16[1,256,32]{1,2,0:T(8,128)(2,1)S(1)}, bf16[1,256,32]{1,2,0:T(8,128)(2,1)}, u32[]{:S(2)}) copy-start(bf16[1,256,32]{1,2,0:T(8,128)(2,1)} %param.9) | copy-start | bytes 49156
  8.6 16.1 %copy-start.2 = (bf16[1,128,1536]{2,1,0:T(8,128)(2,1)S(1)}, bf16[1,128,1536]{2,1,0:T(8,128)(2,1)}, u32[]{:S(2)}) copy-start(bf16[1,128,1536]{2,1,0:T(8,128)(2,1)} %param.5) | copy-start | bytes 1179652
  19.4 18.5 %collective-permute-start.3 = (bf16[128,1536]{1,0:T(8,128)(2,1)}, bf16[128,1536]{1,0:T(8,128)(2,1)}, u32[]{:S(2)}, u32[]{:S(2)}) collective-permute-start(bf16[128,1536]{1,0:T(8,128)(2,1)} %collective-permute-done.1.odd_ref), channel_id=1, source_target_pairs={{68,132},{76,140},{84,148},{92,156},{100,164},{108,172},{116,180},... | collective-permute-start | bytes 1179656 | tf_op jit(solution)/shard_map/ppermute | solution.py:192
  23.0 16.8 %collective-permute-start.2 = (bf16[128,1536]{1,0:T(8,128)(2,1)}, bf16[128,1536]{1,0:T(8,128)(2,1)}, u32[]{:S(2)}, u32[]{:S(2)}) collective-permute-start(bf16[128,1536]{1,0:T(8,128)(2,1)} %collective-permute-done.even_ref), channel_id=1, source_target_pairs={{64,128},{72,136},{80,144},{88,152},{96,160},{104,168},{112,176},{... | collective-permute-start | bytes 1179656 | tf_op jit(solution)/shard_map/ppermute | solution.py:192
  24.5 2.9 %copy-start.6 = (bf16[256,32]{1,0:T(8,128)(2,1)}, bf16[256,32]{1,0:T(8,128)(2,1)S(1)}, u32[]{:S(2)}) copy-start(bf16[256,32]{1,0:T(8,128)(2,1)S(1)} %copy.11.weight_ref) | copy-start | bytes 49156
  27.8 1.1 copy-start.5
  28.9 0.6 copy-start.8
  29.6 0.6 copy-start.10
  30.2 0.6 copy-start.12
  30.9 38.6 %all-to-all-start.1 = ((bf16[8,704,128]{2,1,0:T(8,128)(2,1)}), bf16[8,704,128]{2,1,0:T(8,128)(2,1)S(1)}, u32[]{:S(2)}, u32[]{:S(2)}) async-start(bf16[8,704,128]{2,1,0:T(8,128)(2,1)} %copy-done.5), calls=%async_computation.1 | async-start | bytes 2883584 | tf_op jit(solution)/shard_map/all_to_all | solution.py:257
  37.9 12.0 %collective-permute-start.5 = (bf16[128,1536]{1,0:T(8,128)(2,1)}, bf16[128,1536]{1,0:T(8,128)(2,1)S(1)}, u32[]{:S(2)}, u32[]{:S(2)}) collective-permute-start(bf16[128,1536]{1,0:T(8,128)(2,1)} %collective-permute-done.3.odd_ref), channel_id=1, source_target_pairs={{132,196},{140,204},{148,212},{156,220},{164,228},{172,236},{180,2... | collective-permute-start | bytes 1179656 | tf_op jit(solution)/shard_map/ppermute | solution.py:192
  39.8 12.9 %collective-permute-start.4 = (bf16[128,1536]{1,0:T(8,128)(2,1)}, bf16[128,1536]{1,0:T(8,128)(2,1)S(1)}, u32[]{:S(2)}, u32[]{:S(2)}) collective-permute-start(bf16[128,1536]{1,0:T(8,128)(2,1)} %collective-permute-done.2.even_ref), channel_id=1, source_target_pairs={{128,192},{136,200},{144,208},{152,216},{160,224},{168,232},{176,2... | collective-permute-start | bytes 1179656 | tf_op jit(solution)/shard_map/ppermute | solution.py:192
  50.5 10.9 %collective-permute-start.7 = (bf16[128,1536]{1,0:T(8,128)(2,1)S(1)}, bf16[128,1536]{1,0:T(8,128)(2,1)S(1)}, u32[]{:S(2)}, u32[]{:S(2)}) collective-permute-start(bf16[128,1536]{1,0:T(8,128)(2,1)S(1)} %shard_map.83), channel_id=1, source_target_pairs={{196,260},{204,268},{212,276},{220,284},{228,292},{236,300},{244,3... | collective-permute-start | bytes 1179656 | tf_op jit(solution)/shard_map/ppermute | solution.py:192
  53.7 11.6 %collective-permute-start.6 = (bf16[128,1536]{1,0:T(8,128)(2,1)S(1)}, bf16[128,1536]{1,0:T(8,128)(2,1)S(1)}, u32[]{:S(2)}, u32[]{:S(2)}) collective-permute-start(bf16[128,1536]{1,0:T(8,128)(2,1)S(1)} %shard_map.82), channel_id=1, source_target_pairs={{192,256},{200,264},{208,272},{216,280},{224,288},{232,296},{240,3... | collective-permute-start | bytes 1179656 | tf_op jit(solution)/shard_map/ppermute | solution.py:192
  62.7 10.6 %collective-permute-start.9 = (bf16[128,1536]{1,0:T(8,128)(2,1)}, bf16[128,1536]{1,0:T(8,128)(2,1)}, u32[]{:S(2)}, u32[]{:S(2)}) collective-permute-start(bf16[128,1536]{1,0:T(8,128)(2,1)} %shard_map.86), channel_id=1, source_target_pairs={{260,324},{268,332},{276,340},{284,348},{292,356},{300,364},{308,3... | collective-permute-start | bytes 1179656 | tf_op jit(solution)/shard_map/ppermute | solution.py:192
  67.0 10.0 %collective-permute-start.8 = (bf16[128,1536]{1,0:T(8,128)(2,1)}, bf16[128,1536]{1,0:T(8,128)(2,1)}, u32[]{:S(2)}, u32[]{:S(2)}) collective-permute-start(bf16[128,1536]{1,0:T(8,128)(2,1)} %shard_map.85), channel_id=1, source_target_pairs={{256,320},{264,328},{272,336},{280,344},{288,352},{296,360},{304,3... | collective-permute-start | bytes 1179656 | tf_op jit(solution)/shard_map/ppermute | solution.py:192
  74.4 7.8 %collective-permute-start.11 = (bf16[128,1536]{1,0:T(8,128)(2,1)S(1)}, bf16[128,1536]{1,0:T(8,128)(2,1)S(1)}, u32[]{:S(2)}, u32[]{:S(2)}) collective-permute-start(bf16[128,1536]{1,0:T(8,128)(2,1)S(1)} %shard_map.89), channel_id=1, source_target_pairs={{324,388},{332,396},{340,404},{348,412},{356,420},{364,428},{372,4... | collective-permute-start | bytes 1179656 | tf_op jit(solution)/shard_map/ppermute | solution.py:192
  78.5 8.5 %collective-permute-start.10 = (bf16[128,1536]{1,0:T(8,128)(2,1)S(1)}, bf16[128,1536]{1,0:T(8,128)(2,1)S(1)}, u32[]{:S(2)}, u32[]{:S(2)}) collective-permute-start(bf16[128,1536]{1,0:T(8,128)(2,1)S(1)} %shard_map.88), channel_id=1, source_target_pairs={{320,384},{328,392},{336,400},{344,408},{352,416},{360,424},{368,4... | collective-permute-start | bytes 1179656 | tf_op jit(solution)/shard_map/ppermute | solution.py:192
  82.8 8.2 %collective-permute-start.13 = (bf16[128,1536]{1,0:T(8,128)(2,1)S(1)}, bf16[128,1536]{1,0:T(8,128)(2,1)S(1)}, u32[]{:S(2)}, u32[]{:S(2)}) collective-permute-start(bf16[128,1536]{1,0:T(8,128)(2,1)S(1)} %shard_map.92), channel_id=1, source_target_pairs={{388,452},{396,460},{404,468},{412,476},{420,484},{428,492},{436,5... | collective-permute-start | bytes 1179656 | tf_op jit(solution)/shard_map/ppermute | solution.py:192
  88.0 11.3 %collective-permute-start.12 = (bf16[128,1536]{1,0:T(8,128)(2,1)S(1)}, bf16[128,1536]{1,0:T(8,128)(2,1)S(1)}, u32[]{:S(2)}, u32[]{:S(2)}) collective-permute-start(bf16[128,1536]{1,0:T(8,128)(2,1)S(1)} %shard_map.91), channel_id=1, source_target_pairs={{384,448},{392,456},{400,464},{408,472},{416,480},{424,488},{432,4... | collective-permute-start | bytes 1179656 | tf_op jit(solution)/shard_map/ppermute | solution.py:192
  91.6 28.0 %collective-permute-start.15 = (bf16[128,1536]{1,0:T(8,128)(2,1)S(1)}, bf16[128,1536]{1,0:T(8,128)(2,1)S(1)}, u32[]{:S(2)}, u32[]{:S(2)}) collective-permute-start(bf16[128,1536]{1,0:T(8,128)(2,1)S(1)} %shard_map.97), channel_id=1, source_target_pairs={{192,128},{200,136},{208,144},{216,152},{224,160},{232,168},{240,1... | collective-permute-start | bytes 1179656 | tf_op jit(solution)/shard_map/ppermute | solution.py:192
  100.3 18.5 %copy-start.7 = (bf16[256,32]{1,0:T(8,128)(2,1)S(1)}, bf16[256,32]{1,0:T(8,128)(2,1)}, u32[]{:S(2)}) copy-start(bf16[256,32]{1,0:T(8,128)(2,1)} %copy-done.6) | copy-start | bytes 49156
  100.3 19.4 %collective-permute-start.14 = (bf16[128,1536]{1,0:T(8,128)(2,1)S(1)}, bf16[128,1536]{1,0:T(8,128)(2,1)S(1)}, u32[]{:S(2)}, u32[]{:S(2)}) collective-permute-start(bf16[128,1536]{1,0:T(8,128)(2,1)S(1)} %shard_map.96), channel_id=1, source_target_pairs={{196,132},{204,140},{212,148},{220,156},{228,164},{236,172},{244,1... | collective-permute-start | bytes 1179656 | tf_op jit(solution)/shard_map/ppermute | solution.py:192
  119.7 14.4 %collective-permute-start.16 = (bf16[224,256]{1,0:T(8,128)(2,1)S(1)}, bf16[224,256]{1,0:T(8,128)(2,1)S(1)}, u32[]{:S(2)}, u32[]{:S(2)}) collective-permute-start(bf16[224,256]{1,0:T(8,128)(2,1)S(1)} %shard_map.95), channel_id=1, source_target_pairs={{0,8},{4,12},{8,0},{12,4},{16,24},{20,28},{24,16},{28,20},{32,40},... | collective-permute-start | bytes 344072 | tf_op jit(solution)/shard_map/ppermute | solution.py:273
  127.1 15.3 %collective-permute-start.18 = (bf16[128,1536]{1,0:T(8,128)(2,1)}, bf16[128,1536]{1,0:T(8,128)(2,1)S(1)}, u32[]{:S(2)}, u32[]{:S(2)}) collective-permute-start(bf16[128,1536]{1,0:T(8,128)(2,1)} %shard_map.99), channel_id=1, source_target_pairs={{128,64},{136,72},{144,80},{152,88},{160,96},{168,104},{176,112},{... | collective-permute-start | bytes 1179656 | tf_op jit(solution)/shard_map/ppermute | solution.py:192
  129.5 10.1 %copy-start.18 = (bf16[1,1536]{1,0:T(2,128)(2,1)S(1)}, bf16[1,1536]{1,0:T(2,128)(2,1)}, u32[]{:S(2)}) copy-start(bf16[1,1536]{1,0:T(2,128)(2,1)} %gain_ref.1) | copy-start | bytes 9220
  129.5 10.8 %copy-start.9 = (f32[128,256]{1,0:T(8,128)S(1)}, f32[128,256]{1,0:T(8,128)}, u32[]{:S(2)}) copy-start(f32[128,256]{1,0:T(8,128)} %copy-done.8) | copy-start | bytes 393220
  129.5 10.8 %copy-start.11 = (f32[128,256]{1,0:T(8,128)S(1)}, f32[128,256]{1,0:T(8,128)}, u32[]{:S(2)}) copy-start(f32[128,256]{1,0:T(8,128)} %copy-done.10) | copy-start | bytes 393220
  129.5 26.6 %copy-start.4 = (bf16[1,1536,256]{2,1,0:T(8,128)(2,1)S(1)}, bf16[1,1536,256]{2,1,0:T(8,128)(2,1)}, u32[]{:S(2)}) copy-start(bf16[1,1536,256]{2,1,0:T(8,128)(2,1)} %param.8) | copy-start | bytes 2359300
  129.5 14.3 %collective-permute-start.17 = (bf16[128,1536]{1,0:T(8,128)(2,1)}, bf16[128,1536]{1,0:T(8,128)(2,1)}, u32[]{:S(2)}, u32[]{:S(2)}) collective-permute-start(bf16[128,1536]{1,0:T(8,128)(2,1)} %shard_map.98), channel_id=1, source_target_pairs={{132,68},{140,76},{148,84},{156,92},{164,100},{172,108},{180,116},... | collective-permute-start | bytes 1179656 | tf_op jit(solution)/shard_map/ppermute | solution.py:192
  134.1 0.7 copy-start.19
  135.5 10.4 %all-to-all-start.4 = ((bf16[4,192,256]{2,1,0:T(8,128)(2,1)}), bf16[4,192,256]{2,1,0:T(8,128)(2,1)}, u32[]{:S(2)}, u32[]{:S(2)}) async-start(bf16[4,192,256]{2,1,0:T(8,128)(2,1)} %broadcast_in_dim.9), calls=%async_computation.4 | async-start | bytes 786432 | tf_op jit(solution)/shard_map/all_to_all | solution.py:279
  140.3 0.8 copy-start.13
  141.1 0.7 copy-start.16
  142.3 0.6 copy-start.14
  146.0 17.5 %collective-permute-start.21 = (bf16[4,192,256]{2,1,0:T(8,128)(2,1)}, bf16[4,192,256]{2,1,0:T(8,128)(2,1)S(1)}, u32[]{:S(2)}, u32[]{:S(2)}) collective-permute-start(bf16[4,192,256]{2,1,0:T(8,128)(2,1)} %all-to-all-done.4), channel_id=1, source_target_pairs={{0,4},{4,0},{8,12},{12,8},{16,20},{20,16},{24,28},{28,24},{32,36},... | collective-permute-start | bytes 1179656 | tf_op jit(solution)/shard_map/ppermute | solution.py:284
  159.4 6.4 %collective-permute-start.20 = (bf16[128,1536]{1,0:T(8,128)(2,1)S(1)}, bf16[128,1536]{1,0:T(8,128)(2,1)S(1)}, u32[]{:S(2)}, u32[]{:S(2)}) collective-permute-start(bf16[128,1536]{1,0:T(8,128)(2,1)S(1)} %shard_map.101), channel_id=1, source_target_pairs={{64,0},{72,8},{80,16},{88,24},{96,32},{104,40},{112,48},{120,56},{... | collective-permute-start | bytes 1179656 | tf_op jit(solution)/shard_map/ppermute | solution.py:192
  161.5 11.5 %collective-permute-start.19 = (bf16[128,1536]{1,0:T(8,128)(2,1)S(1)}, bf16[128,1536]{1,0:T(8,128)(2,1)S(1)}, u32[]{:S(2)}, u32[]{:S(2)}) collective-permute-start(bf16[128,1536]{1,0:T(8,128)(2,1)S(1)} %shard_map.100), channel_id=1, source_target_pairs={{68,4},{76,12},{84,20},{92,28},{100,36},{108,44},{116,52},{124,60}... | collective-permute-start | bytes 1179656 | tf_op jit(solution)/shard_map/ppermute | solution.py:192

commit v7 on v6

--- a/solution.py
+++ b/solution.py
@@ -276,11 +276,10 @@
     second_grads = total[chunk:].T / divisor
     spread = jnp.broadcast_to(total[None, :chunk].astype(bf16), (size // 4, chunk, hidden))
     along = [[x * 4 + rest for x in range(size // 4)] for rest in range(4)]
-    own = lax.all_to_all(spread, "dp", 0, 0, axis_index_groups=along, tiled=True)
     for turn in range(layers + 1, layers + LAG):
         chains = [advance(turn, chain) for chain in range(2)]
-        if turn == layers + 1:
-            own, *chains = lax.optimization_barrier((own, *chains))
+    own = lax.all_to_all(spread, "dp", 0, 0, axis_index_groups=along, tiled=True)
+    own, *chains = lax.optimization_barrier((own, *chains))
     far = lax.ppermute(own, "dp", [(i, i ^ 1) for i in range(size)])
     near = (index & 1) == 0
     summed = jnp.stack([jnp.where(near, own, far), jnp.where(near, far, own)], axis=1)

time: 176 us -> 171 us (0.972)
  starting transfers between devices: 63 us -> 59.3 us
    ppermute x20, waiting for transfers between devices: 36.1 us -> 25.2 us  [hop(): return lax.ppermute(array, ('pipe', 'dp'), pairs)]
    ppermute x1, waiting for transfers between devices: 1.51 us -> 9.04 us  [on_device(): other = lax.ppermute(mine, 'dp', [(i, i ^ 2) for i in range(size)])]
    ppermute x1, starting transfers between devices: 10.2 us -> 3.7 us  [on_device(): far = lax.ppermute(own, 'dp', [(i, i ^ 1) for i in range(size)])]
    ppermute x1, starting transfers between devices: 6.14 us -> 8.73 us  [on_device(): other = lax.ppermute(mine, 'dp', [(i, i ^ 2) for i in range(size)])]
    all_to_all x1, waiting for transfers between devices: 2.08 us -> 3.93 us  [on_device(): lax.all_to_all(spread, 'dp', 0, 0, axis_index_groups=along, tiled=True)]
  transfers between devices with their start and end apart: 24 -> 24, of which waited for: 10 -> 8; matrix products, arithmetic and copies ran while one was open for 4% -> 3% of each run, Pallas kernels for 16% -> 17%
where the time goes in v7:
time: 171 us; the launch traced here: 170 us
  starting transfers between devices  59.3 us (35%)
  waiting for transfers between devices  38.1 us (22%)
  Pallas kernels  29.9 us (17%)
  blocking collectives  26 us (15%)
  local copies, waits for them, and re-layouts  9.73 us (6%)
  other arithmetic  4.45 us (3%)
    ppermute x20, starting transfers between devices, hop(): return lax.ppermute(array, ('pipe', 'dp'), pairs)  35.7 us
    ppermute x20, waiting for transfers between devices, hop(): return lax.ppermute(array, ('pipe', 'dp'), pairs)  25.2 us
    pallas_call x14, Pallas kernels, advance(): call(functools.partial(hop_kernel, turn, chain, layers), [shape((tokens,...  14.9 us
    all_to_all x1, blocking collectives, on_device(): packed = lax.all_to_all(packed, 'tensor', 0, 0, tiled=True)  10.5 us
    pallas_call x7, Pallas kernels, on_device(): call(functools.partial(depth_kernel, turn, layers), [shape((columns, toke...  9.72 us
    ppermute x1, waiting for transfers between devices, on_device(): other = lax.ppermute(mine, 'dp', [(i, i ^ 2) for i in range(size)])  9.04 us
    ppermute x1, starting transfers between devices, on_device(): other = lax.ppermute(mine, 'dp', [(i, i ^ 2) for i in range(size)])  8.73 us
    unnamed x40, local copies, waits for them, and re-layouts  8.73 us
  transfers between devices with their start and end apart: 24, of which 8 were waited for; matrix products, arithmetic and copies ran while one was open for 3% of the time, Pallas kernels for 17%

profile of v7, /device:TPU:161, one launch (start us, length us, event | category | flops | bytes accessed | tf_op | source)
XLA Modules:
  0.0 169.9 jit_solution(2810871588857808207)
XLA Ops:
  0.6 1.5 collective-permute-start
  2.2 3.5 %collective-permute-start.1 = (bf16[128,1536]{1,0:T(8,128)(2,1)}, bf16[128,1536]{1,0:T(8,128)(2,1)}, u32[]{:S(2)}, u32[]{:S(2)}) collective-permute-start(bf16[128,1536]{1,0:T(8,128)(2,1)} %bitcast.48), channel_id=1, source_target_pairs={{4,68},{12,76},{20,84},{28,92},{36,100},{44,108},{52,116},{60,124}... | collective-permute-start | bytes 1179656 | tf_op jit(solution)/shard_map/ppermute | solution.py:192
  6.7 1.1 copy-done.3
  8.9 10.5 %all_to_all.25.parts_ref = bf16[4,128,384]{2,1,0:T(8,128)(2,1)S(1)} all-to-all(bf16[4,128,384]{2,1,0:T(8,128)(2,1)S(1)} %get-tuple-element.39), channel_id=1, replica_groups=mesh['pipe'=8,'dp'=16,'tensor'=4] {'tensor'}, dimensions={0} | all-to-all | bytes 786432 | tf_op jit(solution)/shard_map/all_to_all | solution.py:206
  19.4 3.5 %collective-permute-start.3 = (bf16[128,1536]{1,0:T(8,128)(2,1)}, bf16[128,1536]{1,0:T(8,128)(2,1)}, u32[]{:S(2)}, u32[]{:S(2)}) collective-permute-start(bf16[128,1536]{1,0:T(8,128)(2,1)} %collective-permute-done.1.odd_ref), channel_id=1, source_target_pairs={{68,132},{76,140},{84,148},{92,156},{100,164},{108,172},{116,180},... | collective-permute-start | bytes 1179656 | tf_op jit(solution)/shard_map/ppermute | solution.py:192
  23.0 1.4 collective-permute-start.2
  24.6 1.1 shard_map.78.before_ref
  25.7 1.7 %shard_map.79.before_ref = f32[32,128]{1,0:T(8,128)S(1)} custom-call(s32[2]{0:T(128)S(1)} %pad_add_fusion.place_ref, bf16[128,1536]{1,0:T(8,128)(2,1)} %collective-permute-done.even_ref, bf16[128,1536]{1,0:T(8,128)(2,1)} %collective-permute-done.1.odd_ref, bf16[4,128,1536]{2,1,0:T(8,128)(2,1)S(1)} %bitcast.25, f32[32,128]{1,0:T(8,128)S(1)} %shard_map.78.before_ref), custom_call_target="tpu_custom_call" | custom-call | flops 1572864 | bytes 1966080 | tf_op jit(solution)/shard_map/pallas_call | solution.py:247
  27.9 1.1 copy-done.5
  30.9 7.0 %all-to-all-start.1 = ((bf16[8,704,128]{2,1,0:T(8,128)(2,1)}), bf16[8,704,128]{2,1,0:T(8,128)(2,1)S(1)}, u32[]{:S(2)}, u32[]{:S(2)}) async-start(bf16[8,704,128]{2,1,0:T(8,128)(2,1)} %copy-done.5), calls=%async_computation.1 | async-start | bytes 2883584 | tf_op jit(solution)/shard_map/all_to_all | solution.py:257
  37.9 1.9 %collective-permute-start.5 = (bf16[128,1536]{1,0:T(8,128)(2,1)}, bf16[128,1536]{1,0:T(8,128)(2,1)S(1)}, u32[]{:S(2)}, u32[]{:S(2)}) collective-permute-start(bf16[128,1536]{1,0:T(8,128)(2,1)} %collective-permute-done.3.odd_ref), channel_id=1, source_target_pairs={{132,196},{140,204},{148,212},{156,220},{164,228},{172,236},{180,2... | collective-permute-start | bytes 1179656 | tf_op jit(solution)/shard_map/ppermute | solution.py:192
  40.5 1.7 %shard_map.80.before_ref = f32[32,128]{1,0:T(8,128)S(1)} custom-call(s32[2]{0:T(128)S(1)} %pad_add_fusion.place_ref, bf16[128,1536]{1,0:T(8,128)(2,1)} %collective-permute-done.2.even_ref, bf16[128,1536]{1,0:T(8,128)(2,1)} %collective-permute-done.3.odd_ref, bf16[4,128,1536]{2,1,0:T(8,128)(2,1)S(1)} %bitcast.26, f32[32,128]{1,0:T(8,128)S(1)} %shard_map.79.before_ref), custom_call_target="tpu_custom_call" | custom-call | flops 1572864 | bytes 1966080 | tf_op jit(solution)/shard_map/pallas_call | solution.py:247
  42.2 7.7 %collective-permute-done.5.odd_ref.held_ref = bf16[128,1536]{1,0:T(8,128)(2,1)S(1)} collective-permute-done((bf16[128,1536]{1,0:T(8,128)(2,1)}, bf16[128,1536]{1,0:T(8,128)(2,1)S(1)}, u32[]{:S(2)}, u32[]{:S(2)}) %collective-permute-start.5) | collective-permute-done | bytes 393248 | tf_op jit(solution)/shard_map/ppermute | solution.py:192
  50.5 2.2 %collective-permute-start.7 = (bf16[128,1536]{1,0:T(8,128)(2,1)S(1)}, bf16[128,1536]{1,0:T(8,128)(2,1)S(1)}, u32[]{:S(2)}, u32[]{:S(2)}) collective-permute-start(bf16[128,1536]{1,0:T(8,128)(2,1)S(1)} %shard_map.83), channel_id=1, source_target_pairs={{196,260},{204,268},{212,276},{220,284},{228,292},{236,300},{244,3... | collective-permute-start | bytes 1179656 | tf_op jit(solution)/shard_map/ppermute | solution.py:192
  54.4 1.1 shard_map.81.before_ref
  55.6 5.8 %collective-permute-done.7.odd_ref.held_ref = bf16[128,1536]{1,0:T(8,128)(2,1)S(1)} collective-permute-done((bf16[128,1536]{1,0:T(8,128)(2,1)S(1)}, bf16[128,1536]{1,0:T(8,128)(2,1)S(1)}, u32[]{:S(2)}, u32[]{:S(2)}) %collective-permute-start.7) | collective-permute-done | bytes 393248 | tf_op jit(solution)/shard_map/ppermute | solution.py:192
  61.4 1.3 shard_map.86
  62.7 2.5 %collective-permute-start.9 = (bf16[128,1536]{1,0:T(8,128)(2,1)}, bf16[128,1536]{1,0:T(8,128)(2,1)}, u32[]{:S(2)}, u32[]{:S(2)}) collective-permute-start(bf16[128,1536]{1,0:T(8,128)(2,1)} %shard_map.86), channel_id=1, source_target_pairs={{260,324},{268,332},{276,340},{284,348},{292,356},{300,364},{308,3... | collective-permute-start | bytes 1179656 | tf_op jit(solution)/shard_map/ppermute | solution.py:192
  65.3 1.7 %shard_map.85 = bf16[128,1536]{1,0:T(8,128)(2,1)} custom-call(s32[2]{0:T(128)S(1)} %pad_add_fusion.place_ref, bf16[128,1536]{1,0:T(8,128)(2,1)S(1)} %collective-permute-done.6.even_ref.held_ref, bf16[4,128,1536]{2,1,0:T(8,128)(2,1)S(1)} %bitcast.31, f32[128,32]{1,0:T(8,128)S(1)} %get-tuple-element.65.mixing_ref), custom_call_target="tpu_custom_call" | custom-call | flops 1572864 | bytes 2359296 | tf_op jit(solution)/shard_map/pallas_call | solution.py:234
  67.0 1.3 collective-permute-start.8
  68.3 1.1 shard_map.84.before_ref
  69.5 3.9 %collective-permute-done.9.odd_ref.held_ref = bf16[128,1536]{1,0:T(8,128)(2,1)} collective-permute-done((bf16[128,1536]{1,0:T(8,128)(2,1)}, bf16[128,1536]{1,0:T(8,128)(2,1)}, u32[]{:S(2)}, u32[]{:S(2)}) %collective-permute-start.9) | collective-permute-done | bytes 393248 | tf_op jit(solution)/shard_map/ppermute | solution.py:192
  74.4 2.6 %collective-permute-start.11 = (bf16[128,1536]{1,0:T(8,128)(2,1)S(1)}, bf16[128,1536]{1,0:T(8,128)(2,1)S(1)}, u32[]{:S(2)}, u32[]{:S(2)}) collective-permute-start(bf16[128,1536]{1,0:T(8,128)(2,1)S(1)} %shard_map.89), channel_id=1, source_target_pairs={{324,388},{332,396},{340,404},{348,412},{356,420},{364,428},{372,4... | collective-permute-start | bytes 1179656 | tf_op jit(solution)/shard_map/ppermute | solution.py:192
  77.0 1.4 shard_map.88
  78.5 1.9 %collective-permute-start.10 = (bf16[128,1536]{1,0:T(8,128)(2,1)S(1)}, bf16[128,1536]{1,0:T(8,128)(2,1)S(1)}, u32[]{:S(2)}, u32[]{:S(2)}) collective-permute-start(bf16[128,1536]{1,0:T(8,128)(2,1)S(1)} %shard_map.88), channel_id=1, source_target_pairs={{320,384},{328,392},{336,400},{344,408},{352,416},{360,424},{368,4... | collective-permute-start | bytes 1179656 | tf_op jit(solution)/shard_map/ppermute | solution.py:192
  80.4 1.7 %shard_map.87.before_ref = f32[32,128]{1,0:T(8,128)S(1)} custom-call(s32[2]{0:T(128)S(1)} %pad_add_fusion.place_ref, bf16[128,1536]{1,0:T(8,128)(2,1)} %collective-permute-done.8.even_ref.held_ref, bf16[128,1536]{1,0:T(8,128)(2,1)} %collective-permute-done.9.odd_ref.held_ref, bf16[4,128,1536]{2,1,0:T(8,128)(2,1)S(1)} %bitcast.35, ...), custom_call_target="tpu_custom_call" | custom-call | flops 1572864 | bytes 1966080 | tf_op jit(solution)/shard_map/pallas_call | solution.py:247
  83.5 3.4 %collective-permute-done.10.even_ref.held_ref = bf16[128,1536]{1,0:T(8,128)(2,1)S(1)} collective-permute-done((bf16[128,1536]{1,0:T(8,128)(2,1)S(1)}, bf16[128,1536]{1,0:T(8,128)(2,1)S(1)}, u32[]{:S(2)}, u32[]{:S(2)}) %collective-permute-start.10) | collective-permute-done | bytes 393248 | tf_op jit(solution)/shard_map/ppermute | solution.py:192
  88.0 1.9 %collective-permute-start.12 = (bf16[128,1536]{1,0:T(8,128)(2,1)S(1)}, bf16[128,1536]{1,0:T(8,128)(2,1)S(1)}, u32[]{:S(2)}, u32[]{:S(2)}) collective-permute-start(bf16[128,1536]{1,0:T(8,128)(2,1)S(1)} %shard_map.91), channel_id=1, source_target_pairs={{384,448},{392,456},{400,464},{408,472},{416,480},{424,488},{432,4... | collective-permute-start | bytes 1179656 | tf_op jit(solution)/shard_map/ppermute | solution.py:192
  89.9 1.1 shard_map.90.before_ref
  92.3 4.2 %collective-permute-done.12.even_ref.held_ref = bf16[128,1536]{1,0:T(8,128)(2,1)S(1)} collective-permute-done((bf16[128,1536]{1,0:T(8,128)(2,1)S(1)}, bf16[128,1536]{1,0:T(8,128)(2,1)S(1)}, u32[]{:S(2)}, u32[]{:S(2)}) %collective-permute-start.12) | collective-permute-done | bytes 393248 | tf_op jit(solution)/shard_map/ppermute | solution.py:192
  97.5 2.1 %collective-permute-start.14 = (bf16[128,1536]{1,0:T(8,128)(2,1)S(1)}, bf16[128,1536]{1,0:T(8,128)(2,1)S(1)}, u32[]{:S(2)}, u32[]{:S(2)}) collective-permute-start(bf16[128,1536]{1,0:T(8,128)(2,1)S(1)} %shard_map.96), channel_id=1, source_target_pairs={{196,132},{204,140},{212,148},{220,156},{228,164},{236,172},{244,1... | collective-permute-start | bytes 1179656 | tf_op jit(solution)/shard_map/ppermute | solution.py:192
  99.5 1.1 shard_map.93
  100.7 7.0 %all_to_all.26.parts_ref = f32[4,32,128]{2,1,0:T(8,128)S(1)} all-to-all(f32[4,32,128]{2,1,0:T(8,128)S(1)} %broadcast_in_dim.8), channel_id=1, replica_groups=mesh['pipe'=8,'dp'=16,'tensor'=4] {'tensor'}, dimensions={0} | all-to-all | bytes 131072 | tf_op jit(solution)/shard_map/all_to_all | solution.py:262
  107.7 8.4 %all_to_all.27.depth_ref = bf16[8,32,128]{2,1,0:T(8,128)(2,1)S(1)} all-to-all(bf16[8,32,128]{2,1,0:T(8,128)(2,1)S(1)} %shard_map.94.depth_ref), channel_id=1, replica_groups={{0,4,16,20,32,36,48,52},{8,12,24,28,40,44,56,60},{1,5,17,21,33,37,49,53..., dimensions={0} | all-to-all | bytes 131072 | tf_op jit(solution)/shard_map/all_to_all | solution.py:264
  119.3 2.9 %collective-permute-start.17 = (bf16[128,1536]{1,0:T(8,128)(2,1)S(1)}, bf16[128,1536]{1,0:T(8,128)(2,1)S(1)}, u32[]{:S(2)}, u32[]{:S(2)}) collective-permute-start(bf16[128,1536]{1,0:T(8,128)(2,1)S(1)} %shard_map.98), channel_id=1, source_target_pairs={{132,68},{140,76},{148,84},{156,92},{164,100},{172,108},{180,116},... | collective-permute-start | bytes 1179656 | tf_op jit(solution)/shard_map/ppermute | solution.py:192
  122.2 8.7 %collective-permute-start.16 = (bf16[224,256]{1,0:T(8,128)(2,1)S(1)}, bf16[224,256]{1,0:T(8,128)(2,1)S(1)}, u32[]{:S(2)}, u32[]{:S(2)}) collective-permute-start(bf16[224,256]{1,0:T(8,128)(2,1)S(1)} %shard_map.95), channel_id=1, source_target_pairs={{0,8},{4,12},{8,0},{12,4},{16,24},{20,28},{24,16},{28,20},{32,40},... | collective-permute-start | bytes 344072 | tf_op jit(solution)/shard_map/ppermute | solution.py:273
  130.9 1.3 shard_map.101
  133.0 1.7 %shard_map.99 = bf16[128,1536]{1,0:T(8,128)(2,1)} custom-call(s32[2]{0:T(128)S(1)} %pad_add_fusion.place_ref, bf16[128,1536]{1,0:T(8,128)(2,1)S(1)} %collective-permute-done.17.held_ref, bf16[4,128,1536]{2,1,0:T(8,128)(2,1)S(1)} %bitcast.45, f32[128,32]{1,0:T(8,128)S(1)} %get-tuple-element.65.mixing_ref), custom_call_target="tpu_custom_call" | custom-call | flops 1572864 | bytes 2359296 | tf_op jit(solution)/shard_map/pallas_call | solution.py:234
  134.7 2.3 %collective-permute-start.18 = (bf16[128,1536]{1,0:T(8,128)(2,1)}, bf16[128,1536]{1,0:T(8,128)(2,1)}, u32[]{:S(2)}, u32[]{:S(2)}) collective-permute-start(bf16[128,1536]{1,0:T(8,128)(2,1)} %shard_map.99), channel_id=1, source_target_pairs={{68,4},{76,12},{84,20},{92,28},{100,36},{108,44},{116,52},{124,60}... | collective-permute-start | bytes 1179656 | tf_op jit(solution)/shard_map/ppermute | solution.py:192
  137.0 9.0 %collective-permute-done.16 = bf16[224,256]{1,0:T(8,128)(2,1)S(1)} collective-permute-done((bf16[224,256]{1,0:T(8,128)(2,1)S(1)}, bf16[224,256]{1,0:T(8,128)(2,1)S(1)}, u32[]{:S(2)}, u32[]{:S(2)}) %collective-permute-start.16) | collective-permute-done | bytes 114720 | tf_op jit(solution)/shard_map/ppermute | solution.py:273
  147.5 4.1 %all-to-all-start.4 = ((bf16[4,192,256]{2,1,0:T(8,128)(2,1)}), bf16[4,192,256]{2,1,0:T(8,128)(2,1)}, u32[]{:S(2)}, u32[]{:S(2)}) async-start(bf16[4,192,256]{2,1,0:T(8,128)(2,1)} %broadcast_in_dim.9), calls=%async_computation.4 | async-start | bytes 786432 | tf_op jit(solution)/shard_map/all_to_all | solution.py:281
  155.0 3.9 %all-to-all-done.4 = bf16[4,192,256]{2,1,0:T(8,128)(2,1)} async-done(((bf16[4,192,256]{2,1,0:T(8,128)(2,1)}), bf16[4,192,256]{2,1,0:T(8,128)(2,1)}, u32[]{:S(2)}, u32[]{:S(2)}) %all-to-all-start.4) | async-done | bytes 393248 | tf_op jit(solution)/shard_map/all_to_all | solution.py:281
  159.0 3.7 %collective-permute-start.21 = (bf16[4,192,256]{2,1,0:T(8,128)(2,1)}, bf16[4,192,256]{2,1,0:T(8,128)(2,1)S(1)}, u32[]{:S(2)}, u32[]{:S(2)}) collective-permute-start(bf16[4,192,256]{2,1,0:T(8,128)(2,1)} %all-to-all-done.4), channel_id=1, source_target_pairs={{0,4},{4,0},{8,12},{12,8},{16,20},{20,16},{24,28},{28,24},{32,36},... | collective-permute-start | bytes 1179656 | tf_op jit(solution)/shard_map/ppermute | solution.py:283
  162.7 1.2 fusion.generated_ref
  163.9 1.4 fusion.1
  165.3 2.2 %shard_map.103 = bf16[128,1536]{1,0:T(8,128)(2,1)} custom-call(s32[2]{0:T(128)S(1)} %pad_add_fusion.place_ref, bf16[128,1536]{1,0:T(8,128)(2,1)} %collective-permute-done.18.even_ref, bf16[128,1536]{1,0:T(8,128)(2,1)S(1)} %collective-permute-done.20.odd_ref, bf16[4,128,1536]{2,1,0:T(8,128)(2,1)S(1)} %bitcast.46, f32[128,32]{1,0:T(8,128)S(1)} %get-tuple-element.65.mixing_ref, ...), custom_call_target="tpu_custom_call" | custom-call | flops 1572864 | bytes 3145728 | tf_op jit(solution)/shard_map/pallas_call | solution.py:298
  167.5 1.1 select_bitcast_fusion.1
  168.6 1.3 convert_multiply_fusion
  (83 shorter events, 21.8 us)
Async XLA Ops:
  0.6 24.0 %copy-start = (bf16[4,1,128,1536]{3,2,1,0:T(8,128)(2,1)S(1)}, bf16[4,1,128,1536]{3,2,1,0:T(8,128)(2,1)}, u32[]{:S(2)}) copy-start(bf16[4,1,128,1536]{3,2,1,0:T(8,128)(2,1)} %param.6) | copy-start | bytes 4718596
  0.6 18.8 %collective-permute-start = (bf16[128,1536]{1,0:T(8,128)(2,1)}, bf16[128,1536]{1,0:T(8,128)(2,1)}, u32[]{:S(2)}, u32[]{:S(2)}) collective-permute-start(bf16[128,1536]{1,0:T(8,128)(2,1)} %bitcast.47), channel_id=1, source_target_pairs={{0,64},{8,72},{16,80},{24,88},{32,96},{40,104},{48,112},{56,120},{... | collective-permute-start | bytes 1179656 | tf_op jit(solution)/shard_map/ppermute | solution.py:192
  2.2 17.2 %collective-permute-start.1 = (bf16[128,1536]{1,0:T(8,128)(2,1)}, bf16[128,1536]{1,0:T(8,128)(2,1)}, u32[]{:S(2)}, u32[]{:S(2)}) collective-permute-start(bf16[128,1536]{1,0:T(8,128)(2,1)} %bitcast.48), channel_id=1, source_target_pairs={{4,68},{12,76},{20,84},{28,92},{36,100},{44,108},{52,116},{60,124}... | collective-permute-start | bytes 1179656 | tf_op jit(solution)/shard_map/ppermute | solution.py:192
  5.7 1.0 copy-start.1
  6.7 1.1 copy-start.3
  7.9 0.7 copy-start.17
  8.6 15.9 %copy-start.15 = (bf16[1,256,32]{1,2,0:T(8,128)(2,1)S(1)}, bf16[1,256,32]{1,2,0:T(8,128)(2,1)}, u32[]{:S(2)}) copy-start(bf16[1,256,32]{1,2,0:T(8,128)(2,1)} %param.9) | copy-start | bytes 49156
  8.6 16.1 %copy-start.2 = (bf16[1,128,1536]{2,1,0:T(8,128)(2,1)S(1)}, bf16[1,128,1536]{2,1,0:T(8,128)(2,1)}, u32[]{:S(2)}) copy-start(bf16[1,128,1536]{2,1,0:T(8,128)(2,1)} %param.5) | copy-start | bytes 1179652
  19.4 18.5 %collective-permute-start.3 = (bf16[128,1536]{1,0:T(8,128)(2,1)}, bf16[128,1536]{1,0:T(8,128)(2,1)}, u32[]{:S(2)}, u32[]{:S(2)}) collective-permute-start(bf16[128,1536]{1,0:T(8,128)(2,1)} %collective-permute-done.1.odd_ref), channel_id=1, source_target_pairs={{68,132},{76,140},{84,148},{92,156},{100,164},{108,172},{116,180},... | collective-permute-start | bytes 1179656 | tf_op jit(solution)/shard_map/ppermute | solution.py:192
  23.0 16.8 %collective-permute-start.2 = (bf16[128,1536]{1,0:T(8,128)(2,1)}, bf16[128,1536]{1,0:T(8,128)(2,1)}, u32[]{:S(2)}, u32[]{:S(2)}) collective-permute-start(bf16[128,1536]{1,0:T(8,128)(2,1)} %collective-permute-done.even_ref), channel_id=1, source_target_pairs={{64,128},{72,136},{80,144},{88,152},{96,160},{104,168},{112,176},{... | collective-permute-start | bytes 1179656 | tf_op jit(solution)/shard_map/ppermute | solution.py:192
  24.5 2.9 %copy-start.6 = (bf16[256,32]{1,0:T(8,128)(2,1)}, bf16[256,32]{1,0:T(8,128)(2,1)S(1)}, u32[]{:S(2)}) copy-start(bf16[256,32]{1,0:T(8,128)(2,1)S(1)} %copy.11.weight_ref) | copy-start | bytes 49156
  27.8 1.1 copy-start.5
  28.9 0.6 copy-start.8
  29.6 0.6 copy-start.10
  30.2 0.6 copy-start.12
  30.9 38.6 %all-to-all-start.1 = ((bf16[8,704,128]{2,1,0:T(8,128)(2,1)}), bf16[8,704,128]{2,1,0:T(8,128)(2,1)S(1)}, u32[]{:S(2)}, u32[]{:S(2)}) async-start(bf16[8,704,128]{2,1,0:T(8,128)(2,1)} %copy-done.5), calls=%async_computation.1 | async-start | bytes 2883584 | tf_op jit(solution)/shard_map/all_to_all | solution.py:257
  37.9 12.0 %collective-permute-start.5 = (bf16[128,1536]{1,0:T(8,128)(2,1)}, bf16[128,1536]{1,0:T(8,128)(2,1)S(1)}, u32[]{:S(2)}, u32[]{:S(2)}) collective-permute-start(bf16[128,1536]{1,0:T(8,128)(2,1)} %collective-permute-done.3.odd_ref), channel_id=1, source_target_pairs={{132,196},{140,204},{148,212},{156,220},{164,228},{172,236},{180,2... | collective-permute-start | bytes 1179656 | tf_op jit(solution)/shard_map/ppermute | solution.py:192
  39.8 12.9 %collective-permute-start.4 = (bf16[128,1536]{1,0:T(8,128)(2,1)}, bf16[128,1536]{1,0:T(8,128)(2,1)S(1)}, u32[]{:S(2)}, u32[]{:S(2)}) collective-permute-start(bf16[128,1536]{1,0:T(8,128)(2,1)} %collective-permute-done.2.even_ref), channel_id=1, source_target_pairs={{128,192},{136,200},{144,208},{152,216},{160,224},{168,232},{176,2... | collective-permute-start | bytes 1179656 | tf_op jit(solution)/shard_map/ppermute | solution.py:192
  50.5 10.9 %collective-permute-start.7 = (bf16[128,1536]{1,0:T(8,128)(2,1)S(1)}, bf16[128,1536]{1,0:T(8,128)(2,1)S(1)}, u32[]{:S(2)}, u32[]{:S(2)}) collective-permute-start(bf16[128,1536]{1,0:T(8,128)(2,1)S(1)} %shard_map.83), channel_id=1, source_target_pairs={{196,260},{204,268},{212,276},{220,284},{228,292},{236,300},{244,3... | collective-permute-start | bytes 1179656 | tf_op jit(solution)/shard_map/ppermute | solution.py:192
  53.7 11.6 %collective-permute-start.6 = (bf16[128,1536]{1,0:T(8,128)(2,1)S(1)}, bf16[128,1536]{1,0:T(8,128)(2,1)S(1)}, u32[]{:S(2)}, u32[]{:S(2)}) collective-permute-start(bf16[128,1536]{1,0:T(8,128)(2,1)S(1)} %shard_map.82), channel_id=1, source_target_pairs={{192,256},{200,264},{208,272},{216,280},{224,288},{232,296},{240,3... | collective-permute-start | bytes 1179656 | tf_op jit(solution)/shard_map/ppermute | solution.py:192
  62.7 10.6 %collective-permute-start.9 = (bf16[128,1536]{1,0:T(8,128)(2,1)}, bf16[128,1536]{1,0:T(8,128)(2,1)}, u32[]{:S(2)}, u32[]{:S(2)}) collective-permute-start(bf16[128,1536]{1,0:T(8,128)(2,1)} %shard_map.86), channel_id=1, source_target_pairs={{260,324},{268,332},{276,340},{284,348},{292,356},{300,364},{308,3... | collective-permute-start | bytes 1179656 | tf_op jit(solution)/shard_map/ppermute | solution.py:192
  67.0 10.0 %collective-permute-start.8 = (bf16[128,1536]{1,0:T(8,128)(2,1)}, bf16[128,1536]{1,0:T(8,128)(2,1)}, u32[]{:S(2)}, u32[]{:S(2)}) collective-permute-start(bf16[128,1536]{1,0:T(8,128)(2,1)} %shard_map.85), channel_id=1, source_target_pairs={{256,320},{264,328},{272,336},{280,344},{288,352},{296,360},{304,3... | collective-permute-start | bytes 1179656 | tf_op jit(solution)/shard_map/ppermute | solution.py:192
  74.4 7.8 %collective-permute-start.11 = (bf16[128,1536]{1,0:T(8,128)(2,1)S(1)}, bf16[128,1536]{1,0:T(8,128)(2,1)S(1)}, u32[]{:S(2)}, u32[]{:S(2)}) collective-permute-start(bf16[128,1536]{1,0:T(8,128)(2,1)S(1)} %shard_map.89), channel_id=1, source_target_pairs={{324,388},{332,396},{340,404},{348,412},{356,420},{364,428},{372,4... | collective-permute-start | bytes 1179656 | tf_op jit(solution)/shard_map/ppermute | solution.py:192
  78.5 8.5 %collective-permute-start.10 = (bf16[128,1536]{1,0:T(8,128)(2,1)S(1)}, bf16[128,1536]{1,0:T(8,128)(2,1)S(1)}, u32[]{:S(2)}, u32[]{:S(2)}) collective-permute-start(bf16[128,1536]{1,0:T(8,128)(2,1)S(1)} %shard_map.88), channel_id=1, source_target_pairs={{320,384},{328,392},{336,400},{344,408},{352,416},{360,424},{368,4... | collective-permute-start | bytes 1179656 | tf_op jit(solution)/shard_map/ppermute | solution.py:192
  82.8 8.2 %collective-permute-start.13 = (bf16[128,1536]{1,0:T(8,128)(2,1)S(1)}, bf16[128,1536]{1,0:T(8,128)(2,1)S(1)}, u32[]{:S(2)}, u32[]{:S(2)}) collective-permute-start(bf16[128,1536]{1,0:T(8,128)(2,1)S(1)} %shard_map.92), channel_id=1, source_target_pairs={{388,452},{396,460},{404,468},{412,476},{420,484},{428,492},{436,5... | collective-permute-start | bytes 1179656 | tf_op jit(solution)/shard_map/ppermute | solution.py:192
  88.0 8.5 %collective-permute-start.12 = (bf16[128,1536]{1,0:T(8,128)(2,1)S(1)}, bf16[128,1536]{1,0:T(8,128)(2,1)S(1)}, u32[]{:S(2)}, u32[]{:S(2)}) collective-permute-start(bf16[128,1536]{1,0:T(8,128)(2,1)S(1)} %shard_map.91), channel_id=1, source_target_pairs={{384,448},{392,456},{400,464},{408,472},{416,480},{424,488},{432,4... | collective-permute-start | bytes 1179656 | tf_op jit(solution)/shard_map/ppermute | solution.py:192
  91.6 25.4 %collective-permute-start.15 = (bf16[128,1536]{1,0:T(8,128)(2,1)S(1)}, bf16[128,1536]{1,0:T(8,128)(2,1)S(1)}, u32[]{:S(2)}, u32[]{:S(2)}) collective-permute-start(bf16[128,1536]{1,0:T(8,128)(2,1)S(1)} %shard_map.97), channel_id=1, source_target_pairs={{192,128},{200,136},{208,144},{216,152},{224,160},{232,168},{240,1... | collective-permute-start | bytes 1179656 | tf_op jit(solution)/shard_map/ppermute | solution.py:192
  97.5 18.7 %copy-start.7 = (bf16[256,32]{1,0:T(8,128)(2,1)S(1)}, bf16[256,32]{1,0:T(8,128)(2,1)}, u32[]{:S(2)}) copy-start(bf16[256,32]{1,0:T(8,128)(2,1)} %copy-done.6) | copy-start | bytes 49156
  97.5 19.6 %collective-permute-start.14 = (bf16[128,1536]{1,0:T(8,128)(2,1)S(1)}, bf16[128,1536]{1,0:T(8,128)(2,1)S(1)}, u32[]{:S(2)}, u32[]{:S(2)}) collective-permute-start(bf16[128,1536]{1,0:T(8,128)(2,1)S(1)} %shard_map.96), channel_id=1, source_target_pairs={{196,132},{204,140},{212,148},{220,156},{228,164},{236,172},{244,1... | collective-permute-start | bytes 1179656 | tf_op jit(solution)/shard_map/ppermute | solution.py:192
  117.6 13.3 %collective-permute-start.19 = (bf16[128,1536]{1,0:T(8,128)(2,1)S(1)}, bf16[128,1536]{1,0:T(8,128)(2,1)S(1)}, u32[]{:S(2)}, u32[]{:S(2)}) collective-permute-start(bf16[128,1536]{1,0:T(8,128)(2,1)S(1)} %shard_map.100), channel_id=1, source_target_pairs={{128,64},{136,72},{144,80},{152,88},{160,96},{168,104},{176,112},{... | collective-permute-start | bytes 1179656 | tf_op jit(solution)/shard_map/ppermute | solution.py:192
  119.3 13.6 %collective-permute-start.17 = (bf16[128,1536]{1,0:T(8,128)(2,1)S(1)}, bf16[128,1536]{1,0:T(8,128)(2,1)S(1)}, u32[]{:S(2)}, u32[]{:S(2)}) collective-permute-start(bf16[128,1536]{1,0:T(8,128)(2,1)S(1)} %shard_map.98), channel_id=1, source_target_pairs={{132,68},{140,76},{148,84},{156,92},{164,100},{172,108},{180,116},... | collective-permute-start | bytes 1179656 | tf_op jit(solution)/shard_map/ppermute | solution.py:192
  122.2 23.9 %collective-permute-start.16 = (bf16[224,256]{1,0:T(8,128)(2,1)S(1)}, bf16[224,256]{1,0:T(8,128)(2,1)S(1)}, u32[]{:S(2)}, u32[]{:S(2)}) collective-permute-start(bf16[224,256]{1,0:T(8,128)(2,1)S(1)} %shard_map.95), channel_id=1, source_target_pairs={{0,8},{4,12},{8,0},{12,4},{16,24},{20,28},{24,16},{28,20},{32,40},... | collective-permute-start | bytes 344072 | tf_op jit(solution)/shard_map/ppermute | solution.py:273
  132.3 26.7 %collective-permute-start.20 = (bf16[128,1536]{1,0:T(8,128)(2,1)}, bf16[128,1536]{1,0:T(8,128)(2,1)S(1)}, u32[]{:S(2)}, u32[]{:S(2)}) collective-permute-start(bf16[128,1536]{1,0:T(8,128)(2,1)} %shard_map.101), channel_id=1, source_target_pairs={{64,0},{72,8},{80,16},{88,24},{96,32},{104,40},{112,48},{120,56},{... | collective-permute-start | bytes 1179656 | tf_op jit(solution)/shard_map/ppermute | solution.py:192
  134.7 17.0 %copy-start.18 = (bf16[1,1536]{1,0:T(2,128)(2,1)S(1)}, bf16[1,1536]{1,0:T(2,128)(2,1)}, u32[]{:S(2)}) copy-start(bf16[1,1536]{1,0:T(2,128)(2,1)} %gain_ref.1) | copy-start | bytes 9220
  134.7 17.6 %copy-start.9 = (f32[128,256]{1,0:T(8,128)S(1)}, f32[128,256]{1,0:T(8,128)}, u32[]{:S(2)}) copy-start(f32[128,256]{1,0:T(8,128)} %copy-done.8) | copy-start | bytes 393220
  134.7 17.6 %copy-start.11 = (f32[128,256]{1,0:T(8,128)S(1)}, f32[128,256]{1,0:T(8,128)}, u32[]{:S(2)}) copy-start(f32[128,256]{1,0:T(8,128)} %copy-done.10) | copy-start | bytes 393220
  134.7 28.0 %copy-start.4 = (bf16[1,1536,256]{2,1,0:T(8,128)(2,1)S(1)}, bf16[1,1536,256]{2,1,0:T(8,128)(2,1)}, u32[]{:S(2)}) copy-start(bf16[1,1536,256]{2,1,0:T(8,128)(2,1)} %param.8) | copy-start | bytes 2359300
  134.7 24.3 %collective-permute-start.18 = (bf16[128,1536]{1,0:T(8,128)(2,1)}, bf16[128,1536]{1,0:T(8,128)(2,1)}, u32[]{:S(2)}, u32[]{:S(2)}) collective-permute-start(bf16[128,1536]{1,0:T(8,128)(2,1)} %shard_map.99), channel_id=1, source_target_pairs={{68,4},{76,12},{84,20},{92,28},{100,36},{108,44},{116,52},{124,60}... | collective-permute-start | bytes 1179656 | tf_op jit(solution)/shard_map/ppermute | solution.py:192
  146.1 0.7 copy-start.19
  147.5 11.4 %all-to-all-start.4 = ((bf16[4,192,256]{2,1,0:T(8,128)(2,1)}), bf16[4,192,256]{2,1,0:T(8,128)(2,1)}, u32[]{:S(2)}, u32[]{:S(2)}) async-start(bf16[4,192,256]{2,1,0:T(8,128)(2,1)} %broadcast_in_dim.9), calls=%async_computation.4 | async-start | bytes 786432 | tf_op jit(solution)/shard_map/all_to_all | solution.py:281
  152.3 0.8 copy-start.13
  153.1 0.7 copy-start.16
  154.3 0.6 copy-start.14
  159.0 8.6 %collective-permute-start.21 = (bf16[4,192,256]{2,1,0:T(8,128)(2,1)}, bf16[4,192,256]{2,1,0:T(8,128)(2,1)S(1)}, u32[]{:S(2)}, u32[]{:S(2)}) collective-permute-start(bf16[4,192,256]{2,1,0:T(8,128)(2,1)} %all-to-all-done.4), channel_id=1, source_target_pairs={{0,4},{4,0},{8,12},{12,8},{16,20},{20,16},{24,28},{28,24},{32,36},... | collective-permute-start | bytes 1179656 | tf_op jit(solution)/shard_map/ppermute | solution.py:283
